TPU v7x, 1024 devices: a whole 4x8x16 slice. The times are simulated.
1024 devices in a mesh: dp: 256 (over z, y, core), space: 4 (over x).
Axes of the slice: x: 4, y: 8, z: 16, core: 2. Of those that a mesh axis runs over, the one named last changes fastest.
Arguments:
- pressure_tokens: bfloat16 [256, 16, 64, 192], P('dp', 'space'), may hold values from -6 to 6
- dw_kernel: float32 [7, 7, 192], replicated, may hold values from -0.875 to 0.875
- norm_gain: float32 [192], replicated, may hold values from 0.5 to 2
- norm_shift: float32 [192], replicated, may hold values from -3 to 3
- w_expand: bfloat16 [768, 192], P('dp'), may hold values from -0.4375 to 0.4375
- w_reduce: bfloat16 [768, 192], P('dp'), may hold values from -0.21875 to 0.21875
- layer_scale: float32 [192], replicated, may hold values from 0.5 to 2
- cotangent: bfloat16 [256, 16, 64, 192], P('dp', 'space'), may hold values from -6 to 6
Outputs:
- block_out: bfloat16 [256, 16, 64, 192], P('dp', 'space')
- grad_tokens: bfloat16 [256, 16, 64, 192], P('dp', 'space')
- grad_kernel: float32 [7, 7, 192], replicated
- grad_gain: float32 [192], replicated
- grad_shift: float32 [192], replicated
- grad_expand: float32 [768, 192], P('dp')
- grad_reduce: float32 [768, 192], P('dp')
- grad_scale: float32 [192], replicated
All inputs are finite; a program needn't handle non-finite values.
Results may differ from a plain program's by a relative error of at most 0.0095.
Values may be sent and summed in bfloat16 or wider, within the bound.
No kernel may reach another device: no remote copies, remote signals or barrier semaphores. Data moves between devices by JAX's collectives and lax.ppermute only.
A program may use at most 32 MiB of HBM per device.

v0:
```python
import jax
import jax.numpy as jnp
from jax import lax
from jax.sharding import PartitionSpec as P


def padded_2(block, sides, width):
    for axis, dim in sides:
        count = lax.axis_size(axis)
        forward = [(i, i + 1) for i in range(count - 1)]
        backward = [(target, source) for source, target in forward]
        low = lax.ppermute(
            lax.slice_in_dim(block, block.shape[dim] - width, None, axis=dim), axis, forward
        )
        high = lax.ppermute(lax.slice_in_dim(block, 0, width, axis=dim), axis, backward)
        block = jnp.concatenate([low, block, high], axis=dim)
    return block


def shortened(x):
    return jax.tree.map(lambda a: a.astype(jnp.bfloat16) if a.dtype == jnp.float32 else a, x)


def depthwise(padded, kernel):
    channels = padded.shape[-1]
    result = lax.conv_general_dilated(
        padded[None],
        kernel[:, :, None, :],
        (1, 1),
        "VALID",
        dimension_numbers=("NHWC", "HWIO", "NHWC"),
        feature_group_count=channels,
        precision=lax.Precision.HIGHEST,
    )
    return result[0]


def kernel_product(padded, grad):
    channels = padded.shape[-1]
    result = lax.conv_general_dilated(
        padded[None],
        grad[:, :, None, :],
        (1, 1),
        "VALID",
        dimension_numbers=("NHWC", "HWIO", "NHWC"),
        feature_group_count=channels,
        precision=lax.Precision.HIGHEST,
    )
    return result[0]


def gelu_slope(pre):
    return (
        0.5 * (1.0 + lax.erf(pre * 0.7071067811865476))
        + pre * jnp.exp(-0.5 * pre * pre) * 0.3989422804014327
    )


def shards(
    pressure_tokens, dw_kernel, norm_gain, norm_shift, w_expand, w_reduce, layer_scale, cotangent
):
    rows = pressure_tokens.shape[1]
    cols = pressure_tokens.shape[2]
    width = pressure_tokens.shape[3]
    cells = rows * cols
    extended = padded_2(pressure_tokens, (("space", 1),), 3)
    padded = jnp.pad(extended[0].astype(jnp.float32), ((0, 0), (3, 3), (0, 0)))
    source = padded[3 : 3 + rows, 3 : 3 + cols]
    mixed = depthwise(padded, dw_kernel)
    centre = mixed - jnp.mean(mixed, -1, keepdims=True)
    inv_std = lax.rsqrt(jnp.mean(centre * centre, -1, keepdims=True) + 1e-06)
    normed = centre * inv_std
    normed_bf = (normed * norm_gain + norm_shift).astype(jnp.bfloat16).reshape(cells, width)
    expand_piece = lax.all_gather(w_expand, "dp", axis=0, tiled=True)
    reduce_piece = lax.all_gather(w_reduce, "dp", axis=0, tiled=True)
    pre_piece = lax.dot_general(
        normed_bf, expand_piece, (((1,), (1,)), ((), ())), preferred_element_type=jnp.float32
    )
    hidden_piece = jax.nn.gelu(pre_piece, approximate=False).astype(jnp.bfloat16)
    branch_acc = jnp.dot(hidden_piece, reduce_piece, preferred_element_type=jnp.float32)
    pre_all = pre_piece
    flat_source = source.reshape(cells, width)
    block_out = (
        (flat_source + layer_scale * branch_acc).astype(jnp.bfloat16).reshape(1, rows, cols, width)
    )
    upstream_f = cotangent[0].astype(jnp.float32).reshape(cells, width)
    scale_grad = jnp.sum(upstream_f * branch_acc, 0)
    branch_grad = (upstream_f * layer_scale).astype(jnp.bfloat16)
    expand_piece = lax.all_gather(w_expand, "dp", axis=0, tiled=True)
    reduce_piece = lax.all_gather(w_reduce, "dp", axis=0, tiled=True)
    hidden_grad = lax.dot_general(
        branch_grad, reduce_piece, (((1,), (1,)), ((), ())), preferred_element_type=jnp.float32
    )
    pre_piece = pre_all
    pre_grad_piece = (hidden_grad * gelu_slope(pre_piece)).astype(jnp.bfloat16)
    normed_acc = jnp.dot(pre_grad_piece, expand_piece, preferred_element_type=jnp.float32)
    normed_grad = normed_acc
    normed_grad = normed_grad.reshape(rows, cols, width)
    gain_grad = jnp.sum(normed_grad * normed, (0, 1))
    shift_grad = jnp.sum(normed_grad, (0, 1))
    scaled = normed_grad * norm_gain
    mixed_grad = inv_std * (
        scaled
        - jnp.mean(scaled, -1, keepdims=True)
        - normed * jnp.mean(scaled * normed, -1, keepdims=True)
    )
    kernel_grad = kernel_product(padded, mixed_grad)
    grad_ext = padded_2(shortened(mixed_grad), (("space", 0),), 3).astype(mixed_grad.dtype)
    grad_pad = jnp.pad(grad_ext, ((0, 0), (3, 3), (0, 0)))
    back = depthwise(grad_pad, dw_kernel[::-1, ::-1])
    grad_tokens = (
        (upstream_f.reshape(rows, cols, width) + back)
        .astype(jnp.bfloat16)
        .reshape(1, rows, cols, width)
    )
    expand_term = lax.dot_general(
        pre_grad_piece, normed_bf, (((0,), (0,)), ((), ())), preferred_element_type=jnp.float32
    )
    reduce_term = lax.dot_general(
        hidden_piece, branch_grad, (((0,), (0,)), ((), ())), preferred_element_type=jnp.float32
    )
    weight_share = lax.psum_scatter(
        jnp.concatenate([expand_term, reduce_term], 1), "dp", scatter_dimension=0, tiled=True
    )
    weight_share = lax.psum(weight_share, "space")
    kernel_grad, gain_grad, shift_grad, scale_grad = lax.psum(
        (kernel_grad, gain_grad, shift_grad, scale_grad), ("dp", "space")
    )
    grad_expand = weight_share[:, :width]
    grad_reduce = weight_share[:, width:]
    return (
        block_out,
        grad_tokens,
        kernel_grad,
        gain_grad,
        shift_grad,
        grad_expand,
        grad_reduce,
        scale_grad,
    )


def solution(mesh):
    in_specs = (
        P("dp", "space", None, None),
        P(),
        P(),
        P(),
        P("dp", None),
        P("dp", None),
        P(),
        P("dp", "space", None, None),
    )
    out_specs = (
        P("dp", "space", None, None),
        P("dp", "space", None, None),
        P(),
        P(),
        P(),
        P("dp", None),
        P("dp", None),
        P(),
    )
    return jax.shard_map(shards, mesh=mesh, in_specs=in_specs, out_specs=out_specs, check_vma=False)
```

profile of v0, /device:TPU:24, one launch (start us, length us, event | category | flops | bytes accessed | tf_op | source)
XLA Modules:
  0.0 621.3 jit_solution(15575206484513794513)
XLA Ops:
  7.2 1.0 fusion.68
  8.2 3.4 collective-permute-start
  11.6 1.3 collective-permute-start.1
  12.9 1.4 rev.3
  14.3 1.0 copy_convert_fusion
  15.5 113.9 %all-gather = bf16[256,3,192]{2,1,0:T(4,128)(2,1)S(1)} all-gather(bf16[1,3,192]{2,1,0:T(4,128)(2,1)S(1)} %bitcast.83), channel_id=1, replica_groups=mesh['dp'=256,'space'=4] {'dp'}, dimensions={0}, use_global_device_ids=true | all-gather | bytes 296064 | tf_op jit(solution)/shard_map/all_gather | solution.py:74
  129.8 100.1 %all-gather.1 = bf16[256,3,192]{2,1,0:T(4,128)(2,1)S(1)} all-gather(bf16[1,3,192]{2,1,0:T(4,128)(2,1)S(1)} %bitcast.84), channel_id=1, replica_groups=mesh['dp'=256,'space'=4] {'dp'}, dimensions={0}, use_global_device_ids=true | all-gather | bytes 296064 | tf_op jit(solution)/shard_map/all_gather | solution.py:75
  230.2 1.3 dynamic-slice
  232.2 0.9 fusion.62
  233.3 0.9 reshape.136
  234.3 0.7 copy-done.4
  235.0 1.0 fusion.8
  237.2 2.0 fusion.13
  239.1 0.6 fusion
  239.7 1.0 multiply_reduce_fusion.2
  241.6 1.0 slice.34
  242.7 1.4 broadcast_in_dim.11
  244.1 1.1 pad_maximum_fusion
  245.5 0.5 copy-done.1
  247.0 4.6 collective-permute-start.2
  251.6 1.3 collective-permute-start.3
  252.9 2.2 fusion.46
  255.2 0.8 copy.93
  256.0 118.3 %all-reduce.3 = (f32[7,7,192]{2,1,0:T(8,128)}, f32[192]{0:T(256)}, f32[192]{0:T(256)}, f32[192]{0:T(256)}) all-reduce(f32[7,7,192]{2,1,0:T(8,128)S(1)} %bitcast.79, f32[192]{0:T(256)S(1)} %get-tuple-element.40, f32[192]{0:T(256)S(1)} %get-tuple-element.43, ...), channel_id=1, replica_groups=mesh['dp'=256,'space'=4] {'dp','space'}, use_global_device_ids=true, to_apply=%region_4.5 | all-reduce | flops 9984 | bytes 79872 | tf_op jit(solution)/shard_map/psum | solution.py:126
  375.0 0.5 copy-done.5
  375.5 1.2 convolution_select_fusion
  376.9 0.7 copy.112
  377.6 215.6 %all-reduce.6.cloned.1.call-done = f32[768,384]{0,1:T(8,128)} async-done(((f32[768,384]{0,1:T(8,128)}), f32[768,384]{0,1:T(8,128)}) %all-reduce.6.cloned.1.call-update) | async-done | bytes 1179664
  593.2 1.1 constant_dynamic-slice_fusion
  594.3 18.8 %psum.38 = f32[3,384]{0,1:T(8,128)S(1)} all-reduce(f32[3,384]{0,1:T(8,128)S(1)} %constant_dynamic-slice_fusion), channel_id=1, replica_groups=mesh['dp'=256,'space'=4] {'space'}, use_global_device_ids=true, to_apply=%region_10.11 | all-reduce | flops 1152 | bytes 9216 | tf_op jit(solution)/shard_map/psum | solution.py:125
  613.1 0.7 copy.114
  613.8 0.7 copy.113
  (70 shorter events, 5.5 us)
Async XLA Ops:
  7.2 8.4 %copy-start.8 = (bf16[3,192]{1,0:T(4,128)(2,1)S(1)}, bf16[3,192]{1,0:T(4,128)(2,1)}, u32[]{:S(2)}) copy-start(bf16[3,192]{1,0:T(4,128)(2,1)} %param.12) | copy-start | bytes 3460
  7.2 586.0 %all-reduce.6.cloned.1.call-start = ((), (), s32[]{:S(2)}) async-start(), calls=%async_computation | async-start | bytes 2359296
  8.2 223.9 %collective-permute-start = (bf16[1,3,64,192]{3,2,1,0:T(8,128)(2,1)S(1)}, bf16[1,3,64,192]{3,2,1,0:T(8,128)(2,1)S(1)}, u32[]{:S(2)}, u32[]{:S(2)}) collective-permute-start(bf16[1,3,64,192]{3,2,1,0:T(8,128)(2,1)S(1)} %get-tuple-element.60), channel_id=1, source_target_pairs={{0,1},{1,2},{2,3},{4,5},{5,6},{6,7},{8,9},{9,10},{10,11},{12,13},{... | collective-permute-start | bytes 221192 | tf_op jit(solution)/shard_map/ppermute | solution.py:12
  11.6 220.5 %collective-permute-start.1 = (bf16[1,3,64,192]{3,2,1,0:T(8,128)(2,1)S(1)}, bf16[1,3,64,192]{3,2,1,0:T(8,128)(2,1)S(1)}, u32[]{:S(2)}, u32[]{:S(2)}) collective-permute-start(bf16[1,3,64,192]{3,2,1,0:T(8,128)(2,1)S(1)} %get-tuple-element.61), channel_id=1, source_target_pairs={{1,0},{2,1},{3,2},{5,4},{6,5},{7,6},{9,8},{10,9},{11,10},{13,12},{... | collective-permute-start | bytes 221192 | tf_op jit(solution)/shard_map/ppermute | solution.py:15
  15.3 114.4 %copy-start.9 = (bf16[3,192]{1,0:T(4,128)(2,1)S(1)}, bf16[3,192]{1,0:T(4,128)(2,1)}, u32[]{:S(2)}) copy-start(bf16[3,192]{1,0:T(4,128)(2,1)} %param.13) | copy-start | bytes 3460
  129.4 102.7 %copy-start = (bf16[1,4,64,192]{3,2,1,0:T(8,128)(2,1)S(1)}, bf16[1,4,64,192]{3,2,1,0:T(8,128)(2,1)}, u32[]{:S(2)}) copy-start(bf16[1,4,64,192]{3,2,1,0:T(8,128)(2,1)} %param.8) | copy-start | bytes 294916
  234.2 0.8 copy-start.4
  234.2 0.8 copy-start.11
  236.2 1.0 copy-start.6
  236.2 0.9 copy-start.10
  237.1 2.0 copy-start.7
  245.1 0.9 copy-start.1
  246.2 6.7 %copy-start.2 = (f32[1,10,70,192]{3,0,2,1:T(1,128)S(1)}, f32[1,10,70,192]{3,0,2,1:T(1,128)}, u32[]{:S(2)}) copy-start(f32[1,10,70,192]{3,0,2,1:T(1,128)} %broadcast_in_dim.11) | copy-start | bytes 1612804
  247.0 127.3 %collective-permute-start.2 = (bf16[3,64,192]{2,0,1:T(4,128)(2,1)S(1)}, bf16[3,64,192]{2,0,1:T(4,128)(2,1)S(1)}, u32[]{:S(2)}, u32[]{:S(2)}) collective-permute-start(bf16[3,64,192]{2,0,1:T(4,128)(2,1)S(1)} %get-tuple-element.58), channel_id=1, source_target_pairs={{0,1},{1,2},{2,3},{4,5},{5,6},{6,7},{8,9},{9,10},{10,11},{12,13},{... | collective-permute-start | bytes 221192 | tf_op jit(solution)/shard_map/ppermute | solution.py:12
  251.6 122.7 %collective-permute-start.3 = (bf16[3,64,192]{2,0,1:T(4,128)(2,1)S(1)}, bf16[3,64,192]{2,0,1:T(4,128)(2,1)S(1)}, u32[]{:S(2)}, u32[]{:S(2)}) collective-permute-start(bf16[3,64,192]{2,0,1:T(4,128)(2,1)S(1)} %get-tuple-element.59), channel_id=1, source_target_pairs={{1,0},{2,1},{3,2},{5,4},{6,5},{7,6},{9,8},{10,9},{11,10},{13,12},{... | collective-permute-start | bytes 221192 | tf_op jit(solution)/shard_map/ppermute | solution.py:15
  374.6 0.8 copy-start.5
  374.7 0.8 copy-start.12
  375.5 1.3 copy-start.3
Sparse Core Ops, SparseCore 0:
  245.3 347.8 all-reduce.5
where the time goes:
time: 622 us; the launch traced here: 621 us
  blocking collectives  351 us (56%)
  waiting for transfers between devices  216 us (35%)
  local copies, waits for them, and re-layouts  15.3 us (2%)
  between operations  15.2 us (2%)
  starting transfers between devices  10.6 us (2%)
  matrix products  8.79 us (1%)
    unnamed x2, waiting for transfers between devices  216 us
    psum x1, blocking collectives, shards(): lax.psum((kernel_grad, gain_grad, shift_grad, scale_grad), ('dp', 'space'))  118 us
    all_gather x1, blocking collectives, shards(): expand_piece = lax.all_gather(w_expand, 'dp', axis=0, tiled=True)  114 us
    all_gather x1, blocking collectives, shards(): reduce_piece = lax.all_gather(w_reduce, 'dp', axis=0, tiled=True)  100 us
    psum x1, blocking collectives, shards(): weight_share = lax.psum(weight_share, 'space')  18.8 us
  transfers between devices with their start and end apart: 5, of which 1 were waited for; matrix products, arithmetic and copies ran while one was open for 2% of the time, Pallas kernels for 0%

commit v1 on v0

v1 whole, which is shorter than its diff:
```python
import jax
import jax.numpy as jnp
from jax import lax
from jax.sharding import Mesh, PartitionSpec as P

DEPTH, HEIGHT, CORES = 16, 8, 2
DP = ("z", "y", "core")


def padded_2(block, dim, width):
    count = lax.axis_size("space")
    forward = [(i, i + 1) for i in range(count - 1)]
    backward = [(target, source) for source, target in forward]
    low = lax.ppermute(
        lax.slice_in_dim(block, block.shape[dim] - width, None, axis=dim), "space", forward
    )
    high = lax.ppermute(lax.slice_in_dim(block, 0, width, axis=dim), "space", backward)
    return jnp.concatenate([low, block, high], axis=dim)


def depthwise(padded, kernel):
    channels = padded.shape[-1]
    result = lax.conv_general_dilated(
        padded[None],
        kernel[:, :, None, :],
        (1, 1),
        "VALID",
        dimension_numbers=("NHWC", "HWIO", "NHWC"),
        feature_group_count=channels,
        precision=lax.Precision.HIGHEST,
    )
    return result[0]


def kernel_product(padded, grad):
    channels = padded.shape[-1]
    result = lax.conv_general_dilated(
        padded[None],
        grad[:, :, None, :],
        (1, 1),
        "VALID",
        dimension_numbers=("NHWC", "HWIO", "NHWC"),
        feature_group_count=channels,
        precision=lax.Precision.HIGHEST,
    )
    return result[0]


def gelu_slope(pre):
    return (
        0.5 * (1.0 + lax.erf(pre * 0.7071067811865476))
        + pre * jnp.exp(-0.5 * pre * pre) * 0.3989422804014327
    )


def other_core(x):
    return lax.ppermute(x, "core", [(0, 1), (1, 0)])


def spread(x, axes, count):
    copies = jnp.broadcast_to(x[None], (count,) + x.shape)
    return lax.all_to_all(copies, axes, 0, 0, tiled=True)


def gather_weights(w_expand, w_reduce):
    block = jnp.concatenate([w_expand, w_reduce], 1)
    units, lanes = block.shape
    column = spread(block, "z", DEPTH).reshape(DEPTH * units, lanes)
    plane = spread(column, "y", HEIGHT).reshape(HEIGHT * DEPTH * units, lanes)
    return jnp.concatenate([plane, other_core(plane)], 0)


def reduce_all(weight_grad, smalls):
    half, lanes = weight_grad.shape[0] // 2, weight_grad.shape[1]
    quarters = lax.axis_size("space")
    part = lanes // quarters
    peers = HEIGHT * quarters
    units = half // (HEIGHT * DEPTH)
    count = smalls.size
    rows = -(-count // (peers * part))
    flat = jnp.pad(smalls.reshape(-1), (0, peers * rows * part - count))
    small_parts = flat.reshape(peers, rows, part)

    def pieces(grad):
        cut = grad.reshape(HEIGHT, DEPTH * units, quarters, part).transpose(0, 2, 1, 3)
        return jnp.concatenate([cut.reshape(peers, DEPTH * units, part), small_parts], 1)

    mine, theirs = pieces(weight_grad[:half]), pieces(weight_grad[half:])
    sums = (mine + other_core(theirs)).astype(jnp.bfloat16)
    arrived = lax.all_to_all(sums, ("y", "space"), 0, 0, tiled=True)
    total = jnp.sum(arrived.astype(jnp.float32), 0)
    column = jnp.concatenate(
        [
            total[: DEPTH * units].reshape(DEPTH, units, part),
            jnp.broadcast_to(total[None, DEPTH * units :], (DEPTH, rows, part)),
        ],
        1,
    )
    total = jnp.sum(lax.all_to_all(column, "z", 0, 0, tiled=True), 0)
    done = spread(total, ("y", "space"), peers)
    own = lax.dynamic_slice_in_dim(done, lax.axis_index("y") * quarters, quarters, 0)
    weight_share = own[:, :units].transpose(1, 0, 2).reshape(units, lanes)
    return weight_share, done[:, units:].reshape(-1)[:count].reshape(smalls.shape)


def shards(
    pressure_tokens, dw_kernel, norm_gain, norm_shift, w_expand, w_reduce, layer_scale, cotangent
):
    rows = pressure_tokens.shape[1]
    cols = pressure_tokens.shape[2]
    width = pressure_tokens.shape[3]
    cells = rows * cols
    extended = padded_2(pressure_tokens, 1, 3)
    weights = gather_weights(w_expand, w_reduce)
    expand, reduce = weights[:, :width], weights[:, width:]
    padded = jnp.pad(extended[0].astype(jnp.float32), ((0, 0), (3, 3), (0, 0)))
    source = padded[3 : 3 + rows, 3 : 3 + cols]
    mixed = depthwise(padded, dw_kernel)
    centre = mixed - jnp.mean(mixed, -1, keepdims=True)
    inv_std = lax.rsqrt(jnp.mean(centre * centre, -1, keepdims=True) + 1e-06)
    normed = centre * inv_std
    normed_bf = (normed * norm_gain + norm_shift).astype(jnp.bfloat16).reshape(cells, width)
    pre = lax.dot_general(
        normed_bf, expand, (((1,), (1,)), ((), ())), preferred_element_type=jnp.float32
    )
    hidden = jax.nn.gelu(pre, approximate=False).astype(jnp.bfloat16)
    branch = jnp.dot(hidden, reduce, preferred_element_type=jnp.float32)
    flat_source = source.reshape(cells, width)
    block_out = (
        (flat_source + layer_scale * branch).astype(jnp.bfloat16).reshape(1, rows, cols, width)
    )
    upstream_f = cotangent[0].astype(jnp.float32).reshape(cells, width)
    scale_grad = jnp.sum(upstream_f * branch, 0)
    branch_grad = (upstream_f * layer_scale).astype(jnp.bfloat16)
    hidden_grad = lax.dot_general(
        branch_grad, reduce, (((1,), (1,)), ((), ())), preferred_element_type=jnp.float32
    )
    pre_grad = (hidden_grad * gelu_slope(pre)).astype(jnp.bfloat16)
    normed_grad = jnp.dot(pre_grad, expand, preferred_element_type=jnp.float32)
    normed_grad = normed_grad.reshape(rows, cols, width)
    gain_grad = jnp.sum(normed_grad * normed, (0, 1))
    shift_grad = jnp.sum(normed_grad, (0, 1))
    scaled = normed_grad * norm_gain
    mixed_grad = inv_std * (
        scaled
        - jnp.mean(scaled, -1, keepdims=True)
        - normed * jnp.mean(scaled * normed, -1, keepdims=True)
    )
    kernel_grad = kernel_product(padded, mixed_grad)
    grad_ext = padded_2(mixed_grad.astype(jnp.bfloat16), 0, 3).astype(mixed_grad.dtype)
    grad_pad = jnp.pad(grad_ext, ((0, 0), (3, 3), (0, 0)))
    back = depthwise(grad_pad, dw_kernel[::-1, ::-1])
    grad_tokens = (
        (upstream_f.reshape(rows, cols, width) + back)
        .astype(jnp.bfloat16)
        .reshape(1, rows, cols, width)
    )
    expand_term = lax.dot_general(
        pre_grad, normed_bf, (((0,), (0,)), ((), ())), preferred_element_type=jnp.float32
    )
    reduce_term = lax.dot_general(
        hidden, branch_grad, (((0,), (0,)), ((), ())), preferred_element_type=jnp.float32
    )
    smalls = jnp.concatenate(
        [kernel_grad.reshape(-1, width), jnp.stack([gain_grad, shift_grad, scale_grad])], 0
    )
    weight_share, smalls = reduce_all(jnp.concatenate([expand_term, reduce_term], 1), smalls)
    taps = kernel_grad.shape[0] * kernel_grad.shape[1]
    return (
        block_out,
        grad_tokens,
        smalls[:taps].reshape(kernel_grad.shape),
        smalls[taps],
        smalls[taps + 1],
        weight_share[:, :width],
        weight_share[:, width:],
        smalls[taps + 2],
    )


def solution(mesh):
    grid = Mesh(
        mesh.devices.reshape(DEPTH, HEIGHT, CORES, mesh.shape["space"]), DP + ("space",)
    )
    tokens, units = P(DP, "space", None, None), P(DP, None)
    in_specs = (tokens, P(), P(), P(), units, units, P(), tokens)
    out_specs = (tokens, tokens, P(), P(), P(), units, units, P())
    return jax.shard_map(shards, mesh=grid, in_specs=in_specs, out_specs=out_specs, check_vma=False)
```

time: 622 us -> 145 us (0.23)
  the two profiles are of different devices: /device:TPU:24 before, /device:TPU:8 now
where the time goes in v1:
time: 145 us; the launch traced here: 144 us
  starting transfers between devices  63.9 us (44%)
  waiting for transfers between devices  41.5 us (29%)
  local copies, waits for them, and re-layouts  18 us (12%)
  matrix products  11 us (8%)
  other arithmetic  8.49 us (6%)
    all_to_all x3, starting transfers between devices, spread(): return lax.all_to_all(copies, axes, 0, 0, tiled=True)  33 us
    all_to_all x3, waiting for transfers between devices, spread(): return lax.all_to_all(copies, axes, 0, 0, tiled=True)  14.5 us
    all_to_all x1, starting transfers between devices, reduce_all(): total = jnp.sum(lax.all_to_all(column, 'z', 0, 0, tiled=True), 0)  11.7 us
    all_to_all x1, waiting for transfers between devices, reduce_all(): total = jnp.sum(lax.all_to_all(column, 'z', 0, 0, tiled=True), 0)  11.4 us
    ppermute x2, waiting for transfers between devices, padded_2(): lax.ppermute(lax.slice_in_dim(block, 0, width, axis=dim), 'space', backward)  8.38 us
    ppermute x2, starting transfers between devices, padded_2(): lax.ppermute(lax.slice_in_dim(block, block.shape[dim] - width, None, axis...  6.78 us
    all_to_all x1, starting transfers between devices, reduce_all(): arrived = lax.all_to_all(sums, ('y', 'space'), 0, 0, tiled=True)  5.77 us
    ppermute x2, starting transfers between devices, other_core(): return lax.ppermute(x, 'core', [(0, 1), (1, 0)])  4.13 us
  transfers between devices with their start and end apart: 11, of which 9 were waited for; matrix products, arithmetic and copies ran while one was open for 9% of the time, Pallas kernels for 0%

profile of v1, /device:TPU:8, one launch (start us, length us, event | category | flops | bytes accessed | tf_op | source)
XLA Modules:
  0.0 144.1 jit_solution(5716387562050390546)
XLA Ops:
  2.0 19.0 %all-to-all-start = ((bf16[16,3,384]{2,1,0:T(4,128)(2,1)}), bf16[16,3,384]{2,1,0:T(4,128)(2,1)S(1)}, u32[]{:S(2)}, u32[]{:S(2)}) async-start(bf16[16,3,384]{2,1,0:T(4,128)(2,1)} %broadcast_in_dim.23), calls=%async_computation | async-start | bytes 98304 | tf_op jit(solution)/shard_map/all_to_all | solution.py:62
  21.1 1.0 fusion.76
  22.0 3.4 %collective-permute-start = (bf16[1,3,64,192]{3,2,1,0:T(8,128)(2,1)S(1)}, bf16[1,3,64,192]{3,2,1,0:T(8,128)(2,1)S(1)}, u32[]{:S(2)}, u32[]{:S(2)}) collective-permute-start(bf16[1,3,64,192]{3,2,1,0:T(8,128)(2,1)S(1)} %get-tuple-element.72), channel_id=1, source_target_pairs={{0,1},{1,2},{2,3},{4,5},{5,6},{6,7},{8,9},{9,10},{10,11},{12,13},{... | collective-permute-start | bytes 221192 | tf_op jit(solution)/shard_map/ppermute | solution.py:14
  25.4 1.3 collective-permute-start.1
  26.7 1.0 copy_convert_fusion
  28.0 4.0 %collective-permute-done.1 = bf16[1,3,64,192]{3,2,1,0:T(8,128)(2,1)S(1)} collective-permute-done((bf16[1,3,64,192]{3,2,1,0:T(8,128)(2,1)S(1)}, bf16[1,3,64,192]{3,2,1,0:T(8,128)(2,1)S(1)}, u32[]{:S(2)}, u32[]{:S(2)}) %collective-permute-start.1) | collective-permute-done | bytes 73760 | tf_op jit(solution)/shard_map/ppermute | solution.py:17
  34.9 7.5 %all-to-all-start.1 = ((bf16[8,48,384]{2,1,0:T(8,128)(2,1)}), bf16[8,48,384]{2,1,0:T(8,128)(2,1)S(1)}, u32[]{:S(2)}, u32[]{:S(2)}) async-start(bf16[8,48,384]{2,1,0:T(8,128)(2,1)} %broadcast_in_dim.25), calls=%async_computation.1 | async-start | bytes 589824 | tf_op jit(solution)/shard_map/all_to_all | solution.py:62
  42.5 1.0 fusion.8
  43.5 1.0 slice.85
  44.6 1.4 broadcast_in_dim.21
  46.5 5.7 %all-to-all-done.1 = bf16[8,48,384]{2,1,0:T(8,128)(2,1)S(1)} async-done(((bf16[8,48,384]{2,1,0:T(8,128)(2,1)}), bf16[8,48,384]{2,1,0:T(8,128)(2,1)S(1)}, u32[]{:S(2)}, u32[]{:S(2)}) %all-to-all-start.1) | async-done | bytes 294944 | tf_op jit(solution)/shard_map/all_to_all | solution.py:62
  52.2 1.9 %collective-permute-start.2 = (bf16[384,384]{1,0:T(8,128)(2,1)S(1)}, bf16[384,384]{1,0:T(8,128)(2,1)S(1)}, u32[]{:S(2)}, u32[]{:S(2)}) collective-permute-start(bf16[384,384]{1,0:T(8,128)(2,1)S(1)} %bitcast.81), channel_id=1, source_target_pairs={{0,4},{4,0},{1,5},{5,1},{2,6},{6,2},{3,7},{7,3},{8,12},{12,8},{9,1... | collective-permute-start | bytes 884744 | tf_op jit(solution)/shard_map/ppermute | solution.py:57
  55.7 2.0 %fusion.15 = (bf16[256,768]{1,0:T(8,128)(2,1)S(1)}, f32[256,768]{1,0:T(8,128)S(1)}) fusion(bf16[384,384]{1,0:T(8,128)(2,1)S(1)} %bitcast.82, bf16[384,384]{1,0:T(8,128)(2,1)S(1)} %collective-permute-done.2, f32[256,192]{0,1:T(8,128)S(1)} %copy.167, f32[192]{0:T(256)S(1)} %copy-done.15, f32[192]{0:T(256)S(1)} %copy-done.13, f32[256]{0:T(256)S(1)} %rsqrt.13, ...), kind=kOutput, calls=%fused_computation.26 | convolution fusion | flops 89112576 | bytes 1969664 | tf_op jit(solution)/shard_map/dot_general | solution.py:123
  59.7 2.1 %multiply_reduce_fusion.2 = (f32[192]{0:T(256)S(1)}, f32[256]{0:T(256)S(1)}, f32[256]{0:T(256)S(1)}, f32[192]{0:T(256)S(1)}, f32[256,192]{0,1:T(8,128)}) fusion(f32[256,192]{0,1:T(8,128)S(1)} %copy.167, f32[256]{0:T(256)S(1)} %rsqrt.13, f32[256]{0:T(256)S(1)} %div.19, f32[192]{0:T(256)S(1)} %copy-done.13, bf16[256,768]{1,0:T(8,128)(2,1)} %copy-done.6, ...), kind=kOutput, calls=%fused_computation.86 | convolution fusion | flops 76528768 | bytes 1382656 | tf_op jit(solution)/shard_map/dot_general | solution.py:139
  63.9 1.1 copy.174
  65.0 1.1 fusion.49
  66.1 2.8 %convolution_reduce_fusion = f32[7,7,192]{2,1,0:T(8,128)S(1)} fusion(f32[1,10,70,192]{3,0,2,1:T(1,128)} %broadcast_in_dim.21, f32[4,64,1,192]{3,0,1,2:T(4,128)S(1)} %fusion.49), kind=kOutput, calls=%fused_computation.20 | convolution fusion | flops 28901376 | bytes 771840 | tf_op jit(solution)/shard_map/conv_general_dilated | solution.py:37
  70.0 1.1 copy.193
  71.0 2.2 %collective-permute-start.5 = (f32[32,52,96]{2,0,1:T(8,128)}, f32[32,52,96]{2,0,1:T(8,128)}, u32[]{:S(2)}, u32[]{:S(2)}) collective-permute-start(f32[32,52,96]{2,0,1:T(8,128)} %copy.193), channel_id=1, source_target_pairs={{0,4},{4,0},{1,5},{5,1},{2,6},{6,2},{3,7},{7,3},{8,12},{12,8},{9,1... | collective-permute-start | bytes 1916936 | tf_op jit(solution)/shard_map/ppermute | solution.py:57
  74.0 1.6 %collective-permute-done.5 = f32[32,52,96]{2,0,1:T(8,128)} collective-permute-done((f32[32,52,96]{2,0,1:T(8,128)}, f32[32,52,96]{2,0,1:T(8,128)}, u32[]{:S(2)}, u32[]{:S(2)}) %collective-permute-start.5) | collective-permute-done | bytes 639008 | tf_op jit(solution)/shard_map/ppermute | solution.py:57
  75.7 2.5 %fusion.12 = bf16[32,52,96]{2,1,0:T(8,128)(2,1)} fusion(f32[32,4,96]{2,1,0:T(4,128)S(1)} %reshape.178, f32[32,48,96]{2,1,0:T(8,128)S(1)} %bitcast.75, f32[32,52,96]{2,0,1:T(8,128)} %collective-permute-done.5), kind=kLoop, calls=%fused_computation.22 | loop fusion | flops 479232 | bytes 1597440 | tf_op jit(solution)/shard_map/convert_element_type | solution.py:89
  78.1 5.8 %all-to-all-start.2 = ((bf16[32,52,96]{2,1,0:T(8,128)(2,1)}), bf16[32,52,96]{2,1,0:T(8,128)(2,1)S(1)}, u32[]{:S(2)}, u32[]{:S(2)}) async-start(bf16[32,52,96]{2,1,0:T(8,128)(2,1)} %fusion.12), calls=%async_computation.2 | async-start | bytes 917504 | tf_op jit(solution)/shard_map/all_to_all | solution.py:90
  84.4 3.4 %collective-permute-start.3 = (bf16[3,64,192]{2,0,1:T(4,128)(2,1)S(1)}, bf16[3,64,192]{2,0,1:T(4,128)(2,1)S(1)}, u32[]{:S(2)}, u32[]{:S(2)}) collective-permute-start(bf16[3,64,192]{2,0,1:T(4,128)(2,1)S(1)} %get-tuple-element.70), channel_id=1, source_target_pairs={{0,1},{1,2},{2,3},{4,5},{5,6},{6,7},{8,9},{9,10},{10,11},{12,13},{... | collective-permute-start | bytes 221192 | tf_op jit(solution)/shard_map/ppermute | solution.py:14
  87.8 1.3 collective-permute-start.4
  90.0 1.9 %collective-permute-done.3 = bf16[3,64,192]{2,0,1:T(4,128)(2,1)S(1)} collective-permute-done((bf16[3,64,192]{2,0,1:T(4,128)(2,1)S(1)}, bf16[3,64,192]{2,0,1:T(4,128)(2,1)S(1)}, u32[]{:S(2)}, u32[]{:S(2)}) %collective-permute-start.3) | collective-permute-done | bytes 73760 | tf_op jit(solution)/shard_map/ppermute | solution.py:14
  91.9 4.4 %collective-permute-done.4 = bf16[3,64,192]{2,0,1:T(4,128)(2,1)S(1)} collective-permute-done((bf16[3,64,192]{2,0,1:T(4,128)(2,1)S(1)}, bf16[3,64,192]{2,0,1:T(4,128)(2,1)S(1)}, u32[]{:S(2)}, u32[]{:S(2)}) %collective-permute-start.4) | collective-permute-done | bytes 73760 | tf_op jit(solution)/shard_map/ppermute | solution.py:17
  96.9 3.2 %all-to-all-done.2 = bf16[32,52,96]{2,1,0:T(8,128)(2,1)S(1)} async-done(((bf16[32,52,96]{2,1,0:T(8,128)(2,1)}), bf16[32,52,96]{2,1,0:T(8,128)(2,1)S(1)}, u32[]{:S(2)}, u32[]{:S(2)}) %all-to-all-start.2) | async-done | bytes 319520 | tf_op jit(solution)/shard_map/all_to_all | solution.py:90
  100.9 11.7 %all-to-all-start.3 = ((f32[16,7,96]{2,1,0:T(8,128)}), f32[16,7,96]{2,1,0:T(8,128)S(1)}, u32[]{:S(2)}, u32[]{:S(2)}) async-start(f32[16,7,96]{2,1,0:T(8,128)} %pad_maximum_fusion.6), calls=%async_computation.3 | async-start | bytes 131072 | tf_op jit(solution)/shard_map/all_to_all | solution.py:99
  112.6 1.2 convolution_select_fusion
  113.9 11.4 %all-to-all-done.3 = f32[16,7,96]{2,1,0:T(8,128)S(1)} async-done(((f32[16,7,96]{2,1,0:T(8,128)}), f32[16,7,96]{2,1,0:T(8,128)S(1)}, u32[]{:S(2)}, u32[]{:S(2)}) %all-to-all-start.3) | async-done | bytes 43040 | tf_op jit(solution)/shard_map/all_to_all | solution.py:99
  126.1 6.4 %all-to-all-start.4 = ((f32[32,7,96]{2,1,0:T(8,128)}), f32[32,7,96]{2,1,0:T(8,128)S(1)}, u32[]{:S(2)}, u32[]{:S(2)}) async-start(f32[32,7,96]{2,1,0:T(8,128)} %broadcast_in_dim.60), calls=%async_computation.4 | async-start | bytes 262144 | tf_op jit(solution)/shard_map/all_to_all | solution.py:62
  133.3 8.7 %all-to-all-done.4 = f32[32,7,96]{2,1,0:T(8,128)S(1)} async-done(((f32[32,7,96]{2,1,0:T(8,128)}), f32[32,7,96]{2,1,0:T(8,128)S(1)}, u32[]{:S(2)}, u32[]{:S(2)}) %all-to-all-start.4) | async-done | bytes 86048 | tf_op jit(solution)/shard_map/all_to_all | solution.py:62
  (112 shorter events, 18.8 us)
Async XLA Ops:
  2.0 29.9 %copy-start.2 = (bf16[1,4,64,192]{3,2,1,0:T(8,128)(2,1)S(1)}, bf16[1,4,64,192]{3,2,1,0:T(8,128)(2,1)}, u32[]{:S(2)}) copy-start(bf16[1,4,64,192]{3,2,1,0:T(8,128)(2,1)} %param.8) | copy-start | bytes 294916
  2.0 32.1 %all-to-all-start = ((bf16[16,3,384]{2,1,0:T(4,128)(2,1)}), bf16[16,3,384]{2,1,0:T(4,128)(2,1)S(1)}, u32[]{:S(2)}, u32[]{:S(2)}) async-start(bf16[16,3,384]{2,1,0:T(4,128)(2,1)} %broadcast_in_dim.23), calls=%async_computation | async-start | bytes 98304 | tf_op jit(solution)/shard_map/all_to_all | solution.py:62
  22.0 5.9 %collective-permute-start = (bf16[1,3,64,192]{3,2,1,0:T(8,128)(2,1)S(1)}, bf16[1,3,64,192]{3,2,1,0:T(8,128)(2,1)S(1)}, u32[]{:S(2)}, u32[]{:S(2)}) collective-permute-start(bf16[1,3,64,192]{3,2,1,0:T(8,128)(2,1)S(1)} %get-tuple-element.72), channel_id=1, source_target_pairs={{0,1},{1,2},{2,3},{4,5},{5,6},{6,7},{8,9},{9,10},{10,11},{12,13},{... | collective-permute-start | bytes 221192 | tf_op jit(solution)/shard_map/ppermute | solution.py:14
  25.4 6.5 %collective-permute-start.1 = (bf16[1,3,64,192]{3,2,1,0:T(8,128)(2,1)S(1)}, bf16[1,3,64,192]{3,2,1,0:T(8,128)(2,1)S(1)}, u32[]{:S(2)}, u32[]{:S(2)}) collective-permute-start(bf16[1,3,64,192]{3,2,1,0:T(8,128)(2,1)S(1)} %get-tuple-element.73), channel_id=1, source_target_pairs={{1,0},{2,1},{3,2},{5,4},{6,5},{7,6},{9,8},{10,9},{11,10},{13,12},{... | collective-permute-start | bytes 221192 | tf_op jit(solution)/shard_map/ppermute | solution.py:17
  34.0 8.4 %copy-start.11 = (f32[7,7,192]{2,1,0:T(8,128)S(1)}, f32[7,7,192]{2,1,0:T(8,128)}, u32[]{:S(2)}) copy-start(f32[7,7,192]{2,1,0:T(8,128)} %param.9) | copy-start | bytes 112900
  34.1 8.4 %copy-start.16 = (pred[8,9]{0,1:T(8,128)(4,1)S(1)}, pred[8,9]{0,1:T(8,128)(4,1)}, u32[]{:S(2)}) copy-start(pred[8,9]{0,1:T(8,128)(4,1)} %constant.111) | copy-start | bytes 220
  34.9 17.3 %all-to-all-start.1 = ((bf16[8,48,384]{2,1,0:T(8,128)(2,1)}), bf16[8,48,384]{2,1,0:T(8,128)(2,1)S(1)}, u32[]{:S(2)}, u32[]{:S(2)}) async-start(bf16[8,48,384]{2,1,0:T(8,128)(2,1)} %broadcast_in_dim.25), calls=%async_computation.1 | async-start | bytes 589824 | tf_op jit(solution)/shard_map/all_to_all | solution.py:62
  46.1 9.6 %copy-start.13 = (f32[192]{0:T(256)S(1)}, f32[192]{0:T(256)}, u32[]{:S(2)}) copy-start(f32[192]{0:T(256)} %param.10) | copy-start | bytes 2308
  46.1 9.5 %copy-start.15 = (f32[192]{0:T(256)S(1)}, f32[192]{0:T(256)}, u32[]{:S(2)}) copy-start(f32[192]{0:T(256)} %param.11) | copy-start | bytes 2308
  52.2 7.5 %copy-start = (bf16[8,48,384]{2,1,0:T(8,128)(2,1)}, bf16[8,48,384]{2,1,0:T(8,128)(2,1)S(1)}, u32[]{:S(2)}) copy-start(bf16[8,48,384]{2,1,0:T(8,128)(2,1)S(1)} %all-to-all-done.1) | copy-start | bytes 884740
  52.2 3.5 %collective-permute-start.2 = (bf16[384,384]{1,0:T(8,128)(2,1)S(1)}, bf16[384,384]{1,0:T(8,128)(2,1)S(1)}, u32[]{:S(2)}, u32[]{:S(2)}) collective-permute-start(bf16[384,384]{1,0:T(8,128)(2,1)S(1)} %bitcast.81), channel_id=1, source_target_pairs={{0,4},{4,0},{1,5},{5,1},{2,6},{6,2},{3,7},{7,3},{8,12},{12,8},{9,1... | collective-permute-start | bytes 884744 | tf_op jit(solution)/shard_map/ppermute | solution.py:57
  54.4 0.6 copy-start.3
  55.1 2.5 %copy-start.14 = (f32[192]{0:T(256)S(1)}, f32[192]{0:T(256)}, u32[]{:S(2)}) copy-start(f32[192]{0:T(256)} %param.14) | copy-start | bytes 2308
  55.7 2.0 %copy-start.9 = (bf16[384,384]{1,0:T(8,128)(2,1)}, bf16[384,384]{1,0:T(8,128)(2,1)S(1)}, u32[]{:S(2)}) copy-start(bf16[384,384]{1,0:T(8,128)(2,1)S(1)} %collective-permute-done.2) | copy-start | bytes 884740
  58.3 0.8 copy-start.6
  66.1 2.9 %copy-start.1 = (bf16[8,48,384]{2,1,0:T(8,128)(2,1)S(1)}, bf16[8,48,384]{2,1,0:T(8,128)(2,1)}, u32[]{:S(2)}) copy-start(bf16[8,48,384]{2,1,0:T(8,128)(2,1)} %copy-done) | copy-start | bytes 884740
  66.1 2.9 %copy-start.10 = (bf16[384,384]{1,0:T(8,128)(2,1)S(1)}, bf16[384,384]{1,0:T(8,128)(2,1)}, u32[]{:S(2)}) copy-start(bf16[384,384]{1,0:T(8,128)(2,1)} %copy-done.9) | copy-start | bytes 884740
  71.0 4.6 %collective-permute-start.5 = (f32[32,52,96]{2,0,1:T(8,128)}, f32[32,52,96]{2,0,1:T(8,128)}, u32[]{:S(2)}, u32[]{:S(2)}) collective-permute-start(f32[32,52,96]{2,0,1:T(8,128)} %copy.193), channel_id=1, source_target_pairs={{0,4},{4,0},{1,5},{5,1},{2,6},{6,2},{3,7},{7,3},{8,12},{12,8},{9,1... | collective-permute-start | bytes 1916936 | tf_op jit(solution)/shard_map/ppermute | solution.py:57
  78.1 5.8 %copy-start.4 = (f32[4,64]{0,1:T(8,128)S(1)}, f32[4,64]{0,1:T(8,128)}, u32[]{:S(2)}) copy-start(f32[4,64]{0,1:T(8,128)} %copy-done.3) | copy-start | bytes 3076
  78.1 5.8 %copy-start.7 = (f32[4,64]{0,1:T(8,128)S(1)}, f32[4,64]{0,1:T(8,128)}, u32[]{:S(2)}) copy-start(f32[4,64]{0,1:T(8,128)} %copy.176) | copy-start | bytes 3076
  78.1 5.8 %copy-start.8 = (f32[4,64]{0,1:T(8,128)S(1)}, f32[4,64]{0,1:T(8,128)}, u32[]{:S(2)}) copy-start(f32[4,64]{0,1:T(8,128)} %copy.177) | copy-start | bytes 3076
  78.1 11.0 %copy-start.12 = (f32[7,7,192]{2,1,0:T(8,128)S(1)}, f32[7,7,192]{2,1,0:T(8,128)}, u32[]{:S(2)}) copy-start(f32[7,7,192]{2,1,0:T(8,128)} %param.9) | copy-start | bytes 112900
  78.1 22.0 %all-to-all-start.2 = ((bf16[32,52,96]{2,1,0:T(8,128)(2,1)}), bf16[32,52,96]{2,1,0:T(8,128)(2,1)S(1)}, u32[]{:S(2)}, u32[]{:S(2)}) async-start(bf16[32,52,96]{2,1,0:T(8,128)(2,1)} %fusion.12), calls=%async_computation.2 | async-start | bytes 917504 | tf_op jit(solution)/shard_map/all_to_all | solution.py:90
  84.4 7.5 %collective-permute-start.3 = (bf16[3,64,192]{2,0,1:T(4,128)(2,1)S(1)}, bf16[3,64,192]{2,0,1:T(4,128)(2,1)S(1)}, u32[]{:S(2)}, u32[]{:S(2)}) collective-permute-start(bf16[3,64,192]{2,0,1:T(4,128)(2,1)S(1)} %get-tuple-element.70), channel_id=1, source_target_pairs={{0,1},{1,2},{2,3},{4,5},{5,6},{6,7},{8,9},{9,10},{10,11},{12,13},{... | collective-permute-start | bytes 221192 | tf_op jit(solution)/shard_map/ppermute | solution.py:14
  87.8 8.5 %collective-permute-start.4 = (bf16[3,64,192]{2,0,1:T(4,128)(2,1)S(1)}, bf16[3,64,192]{2,0,1:T(4,128)(2,1)S(1)}, u32[]{:S(2)}, u32[]{:S(2)}) collective-permute-start(bf16[3,64,192]{2,0,1:T(4,128)(2,1)S(1)} %get-tuple-element.71), channel_id=1, source_target_pairs={{1,0},{2,1},{3,2},{5,4},{6,5},{7,6},{9,8},{10,9},{11,10},{13,12},{... | collective-permute-start | bytes 221192 | tf_op jit(solution)/shard_map/ppermute | solution.py:17
  96.8 15.8 %copy-start.17 = (pred[8,9]{0,1:T(8,128)(4,1)S(1)}, pred[8,9]{0,1:T(8,128)(4,1)}, u32[]{:S(2)}) copy-start(pred[8,9]{0,1:T(8,128)(4,1)} %constant.111) | copy-start | bytes 220
  100.9 24.4 %all-to-all-start.3 = ((f32[16,7,96]{2,1,0:T(8,128)}), f32[16,7,96]{2,1,0:T(8,128)S(1)}, u32[]{:S(2)}, u32[]{:S(2)}) async-start(f32[16,7,96]{2,1,0:T(8,128)} %pad_maximum_fusion.6), calls=%async_computation.3 | async-start | bytes 131072 | tf_op jit(solution)/shard_map/all_to_all | solution.py:99
  113.8 18.7 %copy-start.5 = (bf16[1,4,64,192]{3,2,1,0:T(8,128)(2,1)S(1)}, bf16[1,4,64,192]{3,2,1,0:T(8,128)(2,1)}, u32[]{:S(2)}) copy-start(bf16[1,4,64,192]{3,2,1,0:T(8,128)(2,1)} %param.15) | copy-start | bytes 294916
  126.1 16.0 %all-to-all-start.4 = ((f32[32,7,96]{2,1,0:T(8,128)}), f32[32,7,96]{2,1,0:T(8,128)S(1)}, u32[]{:S(2)}, u32[]{:S(2)}) async-start(f32[32,7,96]{2,1,0:T(8,128)} %broadcast_in_dim.60), calls=%async_computation.4 | async-start | bytes 262144 | tf_op jit(solution)/shard_map/all_to_all | solution.py:62

commit v2 on v0

v2 whole, which is shorter than its diff:
```python
import jax
import jax.numpy as jnp
from jax import lax
from jax.experimental import pallas as pl
from jax.experimental.pallas import tpu as pltpu
from jax.sharding import Mesh, PartitionSpec as P

DEPTH, HEIGHT, CORES, QUARTERS = 16, 8, 2, 4
DP = ("z", "y", "core")
PEERS = HEIGHT * QUARTERS
ROWS, COLS, WIDTH, TAPS = 4, 64, 192, 7
CELLS = ROWS * COLS
HALO = TAPS // 2
PART = WIDTH // 2
UNITS = 3
HALF = HEIGHT * DEPTH * UNITS
BLOCK = DEPTH * UNITS
MARGIN = 8
F32, BF16 = jnp.float32, jnp.bfloat16
SMALL_ROWS = 4


def kernel_call(body, outs, scratch=(), name=None, cost=None):
    return pl.pallas_call(
        body,
        out_shape=[jax.ShapeDtypeStruct(shape, kind) for shape, kind in outs],
        scratch_shapes=list(scratch),
        compiler_params=pltpu.CompilerParams(vmem_limit_bytes=40 * 2**20),
        name=name,
        cost_estimate=cost,
    )


def dot(a, b):
    return jnp.dot(a, b, preferred_element_type=F32)


def dot_rows(a, b):
    return lax.dot_general(a, b, (((0,), (0,)), ((), ())), preferred_element_type=F32)


def fill_padded(padded, low, block, high):
    padded[:, :MARGIN, :] = jnp.zeros((ROWS + 2 * HALO, MARGIN, WIDTH), F32)
    padded[:, MARGIN + COLS :, :] = jnp.zeros((ROWS + 2 * HALO, MARGIN, WIDTH), F32)
    inside = slice(MARGIN, MARGIN + COLS)
    padded[:HALO, inside, :] = low[...].astype(F32)
    padded[HALO : HALO + ROWS, inside, :] = block[...].astype(F32)
    padded[HALO + ROWS :, inside, :] = high[...].astype(F32)


def convolve(padded, tap, finish):
    chunk = 32
    for start in range(0, COLS, chunk):
        acc = [None] * ROWS
        for i in range(ROWS + 2 * HALO):
            for b in range(TAPS):
                first = MARGIN - HALO + b + start
                shifted = padded[i, first : first + chunk, :]
                for r in range(ROWS):
                    if 0 <= i - r < TAPS:
                        term = shifted * tap(i - r, b)
                        acc[r] = term if acc[r] is None else acc[r] + term
        for r in range(ROWS):
            finish(r, start, chunk, acc[r])


def forward_kernel(
    tokens, low, high, taps, gain, shift, scale, cotangent,
    padded, normed, inv_std, norm_halves, norm_t, up_halves, up_t, mixed,
):
    fill_padded(padded, low, tokens, high)

    def finish(r, start, chunk, value):
        mixed[r * COLS + start : r * COLS + start + chunk, :] = value

    convolve(padded, lambda a, b: taps[a, b : b + 1, :], finish)
    value = mixed[...]
    centre = value - jnp.mean(value, -1, keepdims=True)
    inv = lax.rsqrt(jnp.mean(centre * centre, -1, keepdims=True) + 1e-06)
    norm = centre * inv
    normed[...] = norm
    inv_std[...] = inv
    rounded = (norm * gain[...] + shift[...]).astype(BF16)
    upstream = (cotangent[...].reshape(CELLS, WIDTH).astype(F32) * scale[...]).astype(BF16)
    for h in range(2):
        norm_halves[h] = rounded[:, h * PART : (h + 1) * PART]
        up_halves[h] = upstream[:, h * PART : (h + 1) * PART]
    norm_t[...] = rounded.T
    up_t[...] = upstream.T


def main_kernel(
    own, other, tokens, cotangent, padded, normed, inv_std, norm_halves, norm_t, up_halves, up_t,
    gain, scale, mine, theirs, block_out, mixed_grad, smalls, grad_rows,
):
    branch = jnp.zeros((CELLS, WIDTH), F32)
    normed_grad = jnp.zeros((CELLS, WIDTH), F32)
    for weights, out in ((other, theirs), (own, mine)):
        expand, reduce = weights[:, :WIDTH], weights[:, WIDTH:]
        pre = dot(expand, norm_t[...])
        hidden_grad = dot(reduce, up_t[...])
        cumulative = 0.5 * (1.0 + lax.erf(pre * 0.7071067811865476))
        hidden = (pre * cumulative).astype(BF16)
        slope = cumulative + pre * jnp.exp(-0.5 * pre * pre) * 0.3989422804014327
        pre_grad = (hidden_grad * slope).astype(BF16)
        for q in range(QUARTERS):
            left, right = (pre_grad, norm_halves) if q < 2 else (hidden, up_halves)
            grad = dot(left, right[q % 2])
            for y in range(HEIGHT):
                base = y * BLOCK
                piece = y * QUARTERS + q
                out[piece, 0:40, 0:PART] = grad[base : base + 40]
                tail = grad[base + 40 : base + 48]
                for k in range(3):
                    out[piece, 8 * k : 8 * k + 8, PART:128] = tail[:, 32 * k : 32 * k + 32]
        branch += dot_rows(hidden, reduce)
        normed_grad += dot_rows(pre_grad, expand)
    flat = tokens[...].reshape(CELLS, WIDTH).astype(F32)
    block_out[...] = (flat + scale[...] * branch).astype(BF16).reshape(ROWS, COLS, WIDTH)
    norm = normed[...]
    upstream = cotangent[...].reshape(CELLS, WIDTH).astype(F32)
    smalls[TAPS * TAPS :, :] = jnp.zeros((64 - TAPS * TAPS, WIDTH), F32)
    smalls[49:50, :] = jnp.sum(normed_grad * norm, 0, keepdims=True)
    smalls[50:51, :] = jnp.sum(normed_grad, 0, keepdims=True)
    smalls[51:52, :] = jnp.sum(upstream * branch, 0, keepdims=True)
    scaled = normed_grad * gain[...]
    grad = inv_std[...] * (
        scaled
        - jnp.mean(scaled, -1, keepdims=True)
        - norm * jnp.mean(scaled * norm, -1, keepdims=True)
    )
    grad_rows[...] = grad.reshape(ROWS, COLS, WIDTH)
    mixed_grad[...] = grad.astype(BF16).reshape(ROWS, COLS, WIDTH)
    for b in range(TAPS):
        acc = [None] * TAPS
        for i in range(ROWS + 2 * HALO):
            first = MARGIN - HALO + b
            shifted = padded[i, first : first + COLS, :]
            for r in range(ROWS):
                a = i - r
                if 0 <= a < TAPS:
                    product = (shifted * grad_rows[r]).reshape(COLS // 8, 8, WIDTH)
                    term = jnp.sum(product, 0)
                    acc[a] = term if acc[a] is None else acc[a] + term
        for a in range(TAPS):
            row = a * TAPS + b
            smalls[row : row + 1, :] = jnp.sum(acc[a], 0, keepdims=True)
    for piece in range(PEERS):
        row = SMALL_ROWS * (piece % 16)
        lane = PART * (piece // 16)
        values = smalls[row : row + SMALL_ROWS, lane : lane + PART]
        for out in (mine, theirs):
            for k in range(3):
                at = 24 + SMALL_ROWS * k
                out[piece, at : at + SMALL_ROWS, PART:128] = values[:, 32 * k : 32 * k + 32]
            out[piece, 36:40, PART:128] = jnp.zeros((4, 32), F32)


def middle_kernel(arrived, column):
    total = arrived[0].astype(F32)
    for p in range(1, PEERS):
        total += arrived[p].astype(F32)
    tail = jnp.concatenate([total[8 * k : 8 * k + 8, PART:128] for k in range(3)], 1)
    grad = jnp.concatenate([total[:, :PART], tail], 0)
    at = [24 + SMALL_ROWS * k for k in range(3)]
    small = jnp.concatenate([total[i : i + SMALL_ROWS, PART:128] for i in at], 1)
    for z in range(DEPTH):
        column[z, 0:UNITS, :] = grad[z * UNITS : (z + 1) * UNITS]
        column[z, UNITS : UNITS + SMALL_ROWS, :] = small
        column[z, UNITS + SMALL_ROWS :, :] = jnp.zeros((1, PART), F32)


def spread_kernel(arrived, copies):
    total = jnp.sum(arrived[...], 0)
    for p in range(PEERS):
        copies[p] = total


def final_kernel(height, done, kernel_grad, gain_grad, shift_grad, scale_grad, expand, reduce):
    y = height[0]
    for q in range(QUARTERS):
        out = expand if q < 2 else reduce
        out[:, (q % 2) * PART : (q % 2 + 1) * PART] = done[y * QUARTERS + q, 0:UNITS, :]
    for row in range(TAPS * TAPS + 3):
        p, i = row // SMALL_ROWS, UNITS + row % SMALL_ROWS
        value = jnp.concatenate([done[p, i : i + 1, :], done[16 + p, i : i + 1, :]], 1)
        if row < TAPS * TAPS:
            kernel_grad[row // TAPS, row % TAPS : row % TAPS + 1, :] = value
        else:
            (gain_grad, shift_grad, scale_grad)[row - TAPS * TAPS][...] = value


def backward_kernel(grad, low, high, taps, cotangent, out, padded):
    fill_padded(padded, low, grad, high)

    def finish(r, start, chunk, value):
        upstream = cotangent[r, start : start + chunk, :].astype(F32)
        out[r, start : start + chunk, :] = (upstream + value).astype(BF16)

    convolve(padded, lambda a, b: taps[TAPS - 1 - a, TAPS - 1 - b : TAPS - b, :], finish)


def neighbours(block):
    forward = [(i, i + 1) for i in range(QUARTERS - 1)]
    backward = [(target, source) for source, target in forward]
    low = lax.ppermute(block[ROWS - HALO :], "space", forward)
    high = lax.ppermute(block[:HALO], "space", backward)
    return low, high


def other_core(x):
    return lax.ppermute(x, "core", [(0, 1), (1, 0)])


def exchange(x, axes):
    return lax.all_to_all(x, axes, 0, 0, tiled=True)


def shards(
    pressure_tokens, dw_kernel, norm_gain, norm_shift, w_expand, w_reduce, layer_scale, cotangent
):
    tokens, upstream = pressure_tokens[0], cotangent[0]
    gain, shift, scale = norm_gain[None], norm_shift[None], layer_scale[None]

    def copies(x):
        return jnp.broadcast_to(x[None], (DEPTH,) + x.shape)

    column = exchange(jnp.concatenate([copies(w_expand), copies(w_reduce)], 2), "z")
    column, tokens = lax.optimization_barrier((column, tokens))
    plane = column.reshape(1, BLOCK, 2 * WIDTH)
    own = exchange(jnp.broadcast_to(plane, (HEIGHT, BLOCK, 2 * WIDTH)), "y")
    low, high = neighbours(tokens)
    padded, normed, inv_std, norm_halves, norm_t, up_halves, up_t = kernel_call(
        forward_kernel,
        [
            ((ROWS + 2 * HALO, COLS + 2 * MARGIN, WIDTH), F32),
            ((CELLS, WIDTH), F32),
            ((CELLS, 1), F32),
            ((2, CELLS, PART), BF16),
            ((WIDTH, CELLS), BF16),
            ((2, CELLS, PART), BF16),
            ((WIDTH, CELLS), BF16),
        ],
        [pltpu.VMEM((CELLS, WIDTH), F32)],
        "forward",
        pl.CostEstimate(flops=8_000_000, bytes_accessed=2_000_000, transcendentals=256),
    )(tokens, low, high, dw_kernel, gain, shift, scale, upstream)
    own = own.reshape(HALF, 2 * WIDTH)
    other = other_core(own)
    mine, theirs, block_out, mixed_grad = kernel_call(
        main_kernel,
        [
            ((PEERS, 40, 128), F32),
            ((PEERS, 40, 128), F32),
            ((ROWS, COLS, WIDTH), BF16),
            ((ROWS, COLS, WIDTH), BF16),
        ],
        [pltpu.VMEM((64, WIDTH), F32), pltpu.VMEM((ROWS, COLS, WIDTH), F32)],
        "main",
        pl.CostEstimate(flops=500_000_000, bytes_accessed=4_000_000, transcendentals=400_000),
    )(
        own, other, tokens, upstream, padded, normed, inv_std, norm_halves, norm_t, up_halves,
        up_t, gain, scale,
    )
    sums = (mine + other_core(theirs)).astype(BF16)
    sums, mixed_grad = lax.optimization_barrier((sums, mixed_grad))
    arrived = exchange(sums, ("y", "space"))
    grad_low, grad_high = neighbours(mixed_grad)
    (column,) = kernel_call(middle_kernel, [((DEPTH, 8, PART), F32)], name="middle")(arrived)
    column = exchange(column, "z")
    column, mixed_grad, grad_low, grad_high = lax.optimization_barrier(
        (column, mixed_grad, grad_low, grad_high)
    )
    (spread,) = kernel_call(spread_kernel, [((PEERS, 8, PART), F32)], name="spread")(column)
    done = exchange(spread, ("y", "space"))
    (grad_tokens,) = kernel_call(
        backward_kernel,
        [((ROWS, COLS, WIDTH), BF16)],
        [pltpu.VMEM((ROWS + 2 * HALO, COLS + 2 * MARGIN, WIDTH), F32)],
        "backward",
        pl.CostEstimate(flops=8_000_000, bytes_accessed=1_000_000, transcendentals=0),
    )(mixed_grad, grad_low, grad_high, dw_kernel, upstream)
    kernel_grad, gain_grad, shift_grad, scale_grad, grad_expand, grad_reduce = pl.pallas_call(
        final_kernel,
        out_shape=[
            jax.ShapeDtypeStruct(shape, F32)
            for shape in [(TAPS, TAPS, WIDTH)] + [(1, WIDTH)] * 3 + [(UNITS, WIDTH)] * 2
        ],
        in_specs=[
            pl.BlockSpec(memory_space=pltpu.SMEM),
            pl.BlockSpec(memory_space=pltpu.VMEM),
        ],
        compiler_params=pltpu.CompilerParams(vmem_limit_bytes=40 * 2**20),
        name="final",
    )(lax.axis_index("y").reshape(1), done)
    return (
        block_out[None],
        grad_tokens[None],
        kernel_grad,
        gain_grad[0],
        shift_grad[0],
        grad_expand,
        grad_reduce,
        scale_grad[0],
    )


def solution(mesh):
    grid = Mesh(mesh.devices.reshape(DEPTH, HEIGHT, CORES, QUARTERS), DP + ("space",))
    tokens, units = P(DP, "space", None, None), P(DP, None)
    in_specs = (tokens, P(), P(), P(), units, units, P(), tokens)
    out_specs = (tokens, tokens, P(), P(), P(), units, units, P())
    return jax.shard_map(shards, mesh=grid, in_specs=in_specs, out_specs=out_specs, check_vma=False)
```

time: 622 us -> 127 us (0.20)
  the two profiles are of different devices: /device:TPU:24 before, /device:TPU:8 now
where the time goes in v2:
time: 127 us; the launch traced here: 126 us
  blocking collectives  67.7 us (53%)
  waiting for transfers between devices  23.7 us (19%)
  starting transfers between devices  20.5 us (16%)
  Pallas kernels  11.9 us (9%)
  local copies, waits for them, and re-layouts  1.49 us (1%)
    all_to_all x3, blocking collectives, exchange(): return lax.all_to_all(x, axes, 0, 0, tiled=True)  67.7 us
    all_to_all x2, waiting for transfers between devices, exchange(): return lax.all_to_all(x, axes, 0, 0, tiled=True)  10.9 us
    ppermute x2, waiting for transfers between devices, neighbours(): high = lax.ppermute(block[:HALO], 'space', backward)  8.44 us
    all_to_all x2, starting transfers between devices, exchange(): return lax.all_to_all(x, axes, 0, 0, tiled=True)  8.27 us
    ppermute x2, starting transfers between devices, neighbours(): low = lax.ppermute(block[ROWS - HALO:], 'space', forward)  5.71 us
    pallas_call x1, Pallas kernels, shards(): kernel_call(main_kernel, [((PEERS, 40, 128), F32), ((PEERS, 40, 128), F32...  4.72 us
    ppermute x2, starting transfers between devices, other_core(): return lax.ppermute(x, 'core', [(0, 1), (1, 0)])  3.95 us
    ppermute x2, starting transfers between devices, neighbours(): high = lax.ppermute(block[:HALO], 'space', backward)  2.58 us
  transfers between devices with their start and end apart: 8, of which 7 were waited for; matrix products, arithmetic and copies ran while one was open for 0% of the time, Pallas kernels for 4%

profile of v2, /device:TPU:8, one launch (start us, length us, event | category | flops | bytes accessed | tf_op | source)
XLA Modules:
  0.0 126.4 jit_solution(12737450132557367922)
XLA Ops:
  0.6 0.7 broadcast_in_dim.34
  1.4 0.1 pad_maximum_fusion
  1.5 31.3 %all_to_all.25 = bf16[16,3,384]{2,1,0:T(4,128)(2,1)S(1)} all-to-all(bf16[16,3,384]{2,1,0:T(4,128)(2,1)S(1)} %pad_maximum_fusion), channel_id=1, replica_groups=mesh['z'=16,'y'=8,'core'=2,'space'=4] {'z'}, dimensions={0} | all-to-all | bytes 73728 | tf_op jit(solution)/shard_map/all_to_all | solution.py:216
  32.9 0.0 copy-start
  32.9 17.2 %all_to_all.26 = bf16[8,48,384]{2,1,0:T(8,128)(2,1)S(1)} all-to-all(bf16[8,48,384]{2,1,0:T(8,128)(2,1)S(1)} %broadcast_in_dim.37), channel_id=1, replica_groups=mesh['z'=16,'y'=8,'core'=2,'space'=4] {'y'}, dimensions={0} | all-to-all | bytes 589824 | tf_op jit(solution)/shard_map/all_to_all | solution.py:216
  50.1 2.0 %collective-permute-start = (bf16[384,384]{1,0:T(8,128)(2,1)S(1)}, bf16[384,384]{1,0:T(8,128)(2,1)S(1)}, u32[]{:S(2)}, u32[]{:S(2)}) collective-permute-start(bf16[384,384]{1,0:T(8,128)(2,1)S(1)} %bitcast.18), channel_id=1, source_target_pairs={{0,4},{4,0},{1,5},{5,1},{2,6},{6,2},{3,7},{7,3},{8,12},{12,8},{9,1... | collective-permute-start | bytes 884744 | tf_op jit(solution)/shard_map/ppermute | solution.py:212
  52.1 0.0 copy-start.4
  52.2 0.0 copy-start.5
  52.2 3.4 %collective-permute-start.1 = (bf16[3,64,192]{2,1,0:T(8,128)(2,1)S(1)}, bf16[3,64,192]{2,1,0:T(8,128)(2,1)S(1)}, u32[]{:S(2)}, u32[]{:S(2)}) collective-permute-start(bf16[3,64,192]{2,1,0:T(8,128)(2,1)S(1)} %get-tuple-element.61), channel_id=1, source_target_pairs={{0,1},{1,2},{2,3},{4,5},{5,6},{6,7},{8,9},{9,10},{10,11},{12,13},{... | collective-permute-start | bytes 221192 | tf_op jit(solution)/shard_map/ppermute | solution.py:206
  55.6 1.3 %collective-permute-start.2 = (bf16[3,64,192]{2,1,0:T(8,128)(2,1)S(1)}, bf16[3,64,192]{2,1,0:T(8,128)(2,1)S(1)}, u32[]{:S(2)}, u32[]{:S(2)}) collective-permute-start(bf16[3,64,192]{2,1,0:T(8,128)(2,1)S(1)} %get-tuple-element.60), channel_id=1, source_target_pairs={{1,0},{2,1},{3,2},{5,4},{6,5},{7,6},{9,8},{10,9},{11,10},{13,12},{... | collective-permute-start | bytes 221192 | tf_op jit(solution)/shard_map/ppermute | solution.py:207
  56.9 1.4 %collective-permute-done.1.low = bf16[3,64,192]{2,1,0:T(8,128)(2,1)S(1)} collective-permute-done((bf16[3,64,192]{2,1,0:T(8,128)(2,1)S(1)}, bf16[3,64,192]{2,1,0:T(8,128)(2,1)S(1)}, u32[]{:S(2)}, u32[]{:S(2)}) %collective-permute-start.1) | collective-permute-done | bytes 73760 | tf_op jit(solution)/shard_map/ppermute | solution.py:206
  58.3 4.1 %collective-permute-done.2.high = bf16[3,64,192]{2,1,0:T(8,128)(2,1)S(1)} collective-permute-done((bf16[3,64,192]{2,1,0:T(8,128)(2,1)S(1)}, bf16[3,64,192]{2,1,0:T(8,128)(2,1)S(1)}, u32[]{:S(2)}, u32[]{:S(2)}) %collective-permute-start.2) | collective-permute-done | bytes 73760 | tf_op jit(solution)/shard_map/ppermute | solution.py:207
  62.4 0.7 copy-done.3
  63.1 2.5 %forward.1 = (f32[10,80,192]{2,1,0:T(8,128)S(1)}, f32[256,192]{1,0:T(8,128)S(1)}, f32[256,1]{1,0:T(8,128)S(1)}, bf16[2,256,96]{2,1,0:T(8,128)(2,1)S(1)}, bf16[19...) custom-call(bf16[4,64,192]{2,1,0:T(8,128)(2,1)S(1)} %bitcast.13, ...), custom_call_target="tpu_custom_call" | custom-call | flops 8000000 | bytes 2000000 | tf_op jit(solution)/shard_map/forward/pallas_call | solution.py:233
  65.6 0.0 collective-permute-done.other
  65.6 4.7 %main.1 = (f32[32,40,128]{2,1,0:T(8,128)S(1)}, f32[32,40,128]{2,1,0:T(8,128)S(1)}, bf16[4,64,192]{2,1,0:T(8,128)(2,1)}, bf16[4,64,192]{2,1,0:T(8,128)(2,1)S(1)}) custom-call(bf16[384,384]{1,0:T(8,128)(2,1)S(1)} %bitcast.19, bf16[384,384]{1,0:T(8,128)(2,1)S(1)} %collective-permute-done.other, bf16[4,64,192]{2,1,0:T(8,128)(2,1)S(1)} %bitcast.14, ...), custom_call_target="tpu_custom_call" | custom-call | flops 500000000 | bytes 4000000 | tf_op jit(solution)/shard_map/main/pallas_call | solution.py:250
  70.3 1.9 %collective-permute-start.3 = (f32[32,40,128]{2,1,0:T(8,128)S(1)}, f32[32,40,128]{2,1,0:T(8,128)S(1)}, u32[]{:S(2)}, u32[]{:S(2)}) collective-permute-start(f32[32,40,128]{2,1,0:T(8,128)S(1)} %get-tuple-element.44), channel_id=1, source_target_pairs={{0,4},{4,0},{1,5},{5,1},{2,6},{6,2},{3,7},{7,3},{8,12},{12,8},{9,1... | collective-permute-start | bytes 1966088 | tf_op jit(solution)/shard_map/ppermute | solution.py:212
  72.3 2.1 %collective-permute-done.3 = f32[32,40,128]{2,1,0:T(8,128)S(1)} collective-permute-done((f32[32,40,128]{2,1,0:T(8,128)S(1)}, f32[32,40,128]{2,1,0:T(8,128)S(1)}, u32[]{:S(2)}, u32[]{:S(2)}) %collective-permute-start.3) | collective-permute-done | bytes 655392 | tf_op jit(solution)/shard_map/ppermute | solution.py:212
  74.3 0.1 add_convert_fusion
  74.4 19.1 %all_to_all.27.arrived = bf16[32,40,128]{2,1,0:T(8,128)(2,1)S(1)} all-to-all(bf16[32,40,128]{2,1,0:T(8,128)(2,1)S(1)} %add_convert_fusion), channel_id=1, replica_groups=mesh['z'=16,'y'=8,'core'=2,'space'=4] {'y','space'}, dimensions={0} | all-to-all | bytes 655360 | tf_op jit(solution)/shard_map/all_to_all | solution.py:216
  93.6 0.8 middle.1
  94.3 3.5 %all-to-all-start.3 = ((f32[16,8,96]{2,1,0:T(8,128)}), f32[16,8,96]{2,1,0:T(8,128)S(1)}, u32[]{:S(2)}, u32[]{:S(2)}) async-start(f32[16,8,96]{2,1,0:T(8,128)} %middle.1), calls=%async_computation.3 | async-start | bytes 131072 | tf_op jit(solution)/shard_map/all_to_all | solution.py:216
  97.8 2.3 %collective-permute-start.4 = (bf16[3,64,192]{2,1,0:T(8,128)(2,1)S(1)}, bf16[3,64,192]{2,1,0:T(8,128)(2,1)S(1)}, u32[]{:S(2)}, u32[]{:S(2)}) collective-permute-start(bf16[3,64,192]{2,1,0:T(8,128)(2,1)S(1)} %get-tuple-element.59), channel_id=1, source_target_pairs={{0,1},{1,2},{2,3},{4,5},{5,6},{6,7},{8,9},{9,10},{10,11},{12,13},{... | collective-permute-start | bytes 221192 | tf_op jit(solution)/shard_map/ppermute | solution.py:206
  100.2 1.3 %collective-permute-start.5 = (bf16[3,64,192]{2,1,0:T(8,128)(2,1)S(1)}, bf16[3,64,192]{2,1,0:T(8,128)(2,1)S(1)}, u32[]{:S(2)}, u32[]{:S(2)}) collective-permute-start(bf16[3,64,192]{2,1,0:T(8,128)(2,1)S(1)} %get-tuple-element.58), channel_id=1, source_target_pairs={{1,0},{2,1},{3,2},{5,4},{6,5},{7,6},{9,8},{10,9},{11,10},{13,12},{... | collective-permute-start | bytes 221192 | tf_op jit(solution)/shard_map/ppermute | solution.py:207
  101.5 0.9 collective-permute-done.4.low
  102.4 4.3 %collective-permute-done.5.high = bf16[3,64,192]{2,1,0:T(8,128)(2,1)S(1)} collective-permute-done((bf16[3,64,192]{2,1,0:T(8,128)(2,1)S(1)}, bf16[3,64,192]{2,1,0:T(8,128)(2,1)S(1)}, u32[]{:S(2)}, u32[]{:S(2)}) %collective-permute-start.5) | collective-permute-done | bytes 73760 | tf_op jit(solution)/shard_map/ppermute | solution.py:207
  106.7 3.9 %all-to-all-done.3.arrived = f32[16,8,96]{2,1,0:T(8,128)S(1)} async-done(((f32[16,8,96]{2,1,0:T(8,128)}), f32[16,8,96]{2,1,0:T(8,128)S(1)}, u32[]{:S(2)}, u32[]{:S(2)}) %all-to-all-start.3) | async-done | bytes 49184 | tf_op jit(solution)/shard_map/all_to_all | solution.py:216
  110.6 0.7 spread.1
  111.3 4.8 %all-to-all-start.4 = ((f32[32,8,96]{2,1,0:T(8,128)}), f32[32,8,96]{2,1,0:T(8,128)S(1)}, u32[]{:S(2)}, u32[]{:S(2)}) async-start(f32[32,8,96]{2,1,0:T(8,128)} %spread.1), calls=%async_computation.4 | async-start | bytes 262144 | tf_op jit(solution)/shard_map/all_to_all | solution.py:216
  116.1 2.5 %backward.1 = bf16[4,64,192]{2,1,0:T(8,128)(2,1)} custom-call(bf16[4,64,192]{2,1,0:T(8,128)(2,1)S(1)} %get-tuple-element.48.grad, bf16[3,64,192]{2,1,0:T(8,128)(2,1)S(1)} %collective-permute-done.4.low, bf16[3,64,192]{2,1,0:T(8,128)(2,1)S(1)} %collective-permute-done.5.high, f32[7,7,192]{2,1,0:T(8,128)S(1)} %copy-done.2, bf16[4,64,192]{2,1,0:T(8,128)(2,1)S(1)} %bitcast.17), custom_call_target="tpu_custom_call" | custom-call | flops 8000000 | bytes 1000000 | tf_op jit(solution)/shard_map/backward/pallas_call | solution.py:276
  118.6 7.0 %all-to-all-done.4.done = f32[32,8,96]{2,1,0:T(8,128)S(1)} async-done(((f32[32,8,96]{2,1,0:T(8,128)}), f32[32,8,96]{2,1,0:T(8,128)S(1)}, u32[]{:S(2)}, u32[]{:S(2)}) %all-to-all-start.4) | async-done | bytes 98336 | tf_op jit(solution)/shard_map/all_to_all | solution.py:216
  125.6 0.8 final.1
  (15 shorter events, 0.1 us)
Async XLA Ops:
  0.6 0.7 copy-start.6
  32.9 19.3 %copy-start = (bf16[1,4,64,192]{3,2,1,0:T(8,128)(2,1)S(1)}, bf16[1,4,64,192]{3,2,1,0:T(8,128)(2,1)}, u32[]{:S(2)}) copy-start(bf16[1,4,64,192]{3,2,1,0:T(8,128)(2,1)} %param.8) | copy-start | bytes 294916
  50.1 12.3 %copy-start.1 = (bf16[1,4,64,192]{3,2,1,0:T(8,128)(2,1)S(1)}, bf16[1,4,64,192]{3,2,1,0:T(8,128)(2,1)}, u32[]{:S(2)}) copy-start(bf16[1,4,64,192]{3,2,1,0:T(8,128)(2,1)} %param.15) | copy-start | bytes 294916
  50.1 12.3 %copy-start.2 = (f32[7,7,192]{2,1,0:T(8,128)S(1)}, f32[7,7,192]{2,1,0:T(8,128)}, u32[]{:S(2)}) copy-start(f32[7,7,192]{2,1,0:T(8,128)} %taps.3) | copy-start | bytes 112900
  50.1 15.5 %collective-permute-start = (bf16[384,384]{1,0:T(8,128)(2,1)S(1)}, bf16[384,384]{1,0:T(8,128)(2,1)S(1)}, u32[]{:S(2)}, u32[]{:S(2)}) collective-permute-start(bf16[384,384]{1,0:T(8,128)(2,1)S(1)} %bitcast.18), channel_id=1, source_target_pairs={{0,4},{4,0},{1,5},{5,1},{2,6},{6,2},{3,7},{7,3},{8,12},{12,8},{9,1... | collective-permute-start | bytes 884744 | tf_op jit(solution)/shard_map/ppermute | solution.py:212
  52.1 10.3 %copy-start.4 = (f32[192]{0:T(256)S(1)}, f32[192]{0:T(256)}, u32[]{:S(2)}) copy-start(f32[192]{0:T(256)} %param.14) | copy-start | bytes 2308
  52.2 10.3 %copy-start.5 = (f32[192]{0:T(256)S(1)}, f32[192]{0:T(256)}, u32[]{:S(2)}) copy-start(f32[192]{0:T(256)} %param.11) | copy-start | bytes 2308
  52.2 6.1 %collective-permute-start.1 = (bf16[3,64,192]{2,1,0:T(8,128)(2,1)S(1)}, bf16[3,64,192]{2,1,0:T(8,128)(2,1)S(1)}, u32[]{:S(2)}, u32[]{:S(2)}) collective-permute-start(bf16[3,64,192]{2,1,0:T(8,128)(2,1)S(1)} %get-tuple-element.61), channel_id=1, source_target_pairs={{0,1},{1,2},{2,3},{4,5},{5,6},{6,7},{8,9},{9,10},{10,11},{12,13},{... | collective-permute-start | bytes 221192 | tf_op jit(solution)/shard_map/ppermute | solution.py:206
  55.6 6.8 %collective-permute-start.2 = (bf16[3,64,192]{2,1,0:T(8,128)(2,1)S(1)}, bf16[3,64,192]{2,1,0:T(8,128)(2,1)S(1)}, u32[]{:S(2)}, u32[]{:S(2)}) collective-permute-start(bf16[3,64,192]{2,1,0:T(8,128)(2,1)S(1)} %get-tuple-element.60), channel_id=1, source_target_pairs={{1,0},{2,1},{3,2},{5,4},{6,5},{7,6},{9,8},{10,9},{11,10},{13,12},{... | collective-permute-start | bytes 221192 | tf_op jit(solution)/shard_map/ppermute | solution.py:207
  62.4 0.7 copy-start.3
  70.3 4.0 %collective-permute-start.3 = (f32[32,40,128]{2,1,0:T(8,128)S(1)}, f32[32,40,128]{2,1,0:T(8,128)S(1)}, u32[]{:S(2)}, u32[]{:S(2)}) collective-permute-start(f32[32,40,128]{2,1,0:T(8,128)S(1)} %get-tuple-element.44), channel_id=1, source_target_pairs={{0,4},{4,0},{1,5},{5,1},{2,6},{6,2},{3,7},{7,3},{8,12},{12,8},{9,1... | collective-permute-start | bytes 1966088 | tf_op jit(solution)/shard_map/ppermute | solution.py:212
  94.3 16.3 %all-to-all-start.3 = ((f32[16,8,96]{2,1,0:T(8,128)}), f32[16,8,96]{2,1,0:T(8,128)S(1)}, u32[]{:S(2)}, u32[]{:S(2)}) async-start(f32[16,8,96]{2,1,0:T(8,128)} %middle.1), calls=%async_computation.3 | async-start | bytes 131072 | tf_op jit(solution)/shard_map/all_to_all | solution.py:216
  97.8 4.5 %collective-permute-start.4 = (bf16[3,64,192]{2,1,0:T(8,128)(2,1)S(1)}, bf16[3,64,192]{2,1,0:T(8,128)(2,1)S(1)}, u32[]{:S(2)}, u32[]{:S(2)}) collective-permute-start(bf16[3,64,192]{2,1,0:T(8,128)(2,1)S(1)} %get-tuple-element.59), channel_id=1, source_target_pairs={{0,1},{1,2},{2,3},{4,5},{5,6},{6,7},{8,9},{9,10},{10,11},{12,13},{... | collective-permute-start | bytes 221192 | tf_op jit(solution)/shard_map/ppermute | solution.py:206
  100.2 6.5 %collective-permute-start.5 = (bf16[3,64,192]{2,1,0:T(8,128)(2,1)S(1)}, bf16[3,64,192]{2,1,0:T(8,128)(2,1)S(1)}, u32[]{:S(2)}, u32[]{:S(2)}) collective-permute-start(bf16[3,64,192]{2,1,0:T(8,128)(2,1)S(1)} %get-tuple-element.58), channel_id=1, source_target_pairs={{1,0},{2,1},{3,2},{5,4},{6,5},{7,6},{9,8},{10,9},{11,10},{13,12},{... | collective-permute-start | bytes 221192 | tf_op jit(solution)/shard_map/ppermute | solution.py:207
  111.3 14.3 %all-to-all-start.4 = ((f32[32,8,96]{2,1,0:T(8,128)}), f32[32,8,96]{2,1,0:T(8,128)S(1)}, u32[]{:S(2)}, u32[]{:S(2)}) async-start(f32[32,8,96]{2,1,0:T(8,128)} %spread.1), calls=%async_computation.4 | async-start | bytes 262144 | tf_op jit(solution)/shard_map/all_to_all | solution.py:216

commit v3 on v2

--- a/solution.py
+++ b/solution.py
@@ -91,7 +91,7 @@
 
 def main_kernel(
     own, other, tokens, cotangent, padded, normed, inv_std, norm_halves, norm_t, up_halves, up_t,
-    gain, scale, mine, theirs, block_out, mixed_grad, smalls, grad_rows,
+    gain, scale, mine, theirs_bf, block_out, mixed_grad, smalls, grad_rows, theirs,
 ):
     branch = jnp.zeros((CELLS, WIDTH), F32)
     normed_grad = jnp.zeros((CELLS, WIDTH), F32)
@@ -154,6 +154,7 @@
                 at = 24 + SMALL_ROWS * k
                 out[piece, at : at + SMALL_ROWS, PART:128] = values[:, 32 * k : 32 * k + 32]
             out[piece, 36:40, PART:128] = jnp.zeros((4, 32), F32)
+    theirs_bf[...] = theirs[...].astype(BF16)
 
 
 def middle_kernel(arrived, column):
@@ -245,34 +246,34 @@
         "forward",
         pl.CostEstimate(flops=8_000_000, bytes_accessed=2_000_000, transcendentals=256),
     )(tokens, low, high, dw_kernel, gain, shift, scale, upstream)
+    own, norm_t = lax.optimization_barrier((own, norm_t))
     own = own.reshape(HALF, 2 * WIDTH)
     other = other_core(own)
     mine, theirs, block_out, mixed_grad = kernel_call(
         main_kernel,
         [
             ((PEERS, 40, 128), F32),
-            ((PEERS, 40, 128), F32),
+            ((PEERS, 40, 128), BF16),
             ((ROWS, COLS, WIDTH), BF16),
             ((ROWS, COLS, WIDTH), BF16),
         ],
-        [pltpu.VMEM((64, WIDTH), F32), pltpu.VMEM((ROWS, COLS, WIDTH), F32)],
+        [
+            pltpu.VMEM((64, WIDTH), F32),
+            pltpu.VMEM((ROWS, COLS, WIDTH), F32),
+            pltpu.VMEM((PEERS, 40, 128), F32),
+        ],
         "main",
         pl.CostEstimate(flops=500_000_000, bytes_accessed=4_000_000, transcendentals=400_000),
     )(
         own, other, tokens, upstream, padded, normed, inv_std, norm_halves, norm_t, up_halves,
         up_t, gain, scale,
     )
-    sums = (mine + other_core(theirs)).astype(BF16)
+    sums = (mine + other_core(theirs).astype(F32)).astype(BF16)
     sums, mixed_grad = lax.optimization_barrier((sums, mixed_grad))
     arrived = exchange(sums, ("y", "space"))
     grad_low, grad_high = neighbours(mixed_grad)
     (column,) = kernel_call(middle_kernel, [((DEPTH, 8, PART), F32)], name="middle")(arrived)
     column = exchange(column, "z")
-    column, mixed_grad, grad_low, grad_high = lax.optimization_barrier(
-        (column, mixed_grad, grad_low, grad_high)
-    )
-    (spread,) = kernel_call(spread_kernel, [((PEERS, 8, PART), F32)], name="spread")(column)
-    done = exchange(spread, ("y", "space"))
     (grad_tokens,) = kernel_call(
         backward_kernel,
         [((ROWS, COLS, WIDTH), BF16)],
@@ -280,6 +281,10 @@
         "backward",
         pl.CostEstimate(flops=8_000_000, bytes_accessed=1_000_000, transcendentals=0),
     )(mixed_grad, grad_low, grad_high, dw_kernel, upstream)
+    height = lax.axis_index("y").reshape(1)
+    column, grad_tokens, height = lax.optimization_barrier((column, grad_tokens, height))
+    (spread,) = kernel_call(spread_kernel, [((PEERS, 8, PART), F32)], name="spread")(column)
+    done = exchange(spread, ("y", "space"))
     kernel_grad, gain_grad, shift_grad, scale_grad, grad_expand, grad_reduce = pl.pallas_call(
         final_kernel,
         out_shape=[
@@ -292,7 +297,7 @@
         ],
         compiler_params=pltpu.CompilerParams(vmem_limit_bytes=40 * 2**20),
         name="final",
-    )(lax.axis_index("y").reshape(1), done)
+    )(height, done)
     return (
         block_out[None],
         grad_tokens[None],

time: 127 us -> 122 us (0.961)
  waiting for transfers between devices: 23.7 us -> 14.9 us
  starting transfers between devices: 20.5 us -> 23.6 us
    all_to_all x2, waiting for transfers between devices: 10.9 us -> 1.49 us  [exchange(): return lax.all_to_all(x, axes, 0, 0, tiled=True)]
    all_to_all x2, starting transfers between devices: 8.27 us -> 11.2 us  [exchange(): return lax.all_to_all(x, axes, 0, 0, tiled=True)]
where the time goes in v3:
time: 122 us; the launch traced here: 121 us
  blocking collectives  68.4 us (56%)
  starting transfers between devices  23.6 us (19%)
  waiting for transfers between devices  14.9 us (12%)
  Pallas kernels  11.2 us (9%)
  local copies, waits for them, and re-layouts  2.2 us (2%)
    all_to_all x3, blocking collectives, exchange(): return lax.all_to_all(x, axes, 0, 0, tiled=True)  68.4 us
    all_to_all x2, starting transfers between devices, exchange(): return lax.all_to_all(x, axes, 0, 0, tiled=True)  11.2 us
    ppermute x2, waiting for transfers between devices, neighbours(): high = lax.ppermute(block[:HALO], 'space', backward)  8.64 us
    ppermute x2, starting transfers between devices, neighbours(): low = lax.ppermute(block[ROWS - HALO:], 'space', forward)  5.85 us
    pallas_call x1, Pallas kernels, shards(): kernel_call(main_kernel, [((PEERS, 40, 128), F32), ((PEERS, 40, 128), BF1...  4.7 us
    ppermute x2, starting transfers between devices, other_core(): return lax.ppermute(x, 'core', [(0, 1), (1, 0)])  3.96 us
    ppermute x2, waiting for transfers between devices, other_core(): return lax.ppermute(x, 'core', [(0, 1), (1, 0)])  3.01 us
    ppermute x2, starting transfers between devices, neighbours(): high = lax.ppermute(block[:HALO], 'space', backward)  2.58 us
  transfers between devices with their start and end apart: 8, of which 7 were waited for; matrix products, arithmetic and copies ran while one was open for 0% of the time, Pallas kernels for 4%

profile of v3, /device:TPU:8, one launch (start us, length us, event | category | flops | bytes accessed | tf_op | source)
XLA Modules:
  0.0 121.3 jit_solution(1136254065470842611)
XLA Ops:
  0.6 0.0 copy-start.6
  0.6 0.7 broadcast_in_dim.34
  1.4 0.1 pad_maximum_fusion
  1.5 31.3 %all_to_all.25 = bf16[16,3,384]{2,1,0:T(4,128)(2,1)S(1)} all-to-all(bf16[16,3,384]{2,1,0:T(4,128)(2,1)S(1)} %pad_maximum_fusion), channel_id=1, replica_groups=mesh['z'=16,'y'=8,'core'=2,'space'=4] {'z'}, dimensions={0} | all-to-all | bytes 73728 | tf_op jit(solution)/shard_map/all_to_all | solution.py:217
  32.8 0.7 broadcast_in_dim.37
  33.6 7.7 %all-to-all-start.1 = ((bf16[8,48,384]{2,1,0:T(8,128)(2,1)}), bf16[8,48,384]{2,1,0:T(8,128)(2,1)S(1)}, u32[]{:S(2)}, u32[]{:S(2)}) async-start(bf16[8,48,384]{2,1,0:T(8,128)(2,1)} %broadcast_in_dim.37), calls=%async_computation.1 | async-start | bytes 589824 | tf_op jit(solution)/shard_map/all_to_all | solution.py:217
  41.2 0.0 copy-start.4
  41.3 0.0 copy-start.5
  41.3 3.5 %collective-permute-start = (bf16[3,64,192]{2,1,0:T(8,128)(2,1)S(1)}, bf16[3,64,192]{2,1,0:T(8,128)(2,1)S(1)}, u32[]{:S(2)}, u32[]{:S(2)}) collective-permute-start(bf16[3,64,192]{2,1,0:T(8,128)(2,1)S(1)} %get-tuple-element.63), channel_id=1, source_target_pairs={{0,1},{1,2},{2,3},{4,5},{5,6},{6,7},{8,9},{9,10},{10,11},{12,13},{... | collective-permute-start | bytes 221192 | tf_op jit(solution)/shard_map/ppermute | solution.py:207
  44.8 1.3 %collective-permute-start.1 = (bf16[3,64,192]{2,1,0:T(8,128)(2,1)S(1)}, bf16[3,64,192]{2,1,0:T(8,128)(2,1)S(1)}, u32[]{:S(2)}, u32[]{:S(2)}) collective-permute-start(bf16[3,64,192]{2,1,0:T(8,128)(2,1)S(1)} %get-tuple-element.62), channel_id=1, source_target_pairs={{1,0},{2,1},{3,2},{5,4},{6,5},{7,6},{9,8},{10,9},{11,10},{13,12},{... | collective-permute-start | bytes 221192 | tf_op jit(solution)/shard_map/ppermute | solution.py:208
  46.1 0.9 collective-permute-done.low
  47.0 4.3 %collective-permute-done.1.high = bf16[3,64,192]{2,1,0:T(8,128)(2,1)S(1)} collective-permute-done((bf16[3,64,192]{2,1,0:T(8,128)(2,1)S(1)}, bf16[3,64,192]{2,1,0:T(8,128)(2,1)S(1)}, u32[]{:S(2)}, u32[]{:S(2)}) %collective-permute-start.1) | collective-permute-done | bytes 73760 | tf_op jit(solution)/shard_map/ppermute | solution.py:208
  51.4 0.7 copy-done.3
  52.0 2.4 %forward.1 = (f32[10,80,192]{2,1,0:T(8,128)S(1)}, f32[256,192]{1,0:T(8,128)S(1)}, f32[256,1]{1,0:T(8,128)S(1)}, bf16[2,256,96]{2,1,0:T(8,128)(2,1)S(1)}, bf16[19...) custom-call(bf16[4,64,192]{2,1,0:T(8,128)(2,1)S(1)} %bitcast.13, ...), custom_call_target="tpu_custom_call" | custom-call | flops 8000000 | bytes 2000000 | tf_op jit(solution)/shard_map/forward/pallas_call | solution.py:234
  54.5 0.0 all-to-all-done.1
  54.5 1.9 %collective-permute-start.2 = (bf16[384,384]{1,0:T(8,128)(2,1)S(1)}, bf16[384,384]{1,0:T(8,128)(2,1)S(1)}, u32[]{:S(2)}, u32[]{:S(2)}) collective-permute-start(bf16[384,384]{1,0:T(8,128)(2,1)S(1)} %bitcast.18), channel_id=1, source_target_pairs={{0,4},{4,0},{1,5},{5,1},{2,6},{6,2},{3,7},{7,3},{8,12},{12,8},{9,1... | collective-permute-start | bytes 884744 | tf_op jit(solution)/shard_map/ppermute | solution.py:213
  56.4 1.5 %collective-permute-done.2.other = bf16[384,384]{1,0:T(8,128)(2,1)S(1)} collective-permute-done((bf16[384,384]{1,0:T(8,128)(2,1)S(1)}, bf16[384,384]{1,0:T(8,128)(2,1)S(1)}, u32[]{:S(2)}, u32[]{:S(2)}) %collective-permute-start.2) | collective-permute-done | bytes 294944 | tf_op jit(solution)/shard_map/ppermute | solution.py:213
  58.0 4.7 %main.1 = (f32[32,40,128]{2,1,0:T(8,128)S(1)}, bf16[32,40,128]{2,1,0:T(8,128)(2,1)S(1)}, bf16[4,64,192]{2,1,0:T(8,128)(2,1)}, bf16[4,64,192]{2,1,0:T(8,128)(2,1)S(1)}) custom-call(bf16[384,384]{1,0:T(8,128)(2,1)S(1)} %bitcast.19, bf16[384,384]{1,0:T(8,128)(2,1)S(1)} %collective-permute-done.2.other, bf16[4,64,192]{2,1,0:T(8,128)(2,1)S(1)} %bitcast.14, ...), custom_call_target="tpu_custom_call" | custom-call | flops 500000000 | bytes 4000000 | tf_op jit(solution)/shard_map/main/pallas_call | solution.py:252
  62.7 2.0 %collective-permute-start.3 = (bf16[32,40,128]{2,1,0:T(8,128)(2,1)S(1)}, bf16[32,40,128]{2,1,0:T(8,128)(2,1)S(1)}, u32[]{:S(2)}, u32[]{:S(2)}) collective-permute-start(bf16[32,40,128]{2,1,0:T(8,128)(2,1)S(1)} %get-tuple-element.47), channel_id=1, source_target_pairs={{0,4},{4,0},{1,5},{5,1},{2,6},{6,2},{3,7},{7,3},{8,12},{12,8},{9,1... | collective-permute-start | bytes 983048 | tf_op jit(solution)/shard_map/ppermute | solution.py:213
  64.7 1.5 %collective-permute-done.3 = bf16[32,40,128]{2,1,0:T(8,128)(2,1)S(1)} collective-permute-done((bf16[32,40,128]{2,1,0:T(8,128)(2,1)S(1)}, bf16[32,40,128]{2,1,0:T(8,128)(2,1)S(1)}, u32[]{:S(2)}, u32[]{:S(2)}) %collective-permute-start.3) | collective-permute-done | bytes 327712 | tf_op jit(solution)/shard_map/ppermute | solution.py:213
  66.2 0.1 add_convert_fusion
  66.3 23.0 %all_to_all.26.arrived = bf16[32,40,128]{2,1,0:T(8,128)(2,1)S(1)} all-to-all(bf16[32,40,128]{2,1,0:T(8,128)(2,1)S(1)} %add_convert_fusion), channel_id=1, replica_groups=mesh['z'=16,'y'=8,'core'=2,'space'=4] {'y','space'}, dimensions={0} | all-to-all | bytes 655360 | tf_op jit(solution)/shard_map/all_to_all | solution.py:217
  89.3 0.8 middle.1
  90.1 3.5 %all-to-all-start.3 = ((f32[16,8,96]{2,1,0:T(8,128)}), f32[16,8,96]{2,1,0:T(8,128)S(1)}, u32[]{:S(2)}, u32[]{:S(2)}) async-start(f32[16,8,96]{2,1,0:T(8,128)} %middle.1), calls=%async_computation.3 | async-start | bytes 131072 | tf_op jit(solution)/shard_map/all_to_all | solution.py:217
  93.6 2.3 %collective-permute-start.4 = (bf16[3,64,192]{2,1,0:T(8,128)(2,1)S(1)}, bf16[3,64,192]{2,1,0:T(8,128)(2,1)S(1)}, u32[]{:S(2)}, u32[]{:S(2)}) collective-permute-start(bf16[3,64,192]{2,1,0:T(8,128)(2,1)S(1)} %get-tuple-element.61), channel_id=1, source_target_pairs={{0,1},{1,2},{2,3},{4,5},{5,6},{6,7},{8,9},{9,10},{10,11},{12,13},{... | collective-permute-start | bytes 221192 | tf_op jit(solution)/shard_map/ppermute | solution.py:207
  95.9 1.3 %collective-permute-start.5 = (bf16[3,64,192]{2,1,0:T(8,128)(2,1)S(1)}, bf16[3,64,192]{2,1,0:T(8,128)(2,1)S(1)}, u32[]{:S(2)}, u32[]{:S(2)}) collective-permute-start(bf16[3,64,192]{2,1,0:T(8,128)(2,1)S(1)} %get-tuple-element.60), channel_id=1, source_target_pairs={{1,0},{2,1},{3,2},{5,4},{6,5},{7,6},{9,8},{10,9},{11,10},{13,12},{... | collective-permute-start | bytes 221192 | tf_op jit(solution)/shard_map/ppermute | solution.py:208
  97.2 0.9 collective-permute-done.4.low
  98.1 4.3 %collective-permute-done.5.high = bf16[3,64,192]{2,1,0:T(8,128)(2,1)S(1)} collective-permute-done((bf16[3,64,192]{2,1,0:T(8,128)(2,1)S(1)}, bf16[3,64,192]{2,1,0:T(8,128)(2,1)S(1)}, u32[]{:S(2)}, u32[]{:S(2)}) %collective-permute-start.5) | collective-permute-done | bytes 73760 | tf_op jit(solution)/shard_map/ppermute | solution.py:208
  102.4 2.5 %backward.1 = bf16[4,64,192]{2,1,0:T(8,128)(2,1)} custom-call(bf16[4,64,192]{2,1,0:T(8,128)(2,1)S(1)} %get-tuple-element.50.grad, bf16[3,64,192]{2,1,0:T(8,128)(2,1)S(1)} %collective-permute-done.4.low, bf16[3,64,192]{2,1,0:T(8,128)(2,1)S(1)} %collective-permute-done.5.high, f32[7,7,192]{2,1,0:T(8,128)S(1)} %copy-done.2, bf16[4,64,192]{2,1,0:T(8,128)(2,1)S(1)} %bitcast.17), custom_call_target="tpu_custom_call" | custom-call | flops 8000000 | bytes 1000000 | tf_op jit(solution)/shard_map/backward/pallas_call | solution.py:277
  104.9 1.5 %all-to-all-done.3.arrived = f32[16,8,96]{2,1,0:T(8,128)S(1)} async-done(((f32[16,8,96]{2,1,0:T(8,128)}), f32[16,8,96]{2,1,0:T(8,128)S(1)}, u32[]{:S(2)}, u32[]{:S(2)}) %all-to-all-start.3) | async-done | bytes 49184 | tf_op jit(solution)/shard_map/all_to_all | solution.py:217
  106.5 14.0 %all_to_all.27.done = f32[32,8,96]{2,1,0:T(8,128)S(1)} all-to-all(f32[32,8,96]{2,1,0:T(8,128)S(1)} %spread.1), channel_id=1, replica_groups=mesh['z'=16,'y'=8,'core'=2,'space'=4] {'y','space'}, dimensions={0} | all-to-all | bytes 196608 | tf_op jit(solution)/shard_map/all_to_all | solution.py:217
  120.5 0.8 final.1
  (15 shorter events, 0.1 us)
Async XLA Ops:
  0.6 0.7 copy-start.6
  33.6 7.7 %copy-start = (bf16[1,4,64,192]{3,2,1,0:T(8,128)(2,1)S(1)}, bf16[1,4,64,192]{3,2,1,0:T(8,128)(2,1)}, u32[]{:S(2)}) copy-start(bf16[1,4,64,192]{3,2,1,0:T(8,128)(2,1)} %param.8) | copy-start | bytes 294916
  33.6 20.9 %all-to-all-start.1 = ((bf16[8,48,384]{2,1,0:T(8,128)(2,1)}), bf16[8,48,384]{2,1,0:T(8,128)(2,1)S(1)}, u32[]{:S(2)}, u32[]{:S(2)}) async-start(bf16[8,48,384]{2,1,0:T(8,128)(2,1)} %broadcast_in_dim.37), calls=%async_computation.1 | async-start | bytes 589824 | tf_op jit(solution)/shard_map/all_to_all | solution.py:217
  41.2 10.1 %copy-start.1 = (bf16[1,4,64,192]{3,2,1,0:T(8,128)(2,1)S(1)}, bf16[1,4,64,192]{3,2,1,0:T(8,128)(2,1)}, u32[]{:S(2)}) copy-start(bf16[1,4,64,192]{3,2,1,0:T(8,128)(2,1)} %param.15) | copy-start | bytes 294916
  41.2 10.1 %copy-start.2 = (f32[7,7,192]{2,1,0:T(8,128)S(1)}, f32[7,7,192]{2,1,0:T(8,128)}, u32[]{:S(2)}) copy-start(f32[7,7,192]{2,1,0:T(8,128)} %taps.3) | copy-start | bytes 112900
  41.2 10.1 %copy-start.4 = (f32[192]{0:T(256)S(1)}, f32[192]{0:T(256)}, u32[]{:S(2)}) copy-start(f32[192]{0:T(256)} %param.14) | copy-start | bytes 2308
  41.3 10.1 %copy-start.5 = (f32[192]{0:T(256)S(1)}, f32[192]{0:T(256)}, u32[]{:S(2)}) copy-start(f32[192]{0:T(256)} %param.11) | copy-start | bytes 2308
  41.3 5.7 %collective-permute-start = (bf16[3,64,192]{2,1,0:T(8,128)(2,1)S(1)}, bf16[3,64,192]{2,1,0:T(8,128)(2,1)S(1)}, u32[]{:S(2)}, u32[]{:S(2)}) collective-permute-start(bf16[3,64,192]{2,1,0:T(8,128)(2,1)S(1)} %get-tuple-element.63), channel_id=1, source_target_pairs={{0,1},{1,2},{2,3},{4,5},{5,6},{6,7},{8,9},{9,10},{10,11},{12,13},{... | collective-permute-start | bytes 221192 | tf_op jit(solution)/shard_map/ppermute | solution.py:207
  44.8 6.5 %collective-permute-start.1 = (bf16[3,64,192]{2,1,0:T(8,128)(2,1)S(1)}, bf16[3,64,192]{2,1,0:T(8,128)(2,1)S(1)}, u32[]{:S(2)}, u32[]{:S(2)}) collective-permute-start(bf16[3,64,192]{2,1,0:T(8,128)(2,1)S(1)} %get-tuple-element.62), channel_id=1, source_target_pairs={{1,0},{2,1},{3,2},{5,4},{6,5},{7,6},{9,8},{10,9},{11,10},{13,12},{... | collective-permute-start | bytes 221192 | tf_op jit(solution)/shard_map/ppermute | solution.py:208
  51.3 0.7 copy-start.3
  54.5 3.5 %collective-permute-start.2 = (bf16[384,384]{1,0:T(8,128)(2,1)S(1)}, bf16[384,384]{1,0:T(8,128)(2,1)S(1)}, u32[]{:S(2)}, u32[]{:S(2)}) collective-permute-start(bf16[384,384]{1,0:T(8,128)(2,1)S(1)} %bitcast.18), channel_id=1, source_target_pairs={{0,4},{4,0},{1,5},{5,1},{2,6},{6,2},{3,7},{7,3},{8,12},{12,8},{9,1... | collective-permute-start | bytes 884744 | tf_op jit(solution)/shard_map/ppermute | solution.py:213
  62.7 3.5 %collective-permute-start.3 = (bf16[32,40,128]{2,1,0:T(8,128)(2,1)S(1)}, bf16[32,40,128]{2,1,0:T(8,128)(2,1)S(1)}, u32[]{:S(2)}, u32[]{:S(2)}) collective-permute-start(bf16[32,40,128]{2,1,0:T(8,128)(2,1)S(1)} %get-tuple-element.47), channel_id=1, source_target_pairs={{0,4},{4,0},{1,5},{5,1},{2,6},{6,2},{3,7},{7,3},{8,12},{12,8},{9,1... | collective-permute-start | bytes 983048 | tf_op jit(solution)/shard_map/ppermute | solution.py:213
  90.1 16.4 %all-to-all-start.3 = ((f32[16,8,96]{2,1,0:T(8,128)}), f32[16,8,96]{2,1,0:T(8,128)S(1)}, u32[]{:S(2)}, u32[]{:S(2)}) async-start(f32[16,8,96]{2,1,0:T(8,128)} %middle.1), calls=%async_computation.3 | async-start | bytes 131072 | tf_op jit(solution)/shard_map/all_to_all | solution.py:217
  93.6 4.5 %collective-permute-start.4 = (bf16[3,64,192]{2,1,0:T(8,128)(2,1)S(1)}, bf16[3,64,192]{2,1,0:T(8,128)(2,1)S(1)}, u32[]{:S(2)}, u32[]{:S(2)}) collective-permute-start(bf16[3,64,192]{2,1,0:T(8,128)(2,1)S(1)} %get-tuple-element.61), channel_id=1, source_target_pairs={{0,1},{1,2},{2,3},{4,5},{5,6},{6,7},{8,9},{9,10},{10,11},{12,13},{... | collective-permute-start | bytes 221192 | tf_op jit(solution)/shard_map/ppermute | solution.py:207
  95.9 6.5 %collective-permute-start.5 = (bf16[3,64,192]{2,1,0:T(8,128)(2,1)S(1)}, bf16[3,64,192]{2,1,0:T(8,128)(2,1)S(1)}, u32[]{:S(2)}, u32[]{:S(2)}) collective-permute-start(bf16[3,64,192]{2,1,0:T(8,128)(2,1)S(1)} %get-tuple-element.60), channel_id=1, source_target_pairs={{1,0},{2,1},{3,2},{5,4},{6,5},{7,6},{9,8},{10,9},{11,10},{13,12},{... | collective-permute-start | bytes 221192 | tf_op jit(solution)/shard_map/ppermute | solution.py:208

commit v4 on v3

--- a/solution.py
+++ b/solution.py
@@ -18,6 +18,8 @@
 MARGIN = 8
 F32, BF16 = jnp.float32, jnp.bfloat16
 SMALL_ROWS = 4
+PADDED = (ROWS + 2 * HALO, COLS + 2 * MARGIN, WIDTH)
+SHIFTED = (TAPS, ROWS, COLS + 2 * MARGIN, WIDTH)
 
 
 def kernel_call(body, outs, scratch=(), name=None, cost=None):
@@ -48,40 +50,47 @@
     padded[HALO + ROWS :, inside, :] = high[...].astype(F32)
 
 
-def convolve(padded, tap, finish):
-    chunk = 32
-    for start in range(0, COLS, chunk):
-        acc = [None] * ROWS
-        for i in range(ROWS + 2 * HALO):
+def convolve(padded, shifted, tap, finish):
+    for b in range(TAPS):
+        taps_b = [jnp.broadcast_to(tap(a, b), (8, WIDTH)) for a in range(TAPS)]
+        for t in range((MARGIN - HALO + b) // 8, (MARGIN - HALO + b + COLS + 7) // 8):
+            acc = [None] * ROWS
+            for i in range(ROWS + 2 * HALO):
+                field = padded[i, 8 * t : 8 * t + 8, :]
+                for r in range(ROWS):
+                    if 0 <= i - r < TAPS:
+                        term = field * taps_b[i - r]
+                        acc[r] = term if acc[r] is None else acc[r] + term
+            for r in range(ROWS):
+                shifted[b, r, 8 * t : 8 * t + 8, :] = acc[r]
+    for r in range(ROWS):
+        for start in range(0, COLS, 32):
+            total = None
             for b in range(TAPS):
                 first = MARGIN - HALO + b + start
-                shifted = padded[i, first : first + chunk, :]
-                for r in range(ROWS):
-                    if 0 <= i - r < TAPS:
-                        term = shifted * tap(i - r, b)
-                        acc[r] = term if acc[r] is None else acc[r] + term
-        for r in range(ROWS):
-            finish(r, start, chunk, acc[r])
+                value = shifted[b, r, first : first + 32, :]
+                total = value if total is None else total + value
+            finish(r, start, 32, total)
 
 
 def forward_kernel(
-    tokens, low, high, taps, gain, shift, scale, cotangent,
-    padded, normed, inv_std, norm_halves, norm_t, up_halves, up_t, mixed,
+    tokens, low, high, taps, vectors, cotangent,
+    padded, normed, inv_std, norm_halves, norm_t, up_halves, up_t, mixed, shifted,
 ):
     fill_padded(padded, low, tokens, high)
 
     def finish(r, start, chunk, value):
         mixed[r * COLS + start : r * COLS + start + chunk, :] = value
 
-    convolve(padded, lambda a, b: taps[a, b : b + 1, :], finish)
+    convolve(padded, shifted, lambda a, b: taps[a, b : b + 1, :], finish)
     value = mixed[...]
     centre = value - jnp.mean(value, -1, keepdims=True)
     inv = lax.rsqrt(jnp.mean(centre * centre, -1, keepdims=True) + 1e-06)
     norm = centre * inv
     normed[...] = norm
     inv_std[...] = inv
-    rounded = (norm * gain[...] + shift[...]).astype(BF16)
-    upstream = (cotangent[...].reshape(CELLS, WIDTH).astype(F32) * scale[...]).astype(BF16)
+    rounded = (norm * vectors[0:1] + vectors[1:2]).astype(BF16)
+    upstream = (cotangent[...].reshape(CELLS, WIDTH).astype(F32) * vectors[2:3]).astype(BF16)
     for h in range(2):
         norm_halves[h] = rounded[:, h * PART : (h + 1) * PART]
         up_halves[h] = upstream[:, h * PART : (h + 1) * PART]
@@ -91,7 +100,7 @@
 
 def main_kernel(
     own, other, tokens, cotangent, padded, normed, inv_std, norm_halves, norm_t, up_halves, up_t,
-    gain, scale, mine, theirs_bf, block_out, mixed_grad, smalls, grad_rows, theirs,
+    vectors, mine, theirs_bf, block_out, mixed_grad, smalls, grad_rows, theirs,
 ):
     branch = jnp.zeros((CELLS, WIDTH), F32)
     normed_grad = jnp.zeros((CELLS, WIDTH), F32)
@@ -116,32 +125,35 @@
         branch += dot_rows(hidden, reduce)
         normed_grad += dot_rows(pre_grad, expand)
     flat = tokens[...].reshape(CELLS, WIDTH).astype(F32)
-    block_out[...] = (flat + scale[...] * branch).astype(BF16).reshape(ROWS, COLS, WIDTH)
+    block_out[...] = (flat + vectors[2:3] * branch).astype(BF16).reshape(ROWS, COLS, WIDTH)
     norm = normed[...]
     upstream = cotangent[...].reshape(CELLS, WIDTH).astype(F32)
     smalls[TAPS * TAPS :, :] = jnp.zeros((64 - TAPS * TAPS, WIDTH), F32)
     smalls[49:50, :] = jnp.sum(normed_grad * norm, 0, keepdims=True)
     smalls[50:51, :] = jnp.sum(normed_grad, 0, keepdims=True)
     smalls[51:52, :] = jnp.sum(upstream * branch, 0, keepdims=True)
-    scaled = normed_grad * gain[...]
+    scaled = normed_grad * vectors[0:1]
     grad = inv_std[...] * (
         scaled
         - jnp.mean(scaled, -1, keepdims=True)
         - norm * jnp.mean(scaled * norm, -1, keepdims=True)
     )
-    grad_rows[...] = grad.reshape(ROWS, COLS, WIDTH)
+    grad_rows[:, :MARGIN, :] = jnp.zeros((ROWS, MARGIN, WIDTH), F32)
+    grad_rows[:, MARGIN + COLS :, :] = jnp.zeros((ROWS, MARGIN, WIDTH), F32)
+    grad_rows[:, MARGIN : MARGIN + COLS, :] = grad.reshape(ROWS, COLS, WIDTH)
     mixed_grad[...] = grad.astype(BF16).reshape(ROWS, COLS, WIDTH)
     for b in range(TAPS):
         acc = [None] * TAPS
-        for i in range(ROWS + 2 * HALO):
-            first = MARGIN - HALO + b
-            shifted = padded[i, first : first + COLS, :]
-            for r in range(ROWS):
-                a = i - r
-                if 0 <= a < TAPS:
-                    product = (shifted * grad_rows[r]).reshape(COLS // 8, 8, WIDTH)
-                    term = jnp.sum(product, 0)
-                    acc[a] = term if acc[a] is None else acc[a] + term
+        for t in range((MARGIN - HALO + b) // 8, (MARGIN - HALO + b + COLS + 7) // 8):
+            first = 8 * t + HALO - b
+            grads = [grad_rows[r, first : first + 8, :] for r in range(ROWS)]
+            for i in range(ROWS + 2 * HALO):
+                field = padded[i, 8 * t : 8 * t + 8, :]
+                for r in range(ROWS):
+                    a = i - r
+                    if 0 <= a < TAPS:
+                        term = field * grads[r]
+                        acc[a] = term if acc[a] is None else acc[a] + term
         for a in range(TAPS):
             row = a * TAPS + b
             smalls[row : row + 1, :] = jnp.sum(acc[a], 0, keepdims=True)
@@ -191,14 +203,17 @@
             (gain_grad, shift_grad, scale_grad)[row - TAPS * TAPS][...] = value
 
 
-def backward_kernel(grad, low, high, taps, cotangent, out, padded):
+def backward_kernel(grad, low, high, taps, cotangent, out, padded, shifted):
     fill_padded(padded, low, grad, high)
 
     def finish(r, start, chunk, value):
         upstream = cotangent[r, start : start + chunk, :].astype(F32)
         out[r, start : start + chunk, :] = (upstream + value).astype(BF16)
 
-    convolve(padded, lambda a, b: taps[TAPS - 1 - a, TAPS - 1 - b : TAPS - b, :], finish)
+    def tap(a, b):
+        return taps[TAPS - 1 - a, TAPS - 1 - b : TAPS - b, :]
+
+    convolve(padded, shifted, tap, finish)
 
 
 def neighbours(block):
@@ -221,20 +236,25 @@
     pressure_tokens, dw_kernel, norm_gain, norm_shift, w_expand, w_reduce, layer_scale, cotangent
 ):
     tokens, upstream = pressure_tokens[0], cotangent[0]
-    gain, shift, scale = norm_gain[None], norm_shift[None], layer_scale[None]
 
     def copies(x):
         return jnp.broadcast_to(x[None], (DEPTH,) + x.shape)
 
     column = exchange(jnp.concatenate([copies(w_expand), copies(w_reduce)], 2), "z")
-    column, tokens = lax.optimization_barrier((column, tokens))
+    column, tokens, *rows = lax.optimization_barrier(
+        (column, tokens, norm_gain, norm_shift, layer_scale)
+    )
     plane = column.reshape(1, BLOCK, 2 * WIDTH)
     own = exchange(jnp.broadcast_to(plane, (HEIGHT, BLOCK, 2 * WIDTH)), "y")
     low, high = neighbours(tokens)
+    own, low, high, vectors = lax.optimization_barrier(
+        (own.reshape(HALF, 2 * WIDTH), low, high, jnp.stack(rows))
+    )
+    other = other_core(own)
     padded, normed, inv_std, norm_halves, norm_t, up_halves, up_t = kernel_call(
         forward_kernel,
         [
-            ((ROWS + 2 * HALO, COLS + 2 * MARGIN, WIDTH), F32),
+            (PADDED, F32),
             ((CELLS, WIDTH), F32),
             ((CELLS, 1), F32),
             ((2, CELLS, PART), BF16),
@@ -242,13 +262,10 @@
             ((2, CELLS, PART), BF16),
             ((WIDTH, CELLS), BF16),
         ],
-        [pltpu.VMEM((CELLS, WIDTH), F32)],
+        [pltpu.VMEM((CELLS, WIDTH), F32), pltpu.VMEM(SHIFTED, F32)],
         "forward",
         pl.CostEstimate(flops=8_000_000, bytes_accessed=2_000_000, transcendentals=256),
-    )(tokens, low, high, dw_kernel, gain, shift, scale, upstream)
-    own, norm_t = lax.optimization_barrier((own, norm_t))
-    own = own.reshape(HALF, 2 * WIDTH)
-    other = other_core(own)
+    )(tokens, low, high, dw_kernel, vectors, upstream)
     mine, theirs, block_out, mixed_grad = kernel_call(
         main_kernel,
         [
@@ -259,14 +276,14 @@
         ],
         [
             pltpu.VMEM((64, WIDTH), F32),
-            pltpu.VMEM((ROWS, COLS, WIDTH), F32),
+            pltpu.VMEM((ROWS, COLS + 2 * MARGIN, WIDTH), F32),
             pltpu.VMEM((PEERS, 40, 128), F32),
         ],
         "main",
         pl.CostEstimate(flops=500_000_000, bytes_accessed=4_000_000, transcendentals=400_000),
     )(
         own, other, tokens, upstream, padded, normed, inv_std, norm_halves, norm_t, up_halves,
-        up_t, gain, scale,
+        up_t, vectors,
     )
     sums = (mine + other_core(theirs).astype(F32)).astype(BF16)
     sums, mixed_grad = lax.optimization_barrier((sums, mixed_grad))
@@ -277,7 +294,7 @@
     (grad_tokens,) = kernel_call(
         backward_kernel,
         [((ROWS, COLS, WIDTH), BF16)],
-        [pltpu.VMEM((ROWS + 2 * HALO, COLS + 2 * MARGIN, WIDTH), F32)],
+        [pltpu.VMEM(PADDED, F32), pltpu.VMEM(SHIFTED, F32)],
         "backward",
         pl.CostEstimate(flops=8_000_000, bytes_accessed=1_000_000, transcendentals=0),
     )(mixed_grad, grad_low, grad_high, dw_kernel, upstream)

time: 122 us -> 118 us (0.967)
  Pallas kernels: 11.2 us -> 8.31 us
  waiting for transfers between devices: 14.9 us -> 13.1 us
    ppermute x2, waiting for transfers between devices: 3.01 us -> 1.24 us  [other_core(): return lax.ppermute(x, 'core', [(0, 1), (1, 0)])]
    pallas_call x2, Pallas kernels: 4.96 us -> 3.49 us  [the longest x1 1.76 us: shards(): kernel_call(forward_kernel, [(PADDED, F32), ((CELLS, WIDTH), F32), ((CELL...]
    pallas_call x1, Pallas kernels: 4.7 us -> 3.28 us  [shards(): kernel_call(main_kernel, [((PEERS, 40, 128), F32), ((PEERS, 40, 128), BF1...]
  transfers between devices with their start and end apart: 8 -> 8, of which waited for: 7 -> 6; matrix products, arithmetic and copies ran while one was open for 0% -> 0% of each run, Pallas kernels for 4% -> 3%
where the time goes in v4:
time: 118 us; the launch traced here: 117 us
  blocking collectives  68.7 us (58%)
  starting transfers between devices  23.9 us (20%)
  waiting for transfers between devices  13.1 us (11%)
  Pallas kernels  8.31 us (7%)
  local copies, waits for them, and re-layouts  2.2 us (2%)
    all_to_all x3, blocking collectives, exchange(): return lax.all_to_all(x, axes, 0, 0, tiled=True)  68.7 us
    all_to_all x2, starting transfers between devices, exchange(): return lax.all_to_all(x, axes, 0, 0, tiled=True)  11.2 us
    ppermute x2, waiting for transfers between devices, neighbours(): high = lax.ppermute(block[:HALO], 'space', backward)  8.64 us
    ppermute x2, starting transfers between devices, neighbours(): low = lax.ppermute(block[ROWS - HALO:], 'space', forward)  5.85 us
    ppermute x2, starting transfers between devices, other_core(): return lax.ppermute(x, 'core', [(0, 1), (1, 0)])  4.32 us
    pallas_call x1, Pallas kernels, shards(): kernel_call(main_kernel, [((PEERS, 40, 128), F32), ((PEERS, 40, 128), BF1...  3.28 us
    ppermute x2, starting transfers between devices, neighbours(): high = lax.ppermute(block[:HALO], 'space', backward)  2.58 us
  transfers between devices with their start and end apart: 8, of which 6 were waited for; matrix products, arithmetic and copies ran while one was open for 0% of the time, Pallas kernels for 3%

profile of v4, /device:TPU:8, one launch (start us, length us, event | category | flops | bytes accessed | tf_op | source)
XLA Modules:
  0.0 117.3 jit_solution(14888012973919585293)
XLA Ops:
  0.6 0.7 broadcast_in_dim.12
  1.4 0.1 pad_maximum_fusion
  1.5 31.3 %all_to_all.25 = bf16[16,3,384]{2,1,0:T(4,128)(2,1)S(1)} all-to-all(bf16[16,3,384]{2,1,0:T(4,128)(2,1)S(1)} %pad_maximum_fusion), channel_id=1, replica_groups=mesh['z'=16,'y'=8,'core'=2,'space'=4] {'z'}, dimensions={0} | all-to-all | bytes 73728 | tf_op jit(solution)/shard_map/all_to_all | solution.py:232
  32.8 0.7 broadcast_in_dim.28
  33.6 7.7 %all-to-all-start.1 = ((bf16[8,48,384]{2,1,0:T(8,128)(2,1)}), bf16[8,48,384]{2,1,0:T(8,128)(2,1)S(1)}, u32[]{:S(2)}, u32[]{:S(2)}) async-start(bf16[8,48,384]{2,1,0:T(8,128)(2,1)} %broadcast_in_dim.28), calls=%async_computation.1 | async-start | bytes 589824 | tf_op jit(solution)/shard_map/all_to_all | solution.py:232
  41.2 0.0 copy-start.1
  41.3 0.0 copy-start.2
  41.3 3.5 %collective-permute-start = (bf16[3,64,192]{2,1,0:T(8,128)(2,1)S(1)}, bf16[3,64,192]{2,1,0:T(8,128)(2,1)S(1)}, u32[]{:S(2)}, u32[]{:S(2)}) collective-permute-start(bf16[3,64,192]{2,1,0:T(8,128)(2,1)S(1)} %get-tuple-element.73), channel_id=1, source_target_pairs={{0,1},{1,2},{2,3},{4,5},{5,6},{6,7},{8,9},{9,10},{10,11},{12,13},{... | collective-permute-start | bytes 221192 | tf_op jit(solution)/shard_map/ppermute | solution.py:222
  44.8 1.3 %collective-permute-start.1 = (bf16[3,64,192]{2,1,0:T(8,128)(2,1)S(1)}, bf16[3,64,192]{2,1,0:T(8,128)(2,1)S(1)}, u32[]{:S(2)}, u32[]{:S(2)}) collective-permute-start(bf16[3,64,192]{2,1,0:T(8,128)(2,1)S(1)} %get-tuple-element.72), channel_id=1, source_target_pairs={{1,0},{2,1},{3,2},{5,4},{6,5},{7,6},{9,8},{10,9},{11,10},{13,12},{... | collective-permute-start | bytes 221192 | tf_op jit(solution)/shard_map/ppermute | solution.py:223
  46.1 0.0 copy-start.4
  46.2 0.7 copy-done.4
  46.8 0.2 collective-permute-done.low
  47.0 4.3 %collective-permute-done.1.high = bf16[3,64,192]{2,1,0:T(8,128)(2,1)S(1)} collective-permute-done((bf16[3,64,192]{2,1,0:T(8,128)(2,1)S(1)}, bf16[3,64,192]{2,1,0:T(8,128)(2,1)S(1)}, u32[]{:S(2)}, u32[]{:S(2)}) %collective-permute-start.1) | collective-permute-done | bytes 73760 | tf_op jit(solution)/shard_map/ppermute | solution.py:223
  51.3 0.0 all-to-all-done.1
  51.4 1.9 %collective-permute-start.2 = (bf16[384,384]{1,0:T(8,128)(2,1)S(1)}, bf16[384,384]{1,0:T(8,128)(2,1)S(1)}, u32[]{:S(2)}, u32[]{:S(2)}) collective-permute-start(bf16[384,384]{1,0:T(8,128)(2,1)S(1)} %bitcast.15), channel_id=1, source_target_pairs={{0,4},{4,0},{1,5},{5,1},{2,6},{6,2},{3,7},{7,3},{8,12},{12,8},{9,1... | collective-permute-start | bytes 884744 | tf_op jit(solution)/shard_map/ppermute | solution.py:228
  53.3 1.8 %forward.1 = (f32[10,80,192]{2,1,0:T(8,128)S(1)}, f32[256,192]{1,0:T(8,128)S(1)}, f32[256,1]{1,0:T(8,128)S(1)}, bf16[2,256,96]{2,1,0:T(8,128)(2,1)S(1)}, bf16[19...) custom-call(bf16[4,64,192]{2,1,0:T(8,128)(2,1)S(1)} %bitcast.13, ...), custom_call_target="tpu_custom_call" | custom-call | flops 8000000 | bytes 2000000 | tf_op jit(solution)/shard_map/forward/pallas_call | solution.py:254
  55.1 0.0 collective-permute-done.2.other
  55.1 3.3 %main.1 = (f32[32,40,128]{2,1,0:T(8,128)S(1)}, bf16[32,40,128]{2,1,0:T(8,128)(2,1)S(1)}, bf16[4,64,192]{2,1,0:T(8,128)(2,1)}, bf16[4,64,192]{2,1,0:T(8,128)(2,1)S(1)}) custom-call(bf16[384,384]{1,0:T(8,128)(2,1)S(1)} %bitcast.16, bf16[384,384]{1,0:T(8,128)(2,1)S(1)} %collective-permute-done.2.other, bf16[4,64,192]{2,1,0:T(8,128)(2,1)S(1)} %bitcast.14, ...), custom_call_target="tpu_custom_call" | custom-call | flops 500000000 | bytes 4000000 | tf_op jit(solution)/shard_map/main/pallas_call | solution.py:269
  58.3 2.4 %collective-permute-start.3 = (bf16[32,40,128]{2,1,0:T(8,128)(2,1)S(1)}, bf16[32,40,128]{2,1,0:T(8,128)(2,1)S(1)}, u32[]{:S(2)}, u32[]{:S(2)}) collective-permute-start(bf16[32,40,128]{2,1,0:T(8,128)(2,1)S(1)} %get-tuple-element.57), channel_id=1, source_target_pairs={{0,4},{4,0},{1,5},{5,1},{2,6},{6,2},{3,7},{7,3},{8,12},{12,8},{9,1... | collective-permute-start | bytes 983048 | tf_op jit(solution)/shard_map/ppermute | solution.py:228
  60.8 1.2 %collective-permute-done.3 = bf16[32,40,128]{2,1,0:T(8,128)(2,1)S(1)} collective-permute-done((bf16[32,40,128]{2,1,0:T(8,128)(2,1)S(1)}, bf16[32,40,128]{2,1,0:T(8,128)(2,1)S(1)}, u32[]{:S(2)}, u32[]{:S(2)}) %collective-permute-start.3) | collective-permute-done | bytes 327712 | tf_op jit(solution)/shard_map/ppermute | solution.py:228
  62.0 0.1 add_convert_fusion
  62.1 23.3 %all_to_all.26.arrived = bf16[32,40,128]{2,1,0:T(8,128)(2,1)S(1)} all-to-all(bf16[32,40,128]{2,1,0:T(8,128)(2,1)S(1)} %add_convert_fusion), channel_id=1, replica_groups=mesh['z'=16,'y'=8,'core'=2,'space'=4] {'y','space'}, dimensions={0} | all-to-all | bytes 655360 | tf_op jit(solution)/shard_map/all_to_all | solution.py:232
  85.3 0.8 middle.1
  86.1 3.5 %all-to-all-start.3 = ((f32[16,8,96]{2,1,0:T(8,128)}), f32[16,8,96]{2,1,0:T(8,128)S(1)}, u32[]{:S(2)}, u32[]{:S(2)}) async-start(f32[16,8,96]{2,1,0:T(8,128)} %middle.1), calls=%async_computation.3 | async-start | bytes 131072 | tf_op jit(solution)/shard_map/all_to_all | solution.py:232
  89.6 2.3 %collective-permute-start.4 = (bf16[3,64,192]{2,1,0:T(8,128)(2,1)S(1)}, bf16[3,64,192]{2,1,0:T(8,128)(2,1)S(1)}, u32[]{:S(2)}, u32[]{:S(2)}) collective-permute-start(bf16[3,64,192]{2,1,0:T(8,128)(2,1)S(1)} %get-tuple-element.71), channel_id=1, source_target_pairs={{0,1},{1,2},{2,3},{4,5},{5,6},{6,7},{8,9},{9,10},{10,11},{12,13},{... | collective-permute-start | bytes 221192 | tf_op jit(solution)/shard_map/ppermute | solution.py:222
  91.9 1.3 %collective-permute-start.5 = (bf16[3,64,192]{2,1,0:T(8,128)(2,1)S(1)}, bf16[3,64,192]{2,1,0:T(8,128)(2,1)S(1)}, u32[]{:S(2)}, u32[]{:S(2)}) collective-permute-start(bf16[3,64,192]{2,1,0:T(8,128)(2,1)S(1)} %get-tuple-element.70), channel_id=1, source_target_pairs={{1,0},{2,1},{3,2},{5,4},{6,5},{7,6},{9,8},{10,9},{11,10},{13,12},{... | collective-permute-start | bytes 221192 | tf_op jit(solution)/shard_map/ppermute | solution.py:223
  93.2 0.9 collective-permute-done.4.low
  94.1 4.3 %collective-permute-done.5.high = bf16[3,64,192]{2,1,0:T(8,128)(2,1)S(1)} collective-permute-done((bf16[3,64,192]{2,1,0:T(8,128)(2,1)S(1)}, bf16[3,64,192]{2,1,0:T(8,128)(2,1)S(1)}, u32[]{:S(2)}, u32[]{:S(2)}) %collective-permute-start.5) | collective-permute-done | bytes 73760 | tf_op jit(solution)/shard_map/ppermute | solution.py:223
  98.5 1.7 %backward.1 = bf16[4,64,192]{2,1,0:T(8,128)(2,1)} custom-call(bf16[4,64,192]{2,1,0:T(8,128)(2,1)S(1)} %get-tuple-element.60.grad, bf16[3,64,192]{2,1,0:T(8,128)(2,1)S(1)} %collective-permute-done.4.low, bf16[3,64,192]{2,1,0:T(8,128)(2,1)S(1)} %collective-permute-done.5.high, f32[7,7,192]{2,1,0:T(8,128)S(1)} %copy-done.2, bf16[4,64,192]{2,1,0:T(8,128)(2,1)S(1)} %bitcast.19), custom_call_target="tpu_custom_call" | custom-call | flops 8000000 | bytes 1000000 | tf_op jit(solution)/shard_map/backward/pallas_call | solution.py:294
  100.2 2.2 %all-to-all-done.3.arrived = f32[16,8,96]{2,1,0:T(8,128)S(1)} async-done(((f32[16,8,96]{2,1,0:T(8,128)}), f32[16,8,96]{2,1,0:T(8,128)S(1)}, u32[]{:S(2)}, u32[]{:S(2)}) %all-to-all-start.3) | async-done | bytes 49184 | tf_op jit(solution)/shard_map/all_to_all | solution.py:232
  102.4 14.2 %all_to_all.27.done = f32[32,8,96]{2,1,0:T(8,128)S(1)} all-to-all(f32[32,8,96]{2,1,0:T(8,128)S(1)} %spread.1), channel_id=1, replica_groups=mesh['z'=16,'y'=8,'core'=2,'space'=4] {'y','space'}, dimensions={0} | all-to-all | bytes 196608 | tf_op jit(solution)/shard_map/all_to_all | solution.py:232
  116.6 0.8 final.1
  (16 shorter events, 0.1 us)
Async XLA Ops:
  0.6 0.7 copy-start.3
  33.6 7.7 %copy-start = (bf16[1,4,64,192]{3,2,1,0:T(8,128)(2,1)S(1)}, bf16[1,4,64,192]{3,2,1,0:T(8,128)(2,1)}, u32[]{:S(2)}) copy-start(bf16[1,4,64,192]{3,2,1,0:T(8,128)(2,1)} %param.8) | copy-start | bytes 294916
  33.6 17.8 %all-to-all-start.1 = ((bf16[8,48,384]{2,1,0:T(8,128)(2,1)}), bf16[8,48,384]{2,1,0:T(8,128)(2,1)S(1)}, u32[]{:S(2)}, u32[]{:S(2)}) async-start(bf16[8,48,384]{2,1,0:T(8,128)(2,1)} %broadcast_in_dim.28), calls=%async_computation.1 | async-start | bytes 589824 | tf_op jit(solution)/shard_map/all_to_all | solution.py:232
  41.2 4.9 %copy-start.5 = (f32[192]{0:T(256)S(1)}, f32[192]{0:T(256)}, u32[]{:S(2)}) copy-start(f32[192]{0:T(256)} %param.11) | copy-start | bytes 2308
  41.2 4.9 %copy-start.6 = (f32[192]{0:T(256)S(1)}, f32[192]{0:T(256)}, u32[]{:S(2)}) copy-start(f32[192]{0:T(256)} %param.10) | copy-start | bytes 2308
  41.2 12.0 %copy-start.1 = (bf16[1,4,64,192]{3,2,1,0:T(8,128)(2,1)S(1)}, bf16[1,4,64,192]{3,2,1,0:T(8,128)(2,1)}, u32[]{:S(2)}) copy-start(bf16[1,4,64,192]{3,2,1,0:T(8,128)(2,1)} %param.15) | copy-start | bytes 294916
  41.3 12.0 %copy-start.2 = (f32[7,7,192]{2,1,0:T(8,128)S(1)}, f32[7,7,192]{2,1,0:T(8,128)}, u32[]{:S(2)}) copy-start(f32[7,7,192]{2,1,0:T(8,128)} %taps.3) | copy-start | bytes 112900
  41.3 5.7 %collective-permute-start = (bf16[3,64,192]{2,1,0:T(8,128)(2,1)S(1)}, bf16[3,64,192]{2,1,0:T(8,128)(2,1)S(1)}, u32[]{:S(2)}, u32[]{:S(2)}) collective-permute-start(bf16[3,64,192]{2,1,0:T(8,128)(2,1)S(1)} %get-tuple-element.73), channel_id=1, source_target_pairs={{0,1},{1,2},{2,3},{4,5},{5,6},{6,7},{8,9},{9,10},{10,11},{12,13},{... | collective-permute-start | bytes 221192 | tf_op jit(solution)/shard_map/ppermute | solution.py:222
  44.8 6.5 %collective-permute-start.1 = (bf16[3,64,192]{2,1,0:T(8,128)(2,1)S(1)}, bf16[3,64,192]{2,1,0:T(8,128)(2,1)S(1)}, u32[]{:S(2)}, u32[]{:S(2)}) collective-permute-start(bf16[3,64,192]{2,1,0:T(8,128)(2,1)S(1)} %get-tuple-element.72), channel_id=1, source_target_pairs={{1,0},{2,1},{3,2},{5,4},{6,5},{7,6},{9,8},{10,9},{11,10},{13,12},{... | collective-permute-start | bytes 221192 | tf_op jit(solution)/shard_map/ppermute | solution.py:223
  46.1 0.7 copy-start.4
  51.4 3.7 %collective-permute-start.2 = (bf16[384,384]{1,0:T(8,128)(2,1)S(1)}, bf16[384,384]{1,0:T(8,128)(2,1)S(1)}, u32[]{:S(2)}, u32[]{:S(2)}) collective-permute-start(bf16[384,384]{1,0:T(8,128)(2,1)S(1)} %bitcast.15), channel_id=1, source_target_pairs={{0,4},{4,0},{1,5},{5,1},{2,6},{6,2},{3,7},{7,3},{8,12},{12,8},{9,1... | collective-permute-start | bytes 884744 | tf_op jit(solution)/shard_map/ppermute | solution.py:228
  58.3 3.7 %collective-permute-start.3 = (bf16[32,40,128]{2,1,0:T(8,128)(2,1)S(1)}, bf16[32,40,128]{2,1,0:T(8,128)(2,1)S(1)}, u32[]{:S(2)}, u32[]{:S(2)}) collective-permute-start(bf16[32,40,128]{2,1,0:T(8,128)(2,1)S(1)} %get-tuple-element.57), channel_id=1, source_target_pairs={{0,4},{4,0},{1,5},{5,1},{2,6},{6,2},{3,7},{7,3},{8,12},{12,8},{9,1... | collective-permute-start | bytes 983048 | tf_op jit(solution)/shard_map/ppermute | solution.py:228
  86.1 16.2 %all-to-all-start.3 = ((f32[16,8,96]{2,1,0:T(8,128)}), f32[16,8,96]{2,1,0:T(8,128)S(1)}, u32[]{:S(2)}, u32[]{:S(2)}) async-start(f32[16,8,96]{2,1,0:T(8,128)} %middle.1), calls=%async_computation.3 | async-start | bytes 131072 | tf_op jit(solution)/shard_map/all_to_all | solution.py:232
  89.6 4.5 %collective-permute-start.4 = (bf16[3,64,192]{2,1,0:T(8,128)(2,1)S(1)}, bf16[3,64,192]{2,1,0:T(8,128)(2,1)S(1)}, u32[]{:S(2)}, u32[]{:S(2)}) collective-permute-start(bf16[3,64,192]{2,1,0:T(8,128)(2,1)S(1)} %get-tuple-element.71), channel_id=1, source_target_pairs={{0,1},{1,2},{2,3},{4,5},{5,6},{6,7},{8,9},{9,10},{10,11},{12,13},{... | collective-permute-start | bytes 221192 | tf_op jit(solution)/shard_map/ppermute | solution.py:222
  91.9 6.5 %collective-permute-start.5 = (bf16[3,64,192]{2,1,0:T(8,128)(2,1)S(1)}, bf16[3,64,192]{2,1,0:T(8,128)(2,1)S(1)}, u32[]{:S(2)}, u32[]{:S(2)}) collective-permute-start(bf16[3,64,192]{2,1,0:T(8,128)(2,1)S(1)} %get-tuple-element.70), channel_id=1, source_target_pairs={{1,0},{2,1},{3,2},{5,4},{6,5},{7,6},{9,8},{10,9},{11,10},{13,12},{... | collective-permute-start | bytes 221192 | tf_op jit(solution)/shard_map/ppermute | solution.py:223

commit v5 on v4

--- a/solution.py
+++ b/solution.py
@@ -177,14 +177,14 @@
     grad = jnp.concatenate([total[:, :PART], tail], 0)
     at = [24 + SMALL_ROWS * k for k in range(3)]
     small = jnp.concatenate([total[i : i + SMALL_ROWS, PART:128] for i in at], 1)
+    blank = jnp.zeros((1, PART), F32)
     for z in range(DEPTH):
-        column[z, 0:UNITS, :] = grad[z * UNITS : (z + 1) * UNITS]
-        column[z, UNITS : UNITS + SMALL_ROWS, :] = small
-        column[z, UNITS + SMALL_ROWS :, :] = jnp.zeros((1, PART), F32)
+        rows = [grad[z * UNITS : (z + 1) * UNITS], small, blank]
+        column[z] = jnp.concatenate(rows, 0).astype(BF16)
 
 
 def spread_kernel(arrived, copies):
-    total = jnp.sum(arrived[...], 0)
+    total = jnp.sum(arrived[...].astype(F32), 0).astype(BF16)
     for p in range(PEERS):
         copies[p] = total
 
@@ -193,14 +193,17 @@
     y = height[0]
     for q in range(QUARTERS):
         out = expand if q < 2 else reduce
-        out[:, (q % 2) * PART : (q % 2 + 1) * PART] = done[y * QUARTERS + q, 0:UNITS, :]
-    for row in range(TAPS * TAPS + 3):
-        p, i = row // SMALL_ROWS, UNITS + row % SMALL_ROWS
-        value = jnp.concatenate([done[p, i : i + 1, :], done[16 + p, i : i + 1, :]], 1)
-        if row < TAPS * TAPS:
-            kernel_grad[row // TAPS, row % TAPS : row % TAPS + 1, :] = value
-        else:
-            (gain_grad, shift_grad, scale_grad)[row - TAPS * TAPS][...] = value
+        block = done[y * QUARTERS + q].astype(F32)
+        out[:, (q % 2) * PART : (q % 2 + 1) * PART] = block[0:UNITS]
+    for p in range((TAPS * TAPS + 3 + SMALL_ROWS - 1) // SMALL_ROWS):
+        block = jnp.concatenate([done[p].astype(F32), done[16 + p].astype(F32)], 1)
+        for i in range(SMALL_ROWS):
+            row = SMALL_ROWS * p + i
+            value = block[UNITS + i : UNITS + i + 1]
+            if row < TAPS * TAPS:
+                kernel_grad[row // TAPS, row % TAPS : row % TAPS + 1, :] = value
+            else:
+                (gain_grad, shift_grad, scale_grad)[row - TAPS * TAPS][...] = value
 
 
 def backward_kernel(grad, low, high, taps, cotangent, out, padded, shifted):
@@ -241,15 +244,12 @@
         return jnp.broadcast_to(x[None], (DEPTH,) + x.shape)
 
     column = exchange(jnp.concatenate([copies(w_expand), copies(w_reduce)], 2), "z")
-    column, tokens, *rows = lax.optimization_barrier(
-        (column, tokens, norm_gain, norm_shift, layer_scale)
-    )
+    low, high = neighbours(tokens)
+    vectors = jnp.stack([norm_gain, norm_shift, layer_scale])
+    column, low, high, vectors = lax.optimization_barrier((column, low, high, vectors))
     plane = column.reshape(1, BLOCK, 2 * WIDTH)
     own = exchange(jnp.broadcast_to(plane, (HEIGHT, BLOCK, 2 * WIDTH)), "y")
-    low, high = neighbours(tokens)
-    own, low, high, vectors = lax.optimization_barrier(
-        (own.reshape(HALF, 2 * WIDTH), low, high, jnp.stack(rows))
-    )
+    own, low = lax.optimization_barrier((own.reshape(HALF, 2 * WIDTH), low))
     other = other_core(own)
     padded, normed, inv_std, norm_halves, norm_t, up_halves, up_t = kernel_call(
         forward_kernel,
@@ -289,7 +289,7 @@
     sums, mixed_grad = lax.optimization_barrier((sums, mixed_grad))
     arrived = exchange(sums, ("y", "space"))
     grad_low, grad_high = neighbours(mixed_grad)
-    (column,) = kernel_call(middle_kernel, [((DEPTH, 8, PART), F32)], name="middle")(arrived)
+    (column,) = kernel_call(middle_kernel, [((DEPTH, 8, PART), BF16)], name="middle")(arrived)
     column = exchange(column, "z")
     (grad_tokens,) = kernel_call(
         backward_kernel,
@@ -300,7 +300,7 @@
     )(mixed_grad, grad_low, grad_high, dw_kernel, upstream)
     height = lax.axis_index("y").reshape(1)
     column, grad_tokens, height = lax.optimization_barrier((column, grad_tokens, height))
-    (spread,) = kernel_call(spread_kernel, [((PEERS, 8, PART), F32)], name="spread")(column)
+    (spread,) = kernel_call(spread_kernel, [((PEERS, 8, PART), BF16)], name="spread")(column)
     done = exchange(spread, ("y", "space"))
     kernel_grad, gain_grad, shift_grad, scale_grad, grad_expand, grad_reduce = pl.pallas_call(
         final_kernel,

time: 118 us -> 118 us (level)
  blocking collectives: 68.7 us -> 50.5 us
  starting transfers between devices: 23.9 us -> 40.2 us
  waiting for transfers between devices: 13.1 us -> 15.6 us
    all_to_all x3, blocking collectives: 68.7 us -> 50.5 us  [exchange(): return lax.all_to_all(x, axes, 0, 0, tiled=True)]
    all_to_all x2, starting transfers between devices: 11.2 us -> 27.6 us  [exchange(): return lax.all_to_all(x, axes, 0, 0, tiled=True)]
    all_to_all x2, waiting for transfers between devices: 2.16 us -> 4.69 us  [exchange(): return lax.all_to_all(x, axes, 0, 0, tiled=True)]
  transfers between devices with their start and end apart: 8 -> 8, of which waited for: 6 -> 7; matrix products, arithmetic and copies ran while one was open for 0% -> 0% of each run, Pallas kernels for 3% -> 3%
where the time goes in v5:
time: 118 us
  blocking collectives  50.5 us (43%)
  starting transfers between devices  40.2 us (34%)
  waiting for transfers between devices  15.6 us (13%)
  Pallas kernels  8.31 us (7%)
  local copies, waits for them, and re-layouts  1.5 us (1%)
    all_to_all x3, blocking collectives, exchange(): return lax.all_to_all(x, axes, 0, 0, tiled=True)  50.5 us
    all_to_all x2, starting transfers between devices, exchange(): return lax.all_to_all(x, axes, 0, 0, tiled=True)  27.6 us
    ppermute x2, waiting for transfers between devices, neighbours(): high = lax.ppermute(block[:HALO], 'space', backward)  8.64 us
    ppermute x2, starting transfers between devices, neighbours(): low = lax.ppermute(block[ROWS - HALO:], 'space', forward)  5.72 us
    all_to_all x2, waiting for transfers between devices, exchange(): return lax.all_to_all(x, axes, 0, 0, tiled=True)  4.69 us
    ppermute x2, starting transfers between devices, other_core(): return lax.ppermute(x, 'core', [(0, 1), (1, 0)])  4.3 us
    pallas_call x1, Pallas kernels, shards(): kernel_call(main_kernel, [((PEERS, 40, 128), F32), ((PEERS, 40, 128), BF1...  3.3 us
    ppermute x2, starting transfers between devices, neighbours(): high = lax.ppermute(block[:HALO], 'space', backward)  2.58 us
  transfers between devices with their start and end apart: 8, of which 7 were waited for; matrix products, arithmetic and copies ran while one was open for 0% of the time, Pallas kernels for 3%

profile of v5, /device:TPU:8, one launch (start us, length us, event | category | flops | bytes accessed | tf_op | source)
XLA Modules:
  0.0 117.8 jit_solution(11200158464694362061)
XLA Ops:
  0.6 0.7 broadcast_in_dim.12
  1.4 0.0 copy-start
  1.4 0.7 pad_maximum_fusion
  2.1 18.9 %all-to-all-start = ((bf16[16,3,384]{2,1,0:T(4,128)(2,1)}), bf16[16,3,384]{2,1,0:T(4,128)(2,1)S(1)}, u32[]{:S(2)}, u32[]{:S(2)}) async-start(bf16[16,3,384]{2,1,0:T(4,128)(2,1)} %pad_maximum_fusion), calls=%async_computation | async-start | bytes 98304 | tf_op jit(solution)/shard_map/all_to_all | solution.py:235
  21.0 0.0 copy-start.5
  21.0 0.0 copy-start.6
  21.0 3.4 %collective-permute-start = (bf16[3,64,192]{2,1,0:T(8,128)(2,1)S(1)}, bf16[3,64,192]{2,1,0:T(8,128)(2,1)S(1)}, u32[]{:S(2)}, u32[]{:S(2)}) collective-permute-start(bf16[3,64,192]{2,1,0:T(8,128)(2,1)S(1)} %get-tuple-element.67), channel_id=1, source_target_pairs={{0,1},{1,2},{2,3},{4,5},{5,6},{6,7},{8,9},{9,10},{10,11},{12,13},{... | collective-permute-start | bytes 221192 | tf_op jit(solution)/shard_map/ppermute | solution.py:225
  24.4 1.3 %collective-permute-start.1 = (bf16[3,64,192]{2,1,0:T(8,128)(2,1)S(1)}, bf16[3,64,192]{2,1,0:T(8,128)(2,1)S(1)}, u32[]{:S(2)}, u32[]{:S(2)}) collective-permute-start(bf16[3,64,192]{2,1,0:T(8,128)(2,1)S(1)} %get-tuple-element.66), channel_id=1, source_target_pairs={{1,0},{2,1},{3,2},{5,4},{6,5},{7,6},{9,8},{10,9},{11,10},{13,12},{... | collective-permute-start | bytes 221192 | tf_op jit(solution)/shard_map/ppermute | solution.py:226
  25.7 0.0 copy-start.4
  25.8 0.7 copy-done.4
  26.4 0.2 collective-permute-done.low
  26.6 4.3 %collective-permute-done.1.high = bf16[3,64,192]{2,1,0:T(8,128)(2,1)S(1)} collective-permute-done((bf16[3,64,192]{2,1,0:T(8,128)(2,1)S(1)}, bf16[3,64,192]{2,1,0:T(8,128)(2,1)S(1)}, u32[]{:S(2)}, u32[]{:S(2)}) %collective-permute-start.1) | collective-permute-done | bytes 73760 | tf_op jit(solution)/shard_map/ppermute | solution.py:226
  30.9 2.7 %all-to-all-done = bf16[16,3,384]{2,1,0:T(4,128)(2,1)S(1)} async-done(((bf16[16,3,384]{2,1,0:T(4,128)(2,1)}), bf16[16,3,384]{2,1,0:T(4,128)(2,1)S(1)}, u32[]{:S(2)}, u32[]{:S(2)}) %all-to-all-start) | async-done | bytes 36896 | tf_op jit(solution)/shard_map/all_to_all | solution.py:235
  33.7 0.0 copy-start.2
  33.7 17.2 %all_to_all.25 = bf16[8,48,384]{2,1,0:T(8,128)(2,1)S(1)} all-to-all(bf16[8,48,384]{2,1,0:T(8,128)(2,1)S(1)} %broadcast_in_dim.28), channel_id=1, replica_groups=mesh['z'=16,'y'=8,'core'=2,'space'=4] {'y'}, dimensions={0} | all-to-all | bytes 589824 | tf_op jit(solution)/shard_map/all_to_all | solution.py:235
  50.9 1.9 %collective-permute-start.2 = (bf16[384,384]{1,0:T(8,128)(2,1)S(1)}, bf16[384,384]{1,0:T(8,128)(2,1)S(1)}, u32[]{:S(2)}, u32[]{:S(2)}) collective-permute-start(bf16[384,384]{1,0:T(8,128)(2,1)S(1)} %bitcast.18), channel_id=1, source_target_pairs={{0,4},{4,0},{1,5},{5,1},{2,6},{6,2},{3,7},{7,3},{8,12},{12,8},{9,1... | collective-permute-start | bytes 884744 | tf_op jit(solution)/shard_map/ppermute | solution.py:231
  52.9 1.8 %forward.1 = (f32[10,80,192]{2,1,0:T(8,128)S(1)}, f32[256,192]{1,0:T(8,128)S(1)}, f32[256,1]{1,0:T(8,128)S(1)}, bf16[2,256,96]{2,1,0:T(8,128)(2,1)S(1)}, bf16[19...) custom-call(bf16[4,64,192]{2,1,0:T(8,128)(2,1)S(1)} %bitcast.16, ...), custom_call_target="tpu_custom_call" | custom-call | flops 8000000 | bytes 2000000 | tf_op jit(solution)/shard_map/forward/pallas_call | solution.py:254
  54.6 3.3 %main.1 = (f32[32,40,128]{2,1,0:T(8,128)S(1)}, bf16[32,40,128]{2,1,0:T(8,128)(2,1)S(1)}, bf16[4,64,192]{2,1,0:T(8,128)(2,1)}, bf16[4,64,192]{2,1,0:T(8,128)(2,1)S(1)}) custom-call(bf16[384,384]{1,0:T(8,128)(2,1)S(1)} %bitcast.19, bf16[384,384]{1,0:T(8,128)(2,1)S(1)} %collective-permute-done.2.other, bf16[4,64,192]{2,1,0:T(8,128)(2,1)S(1)} %bitcast.17, ...), custom_call_target="tpu_custom_call" | custom-call | flops 500000000 | bytes 4000000 | tf_op jit(solution)/shard_map/main/pallas_call | solution.py:269
  58.0 2.4 %collective-permute-start.3 = (bf16[32,40,128]{2,1,0:T(8,128)(2,1)S(1)}, bf16[32,40,128]{2,1,0:T(8,128)(2,1)S(1)}, u32[]{:S(2)}, u32[]{:S(2)}) collective-permute-start(bf16[32,40,128]{2,1,0:T(8,128)(2,1)S(1)} %get-tuple-element.51), channel_id=1, source_target_pairs={{0,4},{4,0},{1,5},{5,1},{2,6},{6,2},{3,7},{7,3},{8,12},{12,8},{9,1... | collective-permute-start | bytes 983048 | tf_op jit(solution)/shard_map/ppermute | solution.py:231
  60.4 1.2 %collective-permute-done.3 = bf16[32,40,128]{2,1,0:T(8,128)(2,1)S(1)} collective-permute-done((bf16[32,40,128]{2,1,0:T(8,128)(2,1)S(1)}, bf16[32,40,128]{2,1,0:T(8,128)(2,1)S(1)}, u32[]{:S(2)}, u32[]{:S(2)}) %collective-permute-start.3) | collective-permute-done | bytes 327712 | tf_op jit(solution)/shard_map/ppermute | solution.py:231
  61.6 0.1 add_convert_fusion
  61.7 19.7 %all_to_all.26.arrived = bf16[32,40,128]{2,1,0:T(8,128)(2,1)S(1)} all-to-all(bf16[32,40,128]{2,1,0:T(8,128)(2,1)S(1)} %add_convert_fusion), channel_id=1, replica_groups=mesh['z'=16,'y'=8,'core'=2,'space'=4] {'y','space'}, dimensions={0} | all-to-all | bytes 655360 | tf_op jit(solution)/shard_map/all_to_all | solution.py:235
  81.3 0.7 middle.1
  82.1 8.7 %all-to-all-start.3 = ((bf16[16,8,96]{2,1,0:T(8,128)(2,1)}), bf16[16,8,96]{2,1,0:T(8,128)(2,1)S(1)}, u32[]{:S(2)}, u32[]{:S(2)}) async-start(bf16[16,8,96]{2,1,0:T(8,128)(2,1)} %middle.1), calls=%async_computation.3 | async-start | bytes 65536 | tf_op jit(solution)/shard_map/all_to_all | solution.py:235
  90.8 2.3 %collective-permute-start.4 = (bf16[3,64,192]{2,1,0:T(8,128)(2,1)S(1)}, bf16[3,64,192]{2,1,0:T(8,128)(2,1)S(1)}, u32[]{:S(2)}, u32[]{:S(2)}) collective-permute-start(bf16[3,64,192]{2,1,0:T(8,128)(2,1)S(1)} %get-tuple-element.65), channel_id=1, source_target_pairs={{0,1},{1,2},{2,3},{4,5},{5,6},{6,7},{8,9},{9,10},{10,11},{12,13},{... | collective-permute-start | bytes 221192 | tf_op jit(solution)/shard_map/ppermute | solution.py:225
  93.1 1.3 %collective-permute-start.5 = (bf16[3,64,192]{2,1,0:T(8,128)(2,1)S(1)}, bf16[3,64,192]{2,1,0:T(8,128)(2,1)S(1)}, u32[]{:S(2)}, u32[]{:S(2)}) collective-permute-start(bf16[3,64,192]{2,1,0:T(8,128)(2,1)S(1)} %get-tuple-element.64), channel_id=1, source_target_pairs={{1,0},{2,1},{3,2},{5,4},{6,5},{7,6},{9,8},{10,9},{11,10},{13,12},{... | collective-permute-start | bytes 221192 | tf_op jit(solution)/shard_map/ppermute | solution.py:226
  94.4 0.9 collective-permute-done.4.low
  95.3 4.3 %collective-permute-done.5.high = bf16[3,64,192]{2,1,0:T(8,128)(2,1)S(1)} collective-permute-done((bf16[3,64,192]{2,1,0:T(8,128)(2,1)S(1)}, bf16[3,64,192]{2,1,0:T(8,128)(2,1)S(1)}, u32[]{:S(2)}, u32[]{:S(2)}) %collective-permute-start.5) | collective-permute-done | bytes 73760 | tf_op jit(solution)/shard_map/ppermute | solution.py:226
  99.6 1.7 %backward.1 = bf16[4,64,192]{2,1,0:T(8,128)(2,1)} custom-call(bf16[4,64,192]{2,1,0:T(8,128)(2,1)S(1)} %get-tuple-element.54.grad, bf16[3,64,192]{2,1,0:T(8,128)(2,1)S(1)} %collective-permute-done.4.low, bf16[3,64,192]{2,1,0:T(8,128)(2,1)S(1)} %collective-permute-done.5.high, f32[7,7,192]{2,1,0:T(8,128)S(1)} %copy-done.2, bf16[4,64,192]{2,1,0:T(8,128)(2,1)S(1)} %bitcast.22), custom_call_target="tpu_custom_call" | custom-call | flops 8000000 | bytes 1000000 | tf_op jit(solution)/shard_map/backward/pallas_call | solution.py:294
  101.4 2.0 %all-to-all-done.3.arrived = bf16[16,8,96]{2,1,0:T(8,128)(2,1)S(1)} async-done(((bf16[16,8,96]{2,1,0:T(8,128)(2,1)}), bf16[16,8,96]{2,1,0:T(8,128)(2,1)S(1)}, u32[]{:S(2)}, u32[]{:S(2)}) %all-to-all-start.3) | async-done | bytes 24608 | tf_op jit(solution)/shard_map/all_to_all | solution.py:235
  103.4 13.6 %all_to_all.27.done = bf16[32,8,96]{2,1,0:T(8,128)(2,1)S(1)} all-to-all(bf16[32,8,96]{2,1,0:T(8,128)(2,1)S(1)} %spread.1), channel_id=1, replica_groups=mesh['z'=16,'y'=8,'core'=2,'space'=4] {'y','space'}, dimensions={0} | all-to-all | bytes 98304 | tf_op jit(solution)/shard_map/all_to_all | solution.py:235
  117.1 0.7 final.1
  (16 shorter events, 0.2 us)
Async XLA Ops:
  0.6 0.7 copy-start.3
  1.4 19.6 %copy-start = (bf16[1,4,64,192]{3,2,1,0:T(8,128)(2,1)S(1)}, bf16[1,4,64,192]{3,2,1,0:T(8,128)(2,1)}, u32[]{:S(2)}) copy-start(bf16[1,4,64,192]{3,2,1,0:T(8,128)(2,1)} %param.8) | copy-start | bytes 294916
  2.1 31.5 %all-to-all-start = ((bf16[16,3,384]{2,1,0:T(4,128)(2,1)}), bf16[16,3,384]{2,1,0:T(4,128)(2,1)S(1)}, u32[]{:S(2)}, u32[]{:S(2)}) async-start(bf16[16,3,384]{2,1,0:T(4,128)(2,1)} %pad_maximum_fusion), calls=%async_computation | async-start | bytes 98304 | tf_op jit(solution)/shard_map/all_to_all | solution.py:235
  21.0 4.7 %copy-start.5 = (f32[192]{0:T(256)S(1)}, f32[192]{0:T(256)}, u32[]{:S(2)}) copy-start(f32[192]{0:T(256)} %param.11) | copy-start | bytes 2308
  21.0 4.7 %copy-start.6 = (f32[192]{0:T(256)S(1)}, f32[192]{0:T(256)}, u32[]{:S(2)}) copy-start(f32[192]{0:T(256)} %param.10) | copy-start | bytes 2308
  21.0 5.6 %collective-permute-start = (bf16[3,64,192]{2,1,0:T(8,128)(2,1)S(1)}, bf16[3,64,192]{2,1,0:T(8,128)(2,1)S(1)}, u32[]{:S(2)}, u32[]{:S(2)}) collective-permute-start(bf16[3,64,192]{2,1,0:T(8,128)(2,1)S(1)} %get-tuple-element.67), channel_id=1, source_target_pairs={{0,1},{1,2},{2,3},{4,5},{5,6},{6,7},{8,9},{9,10},{10,11},{12,13},{... | collective-permute-start | bytes 221192 | tf_op jit(solution)/shard_map/ppermute | solution.py:225
  24.4 6.5 %collective-permute-start.1 = (bf16[3,64,192]{2,1,0:T(8,128)(2,1)S(1)}, bf16[3,64,192]{2,1,0:T(8,128)(2,1)S(1)}, u32[]{:S(2)}, u32[]{:S(2)}) collective-permute-start(bf16[3,64,192]{2,1,0:T(8,128)(2,1)S(1)} %get-tuple-element.66), channel_id=1, source_target_pairs={{1,0},{2,1},{3,2},{5,4},{6,5},{7,6},{9,8},{10,9},{11,10},{13,12},{... | collective-permute-start | bytes 221192 | tf_op jit(solution)/shard_map/ppermute | solution.py:226
  25.7 0.7 copy-start.4
  33.7 19.2 %copy-start.1 = (bf16[1,4,64,192]{3,2,1,0:T(8,128)(2,1)S(1)}, bf16[1,4,64,192]{3,2,1,0:T(8,128)(2,1)}, u32[]{:S(2)}) copy-start(bf16[1,4,64,192]{3,2,1,0:T(8,128)(2,1)} %param.15) | copy-start | bytes 294916
  33.7 19.2 %copy-start.2 = (f32[7,7,192]{2,1,0:T(8,128)S(1)}, f32[7,7,192]{2,1,0:T(8,128)}, u32[]{:S(2)}) copy-start(f32[7,7,192]{2,1,0:T(8,128)} %taps.3) | copy-start | bytes 112900
  50.9 3.7 %collective-permute-start.2 = (bf16[384,384]{1,0:T(8,128)(2,1)S(1)}, bf16[384,384]{1,0:T(8,128)(2,1)S(1)}, u32[]{:S(2)}, u32[]{:S(2)}) collective-permute-start(bf16[384,384]{1,0:T(8,128)(2,1)S(1)} %bitcast.18), channel_id=1, source_target_pairs={{0,4},{4,0},{1,5},{5,1},{2,6},{6,2},{3,7},{7,3},{8,12},{12,8},{9,1... | collective-permute-start | bytes 884744 | tf_op jit(solution)/shard_map/ppermute | solution.py:231
  58.0 3.6 %collective-permute-start.3 = (bf16[32,40,128]{2,1,0:T(8,128)(2,1)S(1)}, bf16[32,40,128]{2,1,0:T(8,128)(2,1)S(1)}, u32[]{:S(2)}, u32[]{:S(2)}) collective-permute-start(bf16[32,40,128]{2,1,0:T(8,128)(2,1)S(1)} %get-tuple-element.51), channel_id=1, source_target_pairs={{0,4},{4,0},{1,5},{5,1},{2,6},{6,2},{3,7},{7,3},{8,12},{12,8},{9,1... | collective-permute-start | bytes 983048 | tf_op jit(solution)/shard_map/ppermute | solution.py:231
  82.1 21.3 %all-to-all-start.3 = ((bf16[16,8,96]{2,1,0:T(8,128)(2,1)}), bf16[16,8,96]{2,1,0:T(8,128)(2,1)S(1)}, u32[]{:S(2)}, u32[]{:S(2)}) async-start(bf16[16,8,96]{2,1,0:T(8,128)(2,1)} %middle.1), calls=%async_computation.3 | async-start | bytes 65536 | tf_op jit(solution)/shard_map/all_to_all | solution.py:235
  90.8 4.5 %collective-permute-start.4 = (bf16[3,64,192]{2,1,0:T(8,128)(2,1)S(1)}, bf16[3,64,192]{2,1,0:T(8,128)(2,1)S(1)}, u32[]{:S(2)}, u32[]{:S(2)}) collective-permute-start(bf16[3,64,192]{2,1,0:T(8,128)(2,1)S(1)} %get-tuple-element.65), channel_id=1, source_target_pairs={{0,1},{1,2},{2,3},{4,5},{5,6},{6,7},{8,9},{9,10},{10,11},{12,13},{... | collective-permute-start | bytes 221192 | tf_op jit(solution)/shard_map/ppermute | solution.py:225
  93.1 6.5 %collective-permute-start.5 = (bf16[3,64,192]{2,1,0:T(8,128)(2,1)S(1)}, bf16[3,64,192]{2,1,0:T(8,128)(2,1)S(1)}, u32[]{:S(2)}, u32[]{:S(2)}) collective-permute-start(bf16[3,64,192]{2,1,0:T(8,128)(2,1)S(1)} %get-tuple-element.64), channel_id=1, source_target_pairs={{1,0},{2,1},{3,2},{5,4},{6,5},{7,6},{9,8},{10,9},{11,10},{13,12},{... | collective-permute-start | bytes 221192 | tf_op jit(solution)/shard_map/ppermute | solution.py:226

commit v6 on v5

--- a/solution.py
+++ b/solution.py
@@ -18,6 +18,7 @@
 MARGIN = 8
 F32, BF16 = jnp.float32, jnp.bfloat16
 SMALL_ROWS = 4
+FIRST_Z, FIRST_Y, FIRST_X = 12, 4, 2
 PADDED = (ROWS + 2 * HALO, COLS + 2 * MARGIN, WIDTH)
 SHIFTED = (TAPS, ROWS, COLS + 2 * MARGIN, WIDTH)
 
@@ -231,8 +232,21 @@
     return lax.ppermute(x, "core", [(0, 1), (1, 0)])
 
 
+def turned(count, first):
+    return [(i + first) % count for i in range(count)]
+
+
+ORDERS = {
+    "z": turned(DEPTH, FIRST_Z),
+    "y": turned(HEIGHT, FIRST_Y),
+    ("y", "space"): [
+        y * QUARTERS + x for y in turned(HEIGHT, FIRST_Y) for x in turned(QUARTERS, FIRST_X)
+    ],
+}
+
+
 def exchange(x, axes):
-    return lax.all_to_all(x, axes, 0, 0, tiled=True)
+    return lax.all_to_all(x, axes, 0, 0, axis_index_groups=[ORDERS[axes]], tiled=True)
 
 
 def shards(
@@ -244,12 +258,15 @@
         return jnp.broadcast_to(x[None], (DEPTH,) + x.shape)
 
     column = exchange(jnp.concatenate([copies(w_expand), copies(w_reduce)], 2), "z")
-    low, high = neighbours(tokens)
-    vectors = jnp.stack([norm_gain, norm_shift, layer_scale])
-    column, low, high, vectors = lax.optimization_barrier((column, low, high, vectors))
+    column, tokens, *rows = lax.optimization_barrier(
+        (column, tokens, norm_gain, norm_shift, layer_scale)
+    )
     plane = column.reshape(1, BLOCK, 2 * WIDTH)
     own = exchange(jnp.broadcast_to(plane, (HEIGHT, BLOCK, 2 * WIDTH)), "y")
-    own, low = lax.optimization_barrier((own.reshape(HALF, 2 * WIDTH), low))
+    low, high = neighbours(tokens)
+    own, low, high, vectors = lax.optimization_barrier(
+        (own.reshape(HALF, 2 * WIDTH), low, high, jnp.stack(rows))
+    )
     other = other_core(own)
     padded, normed, inv_std, norm_halves, norm_t, up_halves, up_t = kernel_call(
         forward_kernel,
@@ -289,6 +306,7 @@
     sums, mixed_grad = lax.optimization_barrier((sums, mixed_grad))
     arrived = exchange(sums, ("y", "space"))
     grad_low, grad_high = neighbours(mixed_grad)
+    arrived, grad_low, grad_high = lax.optimization_barrier((arrived, grad_low, grad_high))
     (column,) = kernel_call(middle_kernel, [((DEPTH, 8, PART), BF16)], name="middle")(arrived)
     column = exchange(column, "z")
     (grad_tokens,) = kernel_call(
@@ -298,7 +316,7 @@
         "backward",
         pl.CostEstimate(flops=8_000_000, bytes_accessed=1_000_000, transcendentals=0),
     )(mixed_grad, grad_low, grad_high, dw_kernel, upstream)
-    height = lax.axis_index("y").reshape(1)
+    height = lax.rem(lax.axis_index("y") + (HEIGHT - FIRST_Y), HEIGHT).reshape(1)
     column, grad_tokens, height = lax.optimization_barrier((column, grad_tokens, height))
     (spread,) = kernel_call(spread_kernel, [((PEERS, 8, PART), BF16)], name="spread")(column)
     done = exchange(spread, ("y", "space"))

time: 118 us -> 111 us (0.941)
  the two profiles are of different devices: /device:TPU:8 before, /device:TPU:4 now
where the time goes in v6:
time: 111 us; the launch traced here: 110 us
  blocking collectives  42.1 us (38%)
  starting transfers between devices  41.1 us (37%)
  waiting for transfers between devices  14.8 us (13%)
  Pallas kernels  8.28 us (7%)
  local copies, waits for them, and re-layouts  2.2 us (2%)
    all_to_all x2, blocking collectives, exchange(): lax.all_to_all(x, axes, 0, 0, axis_index_groups=[ORDERS[axes]], tiled=True)  42.1 us
    all_to_all x3, starting transfers between devices, exchange(): lax.all_to_all(x, axes, 0, 0, axis_index_groups=[ORDERS[axes]], tiled=True)  25 us
    ppermute x2, starting transfers between devices, neighbours(): low = lax.ppermute(block[ROWS - HALO:], 'space', forward)  6.61 us
    all_to_all x3, waiting for transfers between devices, exchange(): lax.all_to_all(x, axes, 0, 0, axis_index_groups=[ORDERS[axes]], tiled=True)  6.36 us
    ppermute x2, starting transfers between devices, neighbours(): high = lax.ppermute(block[:HALO], 'space', backward)  5.21 us
    ppermute x2, waiting for transfers between devices, neighbours(): high = lax.ppermute(block[:HALO], 'space', backward)  4.46 us
    ppermute x2, starting transfers between devices, other_core(): return lax.ppermute(x, 'core', [(0, 1), (1, 0)])  4.32 us
    pallas_call x1, Pallas kernels, shards(): kernel_call(main_kernel, [((PEERS, 40, 128), F32), ((PEERS, 40, 128), BF1...  3.28 us
  transfers between devices with their start and end apart: 9, of which 6 were waited for; matrix products, arithmetic and copies ran while one was open for 0% of the time, Pallas kernels for 3%

profile of v6, /device:TPU:4, one launch (start us, length us, event | category | flops | bytes accessed | tf_op | source)
XLA Modules:
  0.0 110.3 jit_solution(5345866722771141782)
XLA Ops:
  0.6 0.7 broadcast_in_dim.12
  1.4 0.1 pad_maximum_fusion
  1.5 28.7 %all_to_all.25 = bf16[16,3,384]{2,1,0:T(4,128)(2,1)S(1)} all-to-all(bf16[16,3,384]{2,1,0:T(4,128)(2,1)S(1)} %pad_maximum_fusion), channel_id=1, replica_groups={{768,832,896,960,0,64,128,192,256,320,384,448,512,576,640,704},{769,833..., dimensions={0} | all-to-all | bytes 73728 | tf_op jit(solution)/shard_map/all_to_all | solution.py:249
  30.2 0.7 broadcast_in_dim.28
  31.0 9.3 %all-to-all-start.1 = ((bf16[8,48,384]{2,1,0:T(8,128)(2,1)}), bf16[8,48,384]{2,1,0:T(8,128)(2,1)S(1)}, u32[]{:S(2)}, u32[]{:S(2)}) async-start(bf16[8,48,384]{2,1,0:T(8,128)(2,1)} %broadcast_in_dim.28), calls=%async_computation.1 | async-start | bytes 589824 | tf_op jit(solution)/shard_map/all_to_all | solution.py:249
  40.3 0.0 copy-start.1
  40.3 0.0 copy-start.2
  40.3 3.2 %collective-permute-start = (bf16[3,64,192]{2,1,0:T(8,128)(2,1)S(1)}, bf16[3,64,192]{2,1,0:T(8,128)(2,1)S(1)}, u32[]{:S(2)}, u32[]{:S(2)}) collective-permute-start(bf16[3,64,192]{2,1,0:T(8,128)(2,1)S(1)} %get-tuple-element.79), channel_id=1, source_target_pairs={{0,1},{1,2},{2,3},{4,5},{5,6},{6,7},{8,9},{9,10},{10,11},{12,13},{... | collective-permute-start | bytes 221192 | tf_op jit(solution)/shard_map/ppermute | solution.py:226
  43.6 2.7 %collective-permute-start.1 = (bf16[3,64,192]{2,1,0:T(8,128)(2,1)S(1)}, bf16[3,64,192]{2,1,0:T(8,128)(2,1)S(1)}, u32[]{:S(2)}, u32[]{:S(2)}) collective-permute-start(bf16[3,64,192]{2,1,0:T(8,128)(2,1)S(1)} %get-tuple-element.78), channel_id=1, source_target_pairs={{1,0},{2,1},{3,2},{5,4},{6,5},{7,6},{9,8},{10,9},{11,10},{13,12},{... | collective-permute-start | bytes 221192 | tf_op jit(solution)/shard_map/ppermute | solution.py:227
  46.3 0.0 copy-start.4
  46.3 0.7 copy-done.4
  47.0 0.0 collective-permute-done.low
  47.0 3.1 %collective-permute-done.1.high = bf16[3,64,192]{2,1,0:T(8,128)(2,1)S(1)} collective-permute-done((bf16[3,64,192]{2,1,0:T(8,128)(2,1)S(1)}, bf16[3,64,192]{2,1,0:T(8,128)(2,1)S(1)}, u32[]{:S(2)}, u32[]{:S(2)}) %collective-permute-start.1) | collective-permute-done | bytes 73760 | tf_op jit(solution)/shard_map/ppermute | solution.py:227
  50.1 1.9 %collective-permute-start.2 = (bf16[384,384]{1,0:T(8,128)(2,1)S(1)}, bf16[384,384]{1,0:T(8,128)(2,1)S(1)}, u32[]{:S(2)}, u32[]{:S(2)}) collective-permute-start(bf16[384,384]{1,0:T(8,128)(2,1)S(1)} %bitcast.15), channel_id=1, source_target_pairs={{0,4},{4,0},{1,5},{5,1},{2,6},{6,2},{3,7},{7,3},{8,12},{12,8},{9,1... | collective-permute-start | bytes 884744 | tf_op jit(solution)/shard_map/ppermute | solution.py:232
  52.0 1.8 %forward.1 = (f32[10,80,192]{2,1,0:T(8,128)S(1)}, f32[256,192]{1,0:T(8,128)S(1)}, f32[256,1]{1,0:T(8,128)S(1)}, bf16[2,256,96]{2,1,0:T(8,128)(2,1)S(1)}, bf16[19...) custom-call(bf16[4,64,192]{2,1,0:T(8,128)(2,1)S(1)} %bitcast.13, ...), custom_call_target="tpu_custom_call" | custom-call | flops 8000000 | bytes 2000000 | tf_op jit(solution)/shard_map/forward/pallas_call | solution.py:271
  53.8 0.0 collective-permute-done.2.other
  53.8 3.3 %main.1 = (f32[32,40,128]{2,1,0:T(8,128)S(1)}, bf16[32,40,128]{2,1,0:T(8,128)(2,1)S(1)}, bf16[4,64,192]{2,1,0:T(8,128)(2,1)}, bf16[4,64,192]{2,1,0:T(8,128)(2,1)S(1)}) custom-call(bf16[384,384]{1,0:T(8,128)(2,1)S(1)} %bitcast.16, bf16[384,384]{1,0:T(8,128)(2,1)S(1)} %collective-permute-done.2.other, bf16[4,64,192]{2,1,0:T(8,128)(2,1)S(1)} %bitcast.14, ...), custom_call_target="tpu_custom_call" | custom-call | flops 500000000 | bytes 4000000 | tf_op jit(solution)/shard_map/main/pallas_call | solution.py:286
  57.1 2.4 %collective-permute-start.3 = (bf16[32,40,128]{2,1,0:T(8,128)(2,1)S(1)}, bf16[32,40,128]{2,1,0:T(8,128)(2,1)S(1)}, u32[]{:S(2)}, u32[]{:S(2)}) collective-permute-start(bf16[32,40,128]{2,1,0:T(8,128)(2,1)S(1)} %get-tuple-element.60), channel_id=1, source_target_pairs={{0,4},{4,0},{1,5},{5,1},{2,6},{6,2},{3,7},{7,3},{8,12},{12,8},{9,1... | collective-permute-start | bytes 983048 | tf_op jit(solution)/shard_map/ppermute | solution.py:232
  59.5 1.2 %collective-permute-done.3 = bf16[32,40,128]{2,1,0:T(8,128)(2,1)S(1)} collective-permute-done((bf16[32,40,128]{2,1,0:T(8,128)(2,1)S(1)}, bf16[32,40,128]{2,1,0:T(8,128)(2,1)S(1)}, u32[]{:S(2)}, u32[]{:S(2)}) %collective-permute-start.3) | collective-permute-done | bytes 327712 | tf_op jit(solution)/shard_map/ppermute | solution.py:232
  60.7 0.8 add_convert_fusion
  61.5 7.7 %all-to-all-start.2 = ((bf16[32,40,128]{2,1,0:T(8,128)(2,1)}), bf16[32,40,128]{2,1,0:T(8,128)(2,1)S(1)}, u32[]{:S(2)}, u32[]{:S(2)}) async-start(bf16[32,40,128]{2,1,0:T(8,128)(2,1)} %add_convert_fusion), calls=%async_computation.2 | async-start | bytes 655360 | tf_op jit(solution)/shard_map/all_to_all | solution.py:249
  69.2 3.4 %collective-permute-start.4 = (bf16[3,64,192]{2,1,0:T(8,128)(2,1)S(1)}, bf16[3,64,192]{2,1,0:T(8,128)(2,1)S(1)}, u32[]{:S(2)}, u32[]{:S(2)}) collective-permute-start(bf16[3,64,192]{2,1,0:T(8,128)(2,1)S(1)} %get-tuple-element.77), channel_id=1, source_target_pairs={{0,1},{1,2},{2,3},{4,5},{5,6},{6,7},{8,9},{9,10},{10,11},{12,13},{... | collective-permute-start | bytes 221192 | tf_op jit(solution)/shard_map/ppermute | solution.py:226
  72.6 2.5 %collective-permute-start.5 = (bf16[3,64,192]{2,1,0:T(8,128)(2,1)S(1)}, bf16[3,64,192]{2,1,0:T(8,128)(2,1)S(1)}, u32[]{:S(2)}, u32[]{:S(2)}) collective-permute-start(bf16[3,64,192]{2,1,0:T(8,128)(2,1)S(1)} %get-tuple-element.76), channel_id=1, source_target_pairs={{1,0},{2,1},{3,2},{5,4},{6,5},{7,6},{9,8},{10,9},{11,10},{13,12},{... | collective-permute-start | bytes 221192 | tf_op jit(solution)/shard_map/ppermute | solution.py:227
  75.0 2.8 %collective-permute-done.4.low = bf16[3,64,192]{2,1,0:T(8,128)(2,1)S(1)} collective-permute-done((bf16[3,64,192]{2,1,0:T(8,128)(2,1)S(1)}, bf16[3,64,192]{2,1,0:T(8,128)(2,1)S(1)}, u32[]{:S(2)}, u32[]{:S(2)}) %collective-permute-start.4) | collective-permute-done | bytes 73760 | tf_op jit(solution)/shard_map/ppermute | solution.py:226
  77.8 1.4 %collective-permute-done.5.high = bf16[3,64,192]{2,1,0:T(8,128)(2,1)S(1)} collective-permute-done((bf16[3,64,192]{2,1,0:T(8,128)(2,1)S(1)}, bf16[3,64,192]{2,1,0:T(8,128)(2,1)S(1)}, u32[]{:S(2)}, u32[]{:S(2)}) %collective-permute-start.5) | collective-permute-done | bytes 73760 | tf_op jit(solution)/shard_map/ppermute | solution.py:227
  79.2 0.3 all-to-all-done.2.arrived
  79.5 0.7 middle.1
  80.3 8.0 %all-to-all-start.3 = ((bf16[16,8,96]{2,1,0:T(8,128)(2,1)}), bf16[16,8,96]{2,1,0:T(8,128)(2,1)S(1)}, u32[]{:S(2)}, u32[]{:S(2)}) async-start(bf16[16,8,96]{2,1,0:T(8,128)(2,1)} %middle.1), calls=%async_computation.3 | async-start | bytes 65536 | tf_op jit(solution)/shard_map/all_to_all | solution.py:249
  88.3 1.7 %backward.1 = bf16[4,64,192]{2,1,0:T(8,128)(2,1)} custom-call(bf16[4,64,192]{2,1,0:T(8,128)(2,1)S(1)} %get-tuple-element.63.grad, bf16[3,64,192]{2,1,0:T(8,128)(2,1)S(1)} %collective-permute-done.4.low, bf16[3,64,192]{2,1,0:T(8,128)(2,1)S(1)} %collective-permute-done.5.high, f32[7,7,192]{2,1,0:T(8,128)S(1)} %copy-done.2, bf16[4,64,192]{2,1,0:T(8,128)(2,1)S(1)} %bitcast.19), custom_call_target="tpu_custom_call" | custom-call | flops 8000000 | bytes 1000000 | tf_op jit(solution)/shard_map/backward/pallas_call | solution.py:312
  90.0 6.1 %all-to-all-done.3.arrived = bf16[16,8,96]{2,1,0:T(8,128)(2,1)S(1)} async-done(((bf16[16,8,96]{2,1,0:T(8,128)(2,1)}), bf16[16,8,96]{2,1,0:T(8,128)(2,1)S(1)}, u32[]{:S(2)}, u32[]{:S(2)}) %all-to-all-start.3) | async-done | bytes 24608 | tf_op jit(solution)/shard_map/all_to_all | solution.py:249
  96.1 13.4 %all_to_all.26.done = bf16[32,8,96]{2,1,0:T(8,128)(2,1)S(1)} all-to-all(bf16[32,8,96]{2,1,0:T(8,128)(2,1)S(1)} %spread.1), channel_id=1, replica_groups={{34,35,32,33,42,43,40,41,50,51,48,49,58,59,56,57,2,3,0,1,10,11,8,9,18,1..., dimensions={0} | all-to-all | bytes 98304 | tf_op jit(solution)/shard_map/all_to_all | solution.py:249
  109.6 0.7 final.1
  (17 shorter events, 0.1 us)
Async XLA Ops:
  0.6 0.7 copy-start.3
  30.9 9.3 %copy-start = (bf16[1,4,64,192]{3,2,1,0:T(8,128)(2,1)S(1)}, bf16[1,4,64,192]{3,2,1,0:T(8,128)(2,1)}, u32[]{:S(2)}) copy-start(bf16[1,4,64,192]{3,2,1,0:T(8,128)(2,1)} %param.8) | copy-start | bytes 294916
  31.0 19.1 %all-to-all-start.1 = ((bf16[8,48,384]{2,1,0:T(8,128)(2,1)}), bf16[8,48,384]{2,1,0:T(8,128)(2,1)S(1)}, u32[]{:S(2)}, u32[]{:S(2)}) async-start(bf16[8,48,384]{2,1,0:T(8,128)(2,1)} %broadcast_in_dim.28), calls=%async_computation.1 | async-start | bytes 589824 | tf_op jit(solution)/shard_map/all_to_all | solution.py:249
  40.3 6.1 %copy-start.5 = (f32[192]{0:T(256)S(1)}, f32[192]{0:T(256)}, u32[]{:S(2)}) copy-start(f32[192]{0:T(256)} %param.11) | copy-start | bytes 2308
  40.3 6.1 %copy-start.6 = (f32[192]{0:T(256)S(1)}, f32[192]{0:T(256)}, u32[]{:S(2)}) copy-start(f32[192]{0:T(256)} %param.10) | copy-start | bytes 2308
  40.3 11.7 %copy-start.1 = (bf16[1,4,64,192]{3,2,1,0:T(8,128)(2,1)S(1)}, bf16[1,4,64,192]{3,2,1,0:T(8,128)(2,1)}, u32[]{:S(2)}) copy-start(bf16[1,4,64,192]{3,2,1,0:T(8,128)(2,1)} %param.15) | copy-start | bytes 294916
  40.3 11.7 %copy-start.2 = (f32[7,7,192]{2,1,0:T(8,128)S(1)}, f32[7,7,192]{2,1,0:T(8,128)}, u32[]{:S(2)}) copy-start(f32[7,7,192]{2,1,0:T(8,128)} %taps.3) | copy-start | bytes 112900
  40.3 6.7 %collective-permute-start = (bf16[3,64,192]{2,1,0:T(8,128)(2,1)S(1)}, bf16[3,64,192]{2,1,0:T(8,128)(2,1)S(1)}, u32[]{:S(2)}, u32[]{:S(2)}) collective-permute-start(bf16[3,64,192]{2,1,0:T(8,128)(2,1)S(1)} %get-tuple-element.79), channel_id=1, source_target_pairs={{0,1},{1,2},{2,3},{4,5},{5,6},{6,7},{8,9},{9,10},{10,11},{12,13},{... | collective-permute-start | bytes 221192 | tf_op jit(solution)/shard_map/ppermute | solution.py:226
  43.6 6.5 %collective-permute-start.1 = (bf16[3,64,192]{2,1,0:T(8,128)(2,1)S(1)}, bf16[3,64,192]{2,1,0:T(8,128)(2,1)S(1)}, u32[]{:S(2)}, u32[]{:S(2)}) collective-permute-start(bf16[3,64,192]{2,1,0:T(8,128)(2,1)S(1)} %get-tuple-element.78), channel_id=1, source_target_pairs={{1,0},{2,1},{3,2},{5,4},{6,5},{7,6},{9,8},{10,9},{11,10},{13,12},{... | collective-permute-start | bytes 221192 | tf_op jit(solution)/shard_map/ppermute | solution.py:227
  46.3 0.7 copy-start.4
  50.1 3.7 %collective-permute-start.2 = (bf16[384,384]{1,0:T(8,128)(2,1)S(1)}, bf16[384,384]{1,0:T(8,128)(2,1)S(1)}, u32[]{:S(2)}, u32[]{:S(2)}) collective-permute-start(bf16[384,384]{1,0:T(8,128)(2,1)S(1)} %bitcast.15), channel_id=1, source_target_pairs={{0,4},{4,0},{1,5},{5,1},{2,6},{6,2},{3,7},{7,3},{8,12},{12,8},{9,1... | collective-permute-start | bytes 884744 | tf_op jit(solution)/shard_map/ppermute | solution.py:232
  57.1 3.7 %collective-permute-start.3 = (bf16[32,40,128]{2,1,0:T(8,128)(2,1)S(1)}, bf16[32,40,128]{2,1,0:T(8,128)(2,1)S(1)}, u32[]{:S(2)}, u32[]{:S(2)}) collective-permute-start(bf16[32,40,128]{2,1,0:T(8,128)(2,1)S(1)} %get-tuple-element.60), channel_id=1, source_target_pairs={{0,4},{4,0},{1,5},{5,1},{2,6},{6,2},{3,7},{7,3},{8,12},{12,8},{9,1... | collective-permute-start | bytes 983048 | tf_op jit(solution)/shard_map/ppermute | solution.py:232
  61.5 18.0 %all-to-all-start.2 = ((bf16[32,40,128]{2,1,0:T(8,128)(2,1)}), bf16[32,40,128]{2,1,0:T(8,128)(2,1)S(1)}, u32[]{:S(2)}, u32[]{:S(2)}) async-start(bf16[32,40,128]{2,1,0:T(8,128)(2,1)} %add_convert_fusion), calls=%async_computation.2 | async-start | bytes 655360 | tf_op jit(solution)/shard_map/all_to_all | solution.py:249
  69.2 8.6 %collective-permute-start.4 = (bf16[3,64,192]{2,1,0:T(8,128)(2,1)S(1)}, bf16[3,64,192]{2,1,0:T(8,128)(2,1)S(1)}, u32[]{:S(2)}, u32[]{:S(2)}) collective-permute-start(bf16[3,64,192]{2,1,0:T(8,128)(2,1)S(1)} %get-tuple-element.77), channel_id=1, source_target_pairs={{0,1},{1,2},{2,3},{4,5},{5,6},{6,7},{8,9},{9,10},{10,11},{12,13},{... | collective-permute-start | bytes 221192 | tf_op jit(solution)/shard_map/ppermute | solution.py:226
  72.6 6.7 %collective-permute-start.5 = (bf16[3,64,192]{2,1,0:T(8,128)(2,1)S(1)}, bf16[3,64,192]{2,1,0:T(8,128)(2,1)S(1)}, u32[]{:S(2)}, u32[]{:S(2)}) collective-permute-start(bf16[3,64,192]{2,1,0:T(8,128)(2,1)S(1)} %get-tuple-element.76), channel_id=1, source_target_pairs={{1,0},{2,1},{3,2},{5,4},{6,5},{7,6},{9,8},{10,9},{11,10},{13,12},{... | collective-permute-start | bytes 221192 | tf_op jit(solution)/shard_map/ppermute | solution.py:227
  80.3 15.8 %all-to-all-start.3 = ((bf16[16,8,96]{2,1,0:T(8,128)(2,1)}), bf16[16,8,96]{2,1,0:T(8,128)(2,1)S(1)}, u32[]{:S(2)}, u32[]{:S(2)}) async-start(bf16[16,8,96]{2,1,0:T(8,128)(2,1)} %middle.1), calls=%async_computation.3 | async-start | bytes 65536 | tf_op jit(solution)/shard_map/all_to_all | solution.py:249

commit v7 on v6

--- a/solution.py
+++ b/solution.py
@@ -18,7 +18,7 @@
 MARGIN = 8
 F32, BF16 = jnp.float32, jnp.bfloat16
 SMALL_ROWS = 4
-FIRST_Z, FIRST_Y, FIRST_X = 12, 4, 2
+FIRST_Z, LAST_Z, FIRST_Y, FIRST_X = 14, 8, 4, 2
 PADDED = (ROWS + 2 * HALO, COLS + 2 * MARGIN, WIDTH)
 SHIFTED = (TAPS, ROWS, COLS + 2 * MARGIN, WIDTH)
 
@@ -181,7 +181,7 @@
     blank = jnp.zeros((1, PART), F32)
     for z in range(DEPTH):
         rows = [grad[z * UNITS : (z + 1) * UNITS], small, blank]
-        column[z] = jnp.concatenate(rows, 0).astype(BF16)
+        column[(z + FIRST_Z - LAST_Z) % DEPTH] = jnp.concatenate(rows, 0).astype(BF16)
 
 
 def spread_kernel(arrived, copies):
@@ -238,6 +238,7 @@
 
 ORDERS = {
     "z": turned(DEPTH, FIRST_Z),
+    "z_back": turned(DEPTH, LAST_Z),
     "y": turned(HEIGHT, FIRST_Y),
     ("y", "space"): [
         y * QUARTERS + x for y in turned(HEIGHT, FIRST_Y) for x in turned(QUARTERS, FIRST_X)
@@ -245,8 +246,9 @@
 }
 
 
-def exchange(x, axes):
-    return lax.all_to_all(x, axes, 0, 0, axis_index_groups=[ORDERS[axes]], tiled=True)
+def exchange(x, axes, order=None):
+    groups = [ORDERS[order or axes]]
+    return lax.all_to_all(x, axes, 0, 0, axis_index_groups=groups, tiled=True)
 
 
 def shards(
@@ -258,15 +260,12 @@
         return jnp.broadcast_to(x[None], (DEPTH,) + x.shape)
 
     column = exchange(jnp.concatenate([copies(w_expand), copies(w_reduce)], 2), "z")
-    column, tokens, *rows = lax.optimization_barrier(
-        (column, tokens, norm_gain, norm_shift, layer_scale)
-    )
+    low, high = neighbours(tokens)
+    vectors = jnp.stack([norm_gain, norm_shift, layer_scale])
+    column, low, high, vectors = lax.optimization_barrier((column, low, high, vectors))
     plane = column.reshape(1, BLOCK, 2 * WIDTH)
     own = exchange(jnp.broadcast_to(plane, (HEIGHT, BLOCK, 2 * WIDTH)), "y")
-    low, high = neighbours(tokens)
-    own, low, high, vectors = lax.optimization_barrier(
-        (own.reshape(HALF, 2 * WIDTH), low, high, jnp.stack(rows))
-    )
+    own, low = lax.optimization_barrier((own.reshape(HALF, 2 * WIDTH), low))
     other = other_core(own)
     padded, normed, inv_std, norm_halves, norm_t, up_halves, up_t = kernel_call(
         forward_kernel,
@@ -308,7 +307,7 @@
     grad_low, grad_high = neighbours(mixed_grad)
     arrived, grad_low, grad_high = lax.optimization_barrier((arrived, grad_low, grad_high))
     (column,) = kernel_call(middle_kernel, [((DEPTH, 8, PART), BF16)], name="middle")(arrived)
-    column = exchange(column, "z")
+    column = exchange(column, "z", "z_back")
     (grad_tokens,) = kernel_call(
         backward_kernel,
         [((ROWS, COLS, WIDTH), BF16)],

time: 111 us -> 108 us (0.973)
  starting transfers between devices: 41.1 us -> 56.6 us
  blocking collectives: 42.1 us -> 28.4 us
  waiting for transfers between devices: 14.8 us -> 10.4 us
    all_to_all x3, starting transfers between devices: 25 us -> 40.6 us  [exchange(): return lax.all_to_all(x, axes, 0, 0, axis_index_groups=groups, tiled=True)]
    all_to_all x2, blocking collectives: 42.1 us -> 28.4 us  [exchange(): return lax.all_to_all(x, axes, 0, 0, axis_index_groups=groups, tiled=True)]
    all_to_all x3, waiting for transfers between devices: 6.36 us -> 1.55 us  [exchange(): return lax.all_to_all(x, axes, 0, 0, axis_index_groups=groups, tiled=True)]
  transfers between devices with their start and end apart: 9 -> 9, of which waited for: 6 -> 7; matrix products, arithmetic and copies ran while one was open for 0% -> 0% of each run, Pallas kernels for 3% -> 3%
where the time goes in v7:
time: 108 us
  starting transfers between devices  56.6 us (52%)
  blocking collectives  28.4 us (26%)
  waiting for transfers between devices  10.4 us (10%)
  Pallas kernels  8.3 us (8%)
  local copies, waits for them, and re-layouts  1.5 us (1%)
  other arithmetic  1.5 us (1%)
    all_to_all x3, starting transfers between devices, exchange(): return lax.all_to_all(x, axes, 0, 0, axis_index_groups=groups, tiled=True)  40.6 us
    all_to_all x2, blocking collectives, exchange(): return lax.all_to_all(x, axes, 0, 0, axis_index_groups=groups, tiled=True)  28.4 us
    ppermute x2, starting transfers between devices, neighbours(): low = lax.ppermute(block[ROWS - HALO:], 'space', forward)  6.48 us
    ppermute x2, starting transfers between devices, neighbours(): high = lax.ppermute(block[:HALO], 'space', backward)  5.2 us
    ppermute x2, waiting for transfers between devices, neighbours(): high = lax.ppermute(block[:HALO], 'space', backward)  4.56 us
    ppermute x2, starting transfers between devices, other_core(): return lax.ppermute(x, 'core', [(0, 1), (1, 0)])  4.33 us
    pallas_call x1, Pallas kernels, shards(): kernel_call(main_kernel, [((PEERS, 40, 128), F32), ((PEERS, 40, 128), BF1...  3.29 us
    ppermute x2, waiting for transfers between devices, neighbours(): low = lax.ppermute(block[ROWS - HALO:], 'space', forward)  3.01 us
  transfers between devices with their start and end apart: 9, of which 7 were waited for; matrix products, arithmetic and copies ran while one was open for 0% of the time, Pallas kernels for 3%

profile of v7, /device:TPU:4, one launch (start us, length us, event | category | flops | bytes accessed | tf_op | source)
XLA Modules:
  0.0 107.6 jit_solution(1550643822154235524)
XLA Ops:
  0.6 0.7 broadcast_in_dim.12
  1.4 0.0 copy-start
  1.4 0.7 pad_maximum_fusion
  2.1 19.6 %all-to-all-start = ((bf16[16,3,384]{2,1,0:T(4,128)(2,1)}), bf16[16,3,384]{2,1,0:T(4,128)(2,1)S(1)}, u32[]{:S(2)}, u32[]{:S(2)}) async-start(bf16[16,3,384]{2,1,0:T(4,128)(2,1)} %pad_maximum_fusion), calls=%async_computation | async-start | bytes 98304 | tf_op jit(solution)/shard_map/all_to_all | solution.py:251
  21.7 0.0 copy-start.5
  21.8 3.1 %collective-permute-start = (bf16[3,64,192]{2,1,0:T(8,128)(2,1)S(1)}, bf16[3,64,192]{2,1,0:T(8,128)(2,1)S(1)}, u32[]{:S(2)}, u32[]{:S(2)}) collective-permute-start(bf16[3,64,192]{2,1,0:T(8,128)(2,1)S(1)} %get-tuple-element.73), channel_id=1, source_target_pairs={{0,1},{1,2},{2,3},{4,5},{5,6},{6,7},{8,9},{9,10},{10,11},{12,13},{... | collective-permute-start | bytes 221192 | tf_op jit(solution)/shard_map/ppermute | solution.py:226
  24.9 2.7 %collective-permute-start.1 = (bf16[3,64,192]{2,1,0:T(8,128)(2,1)S(1)}, bf16[3,64,192]{2,1,0:T(8,128)(2,1)S(1)}, u32[]{:S(2)}, u32[]{:S(2)}) collective-permute-start(bf16[3,64,192]{2,1,0:T(8,128)(2,1)S(1)} %get-tuple-element.72), channel_id=1, source_target_pairs={{1,0},{2,1},{3,2},{5,4},{6,5},{7,6},{9,8},{10,9},{11,10},{13,12},{... | collective-permute-start | bytes 221192 | tf_op jit(solution)/shard_map/ppermute | solution.py:227
  27.6 0.0 copy-start.4
  27.6 0.7 copy-done.4
  28.3 3.1 %collective-permute-done.1.high = bf16[3,64,192]{2,1,0:T(8,128)(2,1)S(1)} collective-permute-done((bf16[3,64,192]{2,1,0:T(8,128)(2,1)S(1)}, bf16[3,64,192]{2,1,0:T(8,128)(2,1)S(1)}, u32[]{:S(2)}, u32[]{:S(2)}) %collective-permute-start.1) | collective-permute-done | bytes 73760 | tf_op jit(solution)/shard_map/ppermute | solution.py:227
  31.4 0.1 all-to-all-done
  31.5 0.0 copy-start.1
  31.5 0.0 copy-start.2
  31.6 15.0 %all_to_all.25 = bf16[8,48,384]{2,1,0:T(8,128)(2,1)S(1)} all-to-all(bf16[8,48,384]{2,1,0:T(8,128)(2,1)S(1)} %broadcast_in_dim.28), channel_id=1, replica_groups={{32,40,48,56,0,8,16,24},{33,41,49,57,1,9,17,25},{34,42,50,58,2,10,18,26..., dimensions={0} | all-to-all | bytes 589824 | tf_op jit(solution)/shard_map/all_to_all | solution.py:251
  46.5 1.9 %collective-permute-start.2 = (bf16[384,384]{1,0:T(8,128)(2,1)S(1)}, bf16[384,384]{1,0:T(8,128)(2,1)S(1)}, u32[]{:S(2)}, u32[]{:S(2)}) collective-permute-start(bf16[384,384]{1,0:T(8,128)(2,1)S(1)} %bitcast.18), channel_id=1, source_target_pairs={{0,4},{4,0},{1,5},{5,1},{2,6},{6,2},{3,7},{7,3},{8,12},{12,8},{9,1... | collective-permute-start | bytes 884744 | tf_op jit(solution)/shard_map/ppermute | solution.py:232
  48.5 1.8 %forward.1 = (f32[10,80,192]{2,1,0:T(8,128)S(1)}, f32[256,192]{1,0:T(8,128)S(1)}, f32[256,1]{1,0:T(8,128)S(1)}, bf16[2,256,96]{2,1,0:T(8,128)(2,1)S(1)}, bf16[19...) custom-call(bf16[4,64,192]{2,1,0:T(8,128)(2,1)S(1)} %bitcast.16, ...), custom_call_target="tpu_custom_call" | custom-call | flops 8000000 | bytes 2000000 | tf_op jit(solution)/shard_map/forward/pallas_call | solution.py:270
  50.2 3.3 %main.1 = (f32[32,40,128]{2,1,0:T(8,128)S(1)}, bf16[32,40,128]{2,1,0:T(8,128)(2,1)S(1)}, bf16[4,64,192]{2,1,0:T(8,128)(2,1)}, bf16[4,64,192]{2,1,0:T(8,128)(2,1)S(1)}) custom-call(bf16[384,384]{1,0:T(8,128)(2,1)S(1)} %bitcast.19, bf16[384,384]{1,0:T(8,128)(2,1)S(1)} %collective-permute-done.2.other, bf16[4,64,192]{2,1,0:T(8,128)(2,1)S(1)} %bitcast.17, ...), custom_call_target="tpu_custom_call" | custom-call | flops 500000000 | bytes 4000000 | tf_op jit(solution)/shard_map/main/pallas_call | solution.py:285
  53.5 2.4 %collective-permute-start.3 = (bf16[32,40,128]{2,1,0:T(8,128)(2,1)S(1)}, bf16[32,40,128]{2,1,0:T(8,128)(2,1)S(1)}, u32[]{:S(2)}, u32[]{:S(2)}) collective-permute-start(bf16[32,40,128]{2,1,0:T(8,128)(2,1)S(1)} %get-tuple-element.54), channel_id=1, source_target_pairs={{0,4},{4,0},{1,5},{5,1},{2,6},{6,2},{3,7},{7,3},{8,12},{12,8},{9,1... | collective-permute-start | bytes 983048 | tf_op jit(solution)/shard_map/ppermute | solution.py:232
  56.0 1.2 %collective-permute-done.3 = bf16[32,40,128]{2,1,0:T(8,128)(2,1)S(1)} collective-permute-done((bf16[32,40,128]{2,1,0:T(8,128)(2,1)S(1)}, bf16[32,40,128]{2,1,0:T(8,128)(2,1)S(1)}, u32[]{:S(2)}, u32[]{:S(2)}) %collective-permute-start.3) | collective-permute-done | bytes 327712 | tf_op jit(solution)/shard_map/ppermute | solution.py:232
  57.2 0.8 add_convert_fusion
  58.0 9.0 %all-to-all-start.2 = ((bf16[32,40,128]{2,1,0:T(8,128)(2,1)}), bf16[32,40,128]{2,1,0:T(8,128)(2,1)S(1)}, u32[]{:S(2)}, u32[]{:S(2)}) async-start(bf16[32,40,128]{2,1,0:T(8,128)(2,1)} %add_convert_fusion), calls=%async_computation.2 | async-start | bytes 655360 | tf_op jit(solution)/shard_map/all_to_all | solution.py:251
  67.0 3.4 %collective-permute-start.4 = (bf16[3,64,192]{2,1,0:T(8,128)(2,1)S(1)}, bf16[3,64,192]{2,1,0:T(8,128)(2,1)S(1)}, u32[]{:S(2)}, u32[]{:S(2)}) collective-permute-start(bf16[3,64,192]{2,1,0:T(8,128)(2,1)S(1)} %get-tuple-element.71), channel_id=1, source_target_pairs={{0,1},{1,2},{2,3},{4,5},{5,6},{6,7},{8,9},{9,10},{10,11},{12,13},{... | collective-permute-start | bytes 221192 | tf_op jit(solution)/shard_map/ppermute | solution.py:226
  70.4 2.5 %collective-permute-start.5 = (bf16[3,64,192]{2,1,0:T(8,128)(2,1)S(1)}, bf16[3,64,192]{2,1,0:T(8,128)(2,1)S(1)}, u32[]{:S(2)}, u32[]{:S(2)}) collective-permute-start(bf16[3,64,192]{2,1,0:T(8,128)(2,1)S(1)} %get-tuple-element.70), channel_id=1, source_target_pairs={{1,0},{2,1},{3,2},{5,4},{6,5},{7,6},{9,8},{10,9},{11,10},{13,12},{... | collective-permute-start | bytes 221192 | tf_op jit(solution)/shard_map/ppermute | solution.py:227
  72.9 3.0 %collective-permute-done.4.low = bf16[3,64,192]{2,1,0:T(8,128)(2,1)S(1)} collective-permute-done((bf16[3,64,192]{2,1,0:T(8,128)(2,1)S(1)}, bf16[3,64,192]{2,1,0:T(8,128)(2,1)S(1)}, u32[]{:S(2)}, u32[]{:S(2)}) %collective-permute-start.4) | collective-permute-done | bytes 73760 | tf_op jit(solution)/shard_map/ppermute | solution.py:226
  75.9 1.5 %collective-permute-done.5.high = bf16[3,64,192]{2,1,0:T(8,128)(2,1)S(1)} collective-permute-done((bf16[3,64,192]{2,1,0:T(8,128)(2,1)S(1)}, bf16[3,64,192]{2,1,0:T(8,128)(2,1)S(1)}, u32[]{:S(2)}, u32[]{:S(2)}) %collective-permute-start.5) | collective-permute-done | bytes 73760 | tf_op jit(solution)/shard_map/ppermute | solution.py:227
  77.4 0.2 all-to-all-done.2.arrived
  77.6 0.7 middle.1
  78.3 12.0 %all-to-all-start.3 = ((bf16[16,8,96]{2,1,0:T(8,128)(2,1)}), bf16[16,8,96]{2,1,0:T(8,128)(2,1)S(1)}, u32[]{:S(2)}, u32[]{:S(2)}) async-start(bf16[16,8,96]{2,1,0:T(8,128)(2,1)} %middle.1), calls=%async_computation.3 | async-start | bytes 65536 | tf_op jit(solution)/shard_map/all_to_all | solution.py:251
  90.4 1.7 %backward.1 = bf16[4,64,192]{2,1,0:T(8,128)(2,1)} custom-call(bf16[4,64,192]{2,1,0:T(8,128)(2,1)S(1)} %get-tuple-element.57.grad, bf16[3,64,192]{2,1,0:T(8,128)(2,1)S(1)} %collective-permute-done.4.low, bf16[3,64,192]{2,1,0:T(8,128)(2,1)S(1)} %collective-permute-done.5.high, f32[7,7,192]{2,1,0:T(8,128)S(1)} %copy-done.2, bf16[4,64,192]{2,1,0:T(8,128)(2,1)S(1)} %bitcast.22), custom_call_target="tpu_custom_call" | custom-call | flops 8000000 | bytes 1000000 | tf_op jit(solution)/shard_map/backward/pallas_call | solution.py:311
  92.1 1.3 %all-to-all-done.3.arrived = bf16[16,8,96]{2,1,0:T(8,128)(2,1)S(1)} async-done(((bf16[16,8,96]{2,1,0:T(8,128)(2,1)}), bf16[16,8,96]{2,1,0:T(8,128)(2,1)S(1)}, u32[]{:S(2)}, u32[]{:S(2)}) %all-to-all-start.3) | async-done | bytes 24608 | tf_op jit(solution)/shard_map/all_to_all | solution.py:251
  93.4 13.5 %all_to_all.26.done = bf16[32,8,96]{2,1,0:T(8,128)(2,1)S(1)} all-to-all(bf16[32,8,96]{2,1,0:T(8,128)(2,1)S(1)} %spread.1), channel_id=1, replica_groups={{34,35,32,33,42,43,40,41,50,51,48,49,58,59,56,57,2,3,0,1,10,11,8,9,18,1..., dimensions={0} | all-to-all | bytes 98304 | tf_op jit(solution)/shard_map/all_to_all | solution.py:251
  106.9 0.7 final.1
  (17 shorter events, 0.2 us)
Async XLA Ops:
  0.6 0.7 copy-start.3
  1.4 20.3 %copy-start = (bf16[1,4,64,192]{3,2,1,0:T(8,128)(2,1)S(1)}, bf16[1,4,64,192]{3,2,1,0:T(8,128)(2,1)}, u32[]{:S(2)}) copy-start(bf16[1,4,64,192]{3,2,1,0:T(8,128)(2,1)} %param.8) | copy-start | bytes 294916
  2.1 29.4 %all-to-all-start = ((bf16[16,3,384]{2,1,0:T(4,128)(2,1)}), bf16[16,3,384]{2,1,0:T(4,128)(2,1)S(1)}, u32[]{:S(2)}, u32[]{:S(2)}) async-start(bf16[16,3,384]{2,1,0:T(4,128)(2,1)} %pad_maximum_fusion), calls=%async_computation | async-start | bytes 98304 | tf_op jit(solution)/shard_map/all_to_all | solution.py:251
  21.7 5.9 %copy-start.5 = (f32[192]{0:T(256)S(1)}, f32[192]{0:T(256)}, u32[]{:S(2)}) copy-start(f32[192]{0:T(256)} %param.11) | copy-start | bytes 2308
  21.7 5.9 %copy-start.6 = (f32[192]{0:T(256)S(1)}, f32[192]{0:T(256)}, u32[]{:S(2)}) copy-start(f32[192]{0:T(256)} %param.10) | copy-start | bytes 2308
  21.8 6.6 %collective-permute-start = (bf16[3,64,192]{2,1,0:T(8,128)(2,1)S(1)}, bf16[3,64,192]{2,1,0:T(8,128)(2,1)S(1)}, u32[]{:S(2)}, u32[]{:S(2)}) collective-permute-start(bf16[3,64,192]{2,1,0:T(8,128)(2,1)S(1)} %get-tuple-element.73), channel_id=1, source_target_pairs={{0,1},{1,2},{2,3},{4,5},{5,6},{6,7},{8,9},{9,10},{10,11},{12,13},{... | collective-permute-start | bytes 221192 | tf_op jit(solution)/shard_map/ppermute | solution.py:226
  24.9 6.5 %collective-permute-start.1 = (bf16[3,64,192]{2,1,0:T(8,128)(2,1)S(1)}, bf16[3,64,192]{2,1,0:T(8,128)(2,1)S(1)}, u32[]{:S(2)}, u32[]{:S(2)}) collective-permute-start(bf16[3,64,192]{2,1,0:T(8,128)(2,1)S(1)} %get-tuple-element.72), channel_id=1, source_target_pairs={{1,0},{2,1},{3,2},{5,4},{6,5},{7,6},{9,8},{10,9},{11,10},{13,12},{... | collective-permute-start | bytes 221192 | tf_op jit(solution)/shard_map/ppermute | solution.py:227
  27.6 0.7 copy-start.4
  31.5 16.9 %copy-start.1 = (bf16[1,4,64,192]{3,2,1,0:T(8,128)(2,1)S(1)}, bf16[1,4,64,192]{3,2,1,0:T(8,128)(2,1)}, u32[]{:S(2)}) copy-start(bf16[1,4,64,192]{3,2,1,0:T(8,128)(2,1)} %param.15) | copy-start | bytes 294916
  31.5 16.9 %copy-start.2 = (f32[7,7,192]{2,1,0:T(8,128)S(1)}, f32[7,7,192]{2,1,0:T(8,128)}, u32[]{:S(2)}) copy-start(f32[7,7,192]{2,1,0:T(8,128)} %taps.3) | copy-start | bytes 112900
  46.5 3.7 %collective-permute-start.2 = (bf16[384,384]{1,0:T(8,128)(2,1)S(1)}, bf16[384,384]{1,0:T(8,128)(2,1)S(1)}, u32[]{:S(2)}, u32[]{:S(2)}) collective-permute-start(bf16[384,384]{1,0:T(8,128)(2,1)S(1)} %bitcast.18), channel_id=1, source_target_pairs={{0,4},{4,0},{1,5},{5,1},{2,6},{6,2},{3,7},{7,3},{8,12},{12,8},{9,1... | collective-permute-start | bytes 884744 | tf_op jit(solution)/shard_map/ppermute | solution.py:232
  53.5 3.7 %collective-permute-start.3 = (bf16[32,40,128]{2,1,0:T(8,128)(2,1)S(1)}, bf16[32,40,128]{2,1,0:T(8,128)(2,1)S(1)}, u32[]{:S(2)}, u32[]{:S(2)}) collective-permute-start(bf16[32,40,128]{2,1,0:T(8,128)(2,1)S(1)} %get-tuple-element.54), channel_id=1, source_target_pairs={{0,4},{4,0},{1,5},{5,1},{2,6},{6,2},{3,7},{7,3},{8,12},{12,8},{9,1... | collective-permute-start | bytes 983048 | tf_op jit(solution)/shard_map/ppermute | solution.py:232
  58.0 19.6 %all-to-all-start.2 = ((bf16[32,40,128]{2,1,0:T(8,128)(2,1)}), bf16[32,40,128]{2,1,0:T(8,128)(2,1)S(1)}, u32[]{:S(2)}, u32[]{:S(2)}) async-start(bf16[32,40,128]{2,1,0:T(8,128)(2,1)} %add_convert_fusion), calls=%async_computation.2 | async-start | bytes 655360 | tf_op jit(solution)/shard_map/all_to_all | solution.py:251
  67.0 8.9 %collective-permute-start.4 = (bf16[3,64,192]{2,1,0:T(8,128)(2,1)S(1)}, bf16[3,64,192]{2,1,0:T(8,128)(2,1)S(1)}, u32[]{:S(2)}, u32[]{:S(2)}) collective-permute-start(bf16[3,64,192]{2,1,0:T(8,128)(2,1)S(1)} %get-tuple-element.71), channel_id=1, source_target_pairs={{0,1},{1,2},{2,3},{4,5},{5,6},{6,7},{8,9},{9,10},{10,11},{12,13},{... | collective-permute-start | bytes 221192 | tf_op jit(solution)/shard_map/ppermute | solution.py:226
  70.4 7.0 %collective-permute-start.5 = (bf16[3,64,192]{2,1,0:T(8,128)(2,1)S(1)}, bf16[3,64,192]{2,1,0:T(8,128)(2,1)S(1)}, u32[]{:S(2)}, u32[]{:S(2)}) collective-permute-start(bf16[3,64,192]{2,1,0:T(8,128)(2,1)S(1)} %get-tuple-element.70), channel_id=1, source_target_pairs={{1,0},{2,1},{3,2},{5,4},{6,5},{7,6},{9,8},{10,9},{11,10},{13,12},{... | collective-permute-start | bytes 221192 | tf_op jit(solution)/shard_map/ppermute | solution.py:227
  78.3 15.0 %all-to-all-start.3 = ((bf16[16,8,96]{2,1,0:T(8,128)(2,1)}), bf16[16,8,96]{2,1,0:T(8,128)(2,1)S(1)}, u32[]{:S(2)}, u32[]{:S(2)}) async-start(bf16[16,8,96]{2,1,0:T(8,128)(2,1)} %middle.1), calls=%async_computation.3 | async-start | bytes 65536 | tf_op jit(solution)/shard_map/all_to_all | solution.py:251

commit v8 on v7

--- a/solution.py
+++ b/solution.py
@@ -100,8 +100,8 @@
 
 
 def main_kernel(
-    own, other, tokens, cotangent, padded, normed, inv_std, norm_halves, norm_t, up_halves, up_t,
-    vectors, mine, theirs_bf, block_out, mixed_grad, smalls, grad_rows, theirs,
+    own, other, cotangent, padded, normed, inv_std, norm_halves, norm_t, up_halves, up_t,
+    vectors, mine, theirs_bf, branch_out, mixed_grad, smalls, grad_rows, theirs,
 ):
     branch = jnp.zeros((CELLS, WIDTH), F32)
     normed_grad = jnp.zeros((CELLS, WIDTH), F32)
@@ -125,8 +125,7 @@
                     out[piece, 8 * k : 8 * k + 8, PART:128] = tail[:, 32 * k : 32 * k + 32]
         branch += dot_rows(hidden, reduce)
         normed_grad += dot_rows(pre_grad, expand)
-    flat = tokens[...].reshape(CELLS, WIDTH).astype(F32)
-    block_out[...] = (flat + vectors[2:3] * branch).astype(BF16).reshape(ROWS, COLS, WIDTH)
+    branch_out[...] = branch
     norm = normed[...]
     upstream = cotangent[...].reshape(CELLS, WIDTH).astype(F32)
     smalls[TAPS * TAPS :, :] = jnp.zeros((64 - TAPS * TAPS, WIDTH), F32)
@@ -207,7 +206,12 @@
                 (gain_grad, shift_grad, scale_grad)[row - TAPS * TAPS][...] = value
 
 
-def backward_kernel(grad, low, high, taps, cotangent, out, padded, shifted):
+def backward_kernel(
+    grad, low, high, taps, cotangent, tokens, branch, vectors, out, block_out, padded, shifted
+):
+    flat = tokens[...].reshape(CELLS, WIDTH).astype(F32)
+    total = flat + vectors[2:3] * branch[...]
+    block_out[...] = total.astype(BF16).reshape(ROWS, COLS, WIDTH)
     fill_padded(padded, low, grad, high)
 
     def finish(r, start, chunk, value):
@@ -282,12 +286,12 @@
         "forward",
         pl.CostEstimate(flops=8_000_000, bytes_accessed=2_000_000, transcendentals=256),
     )(tokens, low, high, dw_kernel, vectors, upstream)
-    mine, theirs, block_out, mixed_grad = kernel_call(
+    mine, theirs, branch, mixed_grad = kernel_call(
         main_kernel,
         [
             ((PEERS, 40, 128), F32),
             ((PEERS, 40, 128), BF16),
-            ((ROWS, COLS, WIDTH), BF16),
+            ((CELLS, WIDTH), F32),
             ((ROWS, COLS, WIDTH), BF16),
         ],
         [
@@ -298,7 +302,7 @@
         "main",
         pl.CostEstimate(flops=500_000_000, bytes_accessed=4_000_000, transcendentals=400_000),
     )(
-        own, other, tokens, upstream, padded, normed, inv_std, norm_halves, norm_t, up_halves,
+        own, other, upstream, padded, normed, inv_std, norm_halves, norm_t, up_halves,
         up_t, vectors,
     )
     sums = (mine + other_core(theirs).astype(F32)).astype(BF16)
@@ -308,13 +312,13 @@
     arrived, grad_low, grad_high = lax.optimization_barrier((arrived, grad_low, grad_high))
     (column,) = kernel_call(middle_kernel, [((DEPTH, 8, PART), BF16)], name="middle")(arrived)
     column = exchange(column, "z", "z_back")
-    (grad_tokens,) = kernel_call(
+    grad_tokens, block_out = kernel_call(
         backward_kernel,
-        [((ROWS, COLS, WIDTH), BF16)],
+        [((ROWS, COLS, WIDTH), BF16)] * 2,
         [pltpu.VMEM(PADDED, F32), pltpu.VMEM(SHIFTED, F32)],
         "backward",
         pl.CostEstimate(flops=8_000_000, bytes_accessed=1_000_000, transcendentals=0),
-    )(mixed_grad, grad_low, grad_high, dw_kernel, upstream)
+    )(mixed_grad, grad_low, grad_high, dw_kernel, upstream, tokens, branch, vectors)
     height = lax.rem(lax.axis_index("y") + (HEIGHT - FIRST_Y), HEIGHT).reshape(1)
     column, grad_tokens, height = lax.optimization_barrier((column, grad_tokens, height))
     (spread,) = kernel_call(spread_kernel, [((PEERS, 8, PART), BF16)], name="spread")(column)

time: 108 us -> 108 us (level)
  no operation moved by 1% of the time
where the time goes in v8:
time: 108 us
  starting transfers between devices  56.6 us (52%)
  blocking collectives  28.4 us (26%)
  waiting for transfers between devices  10.3 us (10%)
  Pallas kernels  8.32 us (8%)
  other arithmetic  1.53 us (1%)
  local copies, waits for them, and re-layouts  1.5 us (1%)
    all_to_all x3, starting transfers between devices, exchange(): return lax.all_to_all(x, axes, 0, 0, axis_index_groups=groups, tiled=True)  40.6 us
    all_to_all x2, blocking collectives, exchange(): return lax.all_to_all(x, axes, 0, 0, axis_index_groups=groups, tiled=True)  28.4 us
    ppermute x2, starting transfers between devices, neighbours(): low = lax.ppermute(block[ROWS - HALO:], 'space', forward)  6.48 us
    ppermute x2, starting transfers between devices, neighbours(): high = lax.ppermute(block[:HALO], 'space', backward)  5.2 us
    ppermute x2, waiting for transfers between devices, neighbours(): high = lax.ppermute(block[:HALO], 'space', backward)  4.56 us
    ppermute x2, starting transfers between devices, other_core(): return lax.ppermute(x, 'core', [(0, 1), (1, 0)])  4.31 us
    pallas_call x1, Pallas kernels, shards(): kernel_call(main_kernel, [((PEERS, 40, 128), F32), ((PEERS, 40, 128), BF1...  3.26 us
    ppermute x2, waiting for transfers between devices, neighbours(): low = lax.ppermute(block[ROWS - HALO:], 'space', forward)  3.01 us
  transfers between devices with their start and end apart: 9, of which 7 were waited for; matrix products, arithmetic and copies ran while one was open for 0% of the time, Pallas kernels for 3%

profile of v8, /device:TPU:4, one launch (start us, length us, event | category | flops | bytes accessed | tf_op | source)
XLA Modules:
  0.0 107.6 jit_solution(8200618945126771551)
XLA Ops:
  0.6 0.7 broadcast_in_dim.12
  1.4 0.0 copy-start
  1.4 0.7 pad_maximum_fusion
  2.1 19.6 %all-to-all-start = ((bf16[16,3,384]{2,1,0:T(4,128)(2,1)}), bf16[16,3,384]{2,1,0:T(4,128)(2,1)S(1)}, u32[]{:S(2)}, u32[]{:S(2)}) async-start(bf16[16,3,384]{2,1,0:T(4,128)(2,1)} %pad_maximum_fusion), calls=%async_computation | async-start | bytes 98304 | tf_op jit(solution)/shard_map/all_to_all | solution.py:255
  21.7 0.0 copy-start.5
  21.8 3.1 %collective-permute-start = (bf16[3,64,192]{2,1,0:T(8,128)(2,1)S(1)}, bf16[3,64,192]{2,1,0:T(8,128)(2,1)S(1)}, u32[]{:S(2)}, u32[]{:S(2)}) collective-permute-start(bf16[3,64,192]{2,1,0:T(8,128)(2,1)S(1)} %get-tuple-element.77), channel_id=1, source_target_pairs={{0,1},{1,2},{2,3},{4,5},{5,6},{6,7},{8,9},{9,10},{10,11},{12,13},{... | collective-permute-start | bytes 221192 | tf_op jit(solution)/shard_map/ppermute | solution.py:230
  24.9 2.7 %collective-permute-start.1 = (bf16[3,64,192]{2,1,0:T(8,128)(2,1)S(1)}, bf16[3,64,192]{2,1,0:T(8,128)(2,1)S(1)}, u32[]{:S(2)}, u32[]{:S(2)}) collective-permute-start(bf16[3,64,192]{2,1,0:T(8,128)(2,1)S(1)} %get-tuple-element.76), channel_id=1, source_target_pairs={{1,0},{2,1},{3,2},{5,4},{6,5},{7,6},{9,8},{10,9},{11,10},{13,12},{... | collective-permute-start | bytes 221192 | tf_op jit(solution)/shard_map/ppermute | solution.py:231
  27.6 0.0 copy-start.4
  27.6 0.7 copy-done.4
  28.3 3.1 %collective-permute-done.1.high = bf16[3,64,192]{2,1,0:T(8,128)(2,1)S(1)} collective-permute-done((bf16[3,64,192]{2,1,0:T(8,128)(2,1)S(1)}, bf16[3,64,192]{2,1,0:T(8,128)(2,1)S(1)}, u32[]{:S(2)}, u32[]{:S(2)}) %collective-permute-start.1) | collective-permute-done | bytes 73760 | tf_op jit(solution)/shard_map/ppermute | solution.py:231
  31.4 0.1 all-to-all-done
  31.5 0.0 copy-start.1
  31.5 0.0 copy-start.2
  31.6 15.0 %all_to_all.25 = bf16[8,48,384]{2,1,0:T(8,128)(2,1)S(1)} all-to-all(bf16[8,48,384]{2,1,0:T(8,128)(2,1)S(1)} %broadcast_in_dim.28), channel_id=1, replica_groups={{32,40,48,56,0,8,16,24},{33,41,49,57,1,9,17,25},{34,42,50,58,2,10,18,26..., dimensions={0} | all-to-all | bytes 589824 | tf_op jit(solution)/shard_map/all_to_all | solution.py:255
  46.5 1.9 %collective-permute-start.2 = (bf16[384,384]{1,0:T(8,128)(2,1)S(1)}, bf16[384,384]{1,0:T(8,128)(2,1)S(1)}, u32[]{:S(2)}, u32[]{:S(2)}) collective-permute-start(bf16[384,384]{1,0:T(8,128)(2,1)S(1)} %bitcast.18), channel_id=1, source_target_pairs={{0,4},{4,0},{1,5},{5,1},{2,6},{6,2},{3,7},{7,3},{8,12},{12,8},{9,1... | collective-permute-start | bytes 884744 | tf_op jit(solution)/shard_map/ppermute | solution.py:236
  48.5 1.8 %forward.1 = (f32[10,80,192]{2,1,0:T(8,128)S(1)}, f32[256,192]{1,0:T(8,128)S(1)}, f32[256,1]{1,0:T(8,128)S(1)}, bf16[2,256,96]{2,1,0:T(8,128)(2,1)S(1)}, bf16[19...) custom-call(bf16[4,64,192]{2,1,0:T(8,128)(2,1)S(1)} %bitcast.16, ...), custom_call_target="tpu_custom_call" | custom-call | flops 8000000 | bytes 2000000 | tf_op jit(solution)/shard_map/forward/pallas_call | solution.py:274
  50.2 3.3 %main.1 = (f32[32,40,128]{2,1,0:T(8,128)S(1)}, bf16[32,40,128]{2,1,0:T(8,128)(2,1)S(1)}, f32[256,192]{1,0:T(8,128)S(1)}, bf16[4,64,192]{2,1,0:T(8,128)(2,1)S(1)}) custom-call(bf16[384,384]{1,0:T(8,128)(2,1)S(1)} %bitcast.19, bf16[384,384]{1,0:T(8,128)(2,1)S(1)} %collective-permute-done.2.other, bf16[4,64,192]{2,1,0:T(8,128)(2,1)S(1)} %bitcast.21, ...), custom_call_target="tpu_custom_call" | custom-call | flops 500000000 | bytes 4000000 | tf_op jit(solution)/shard_map/main/pallas_call | solution.py:289
  53.5 2.4 %collective-permute-start.3 = (bf16[32,40,128]{2,1,0:T(8,128)(2,1)S(1)}, bf16[32,40,128]{2,1,0:T(8,128)(2,1)S(1)}, u32[]{:S(2)}, u32[]{:S(2)}) collective-permute-start(bf16[32,40,128]{2,1,0:T(8,128)(2,1)S(1)} %get-tuple-element.55), channel_id=1, source_target_pairs={{0,4},{4,0},{1,5},{5,1},{2,6},{6,2},{3,7},{7,3},{8,12},{12,8},{9,1... | collective-permute-start | bytes 983048 | tf_op jit(solution)/shard_map/ppermute | solution.py:236
  55.9 1.2 %collective-permute-done.3 = bf16[32,40,128]{2,1,0:T(8,128)(2,1)S(1)} collective-permute-done((bf16[32,40,128]{2,1,0:T(8,128)(2,1)S(1)}, bf16[32,40,128]{2,1,0:T(8,128)(2,1)S(1)}, u32[]{:S(2)}, u32[]{:S(2)}) %collective-permute-start.3) | collective-permute-done | bytes 327712 | tf_op jit(solution)/shard_map/ppermute | solution.py:236
  57.1 0.8 add_convert_fusion
  58.0 9.0 %all-to-all-start.2 = ((bf16[32,40,128]{2,1,0:T(8,128)(2,1)}), bf16[32,40,128]{2,1,0:T(8,128)(2,1)S(1)}, u32[]{:S(2)}, u32[]{:S(2)}) async-start(bf16[32,40,128]{2,1,0:T(8,128)(2,1)} %add_convert_fusion), calls=%async_computation.2 | async-start | bytes 655360 | tf_op jit(solution)/shard_map/all_to_all | solution.py:255
  67.0 3.4 %collective-permute-start.4 = (bf16[3,64,192]{2,1,0:T(8,128)(2,1)S(1)}, bf16[3,64,192]{2,1,0:T(8,128)(2,1)S(1)}, u32[]{:S(2)}, u32[]{:S(2)}) collective-permute-start(bf16[3,64,192]{2,1,0:T(8,128)(2,1)S(1)} %get-tuple-element.75), channel_id=1, source_target_pairs={{0,1},{1,2},{2,3},{4,5},{5,6},{6,7},{8,9},{9,10},{10,11},{12,13},{... | collective-permute-start | bytes 221192 | tf_op jit(solution)/shard_map/ppermute | solution.py:230
  70.4 2.5 %collective-permute-start.5 = (bf16[3,64,192]{2,1,0:T(8,128)(2,1)S(1)}, bf16[3,64,192]{2,1,0:T(8,128)(2,1)S(1)}, u32[]{:S(2)}, u32[]{:S(2)}) collective-permute-start(bf16[3,64,192]{2,1,0:T(8,128)(2,1)S(1)} %get-tuple-element.74), channel_id=1, source_target_pairs={{1,0},{2,1},{3,2},{5,4},{6,5},{7,6},{9,8},{10,9},{11,10},{13,12},{... | collective-permute-start | bytes 221192 | tf_op jit(solution)/shard_map/ppermute | solution.py:231
  72.9 3.0 %collective-permute-done.4.low = bf16[3,64,192]{2,1,0:T(8,128)(2,1)S(1)} collective-permute-done((bf16[3,64,192]{2,1,0:T(8,128)(2,1)S(1)}, bf16[3,64,192]{2,1,0:T(8,128)(2,1)S(1)}, u32[]{:S(2)}, u32[]{:S(2)}) %collective-permute-start.4) | collective-permute-done | bytes 73760 | tf_op jit(solution)/shard_map/ppermute | solution.py:230
  75.9 1.5 %collective-permute-done.5.high = bf16[3,64,192]{2,1,0:T(8,128)(2,1)S(1)} collective-permute-done((bf16[3,64,192]{2,1,0:T(8,128)(2,1)S(1)}, bf16[3,64,192]{2,1,0:T(8,128)(2,1)S(1)}, u32[]{:S(2)}, u32[]{:S(2)}) %collective-permute-start.5) | collective-permute-done | bytes 73760 | tf_op jit(solution)/shard_map/ppermute | solution.py:231
  77.4 0.2 all-to-all-done.2.arrived
  77.6 0.7 middle.1
  78.3 12.0 %all-to-all-start.3 = ((bf16[16,8,96]{2,1,0:T(8,128)(2,1)}), bf16[16,8,96]{2,1,0:T(8,128)(2,1)S(1)}, u32[]{:S(2)}, u32[]{:S(2)}) async-start(bf16[16,8,96]{2,1,0:T(8,128)(2,1)} %middle.1), calls=%async_computation.3 | async-start | bytes 65536 | tf_op jit(solution)/shard_map/all_to_all | solution.py:255
  90.3 1.8 %backward.1 = (bf16[4,64,192]{2,1,0:T(8,128)(2,1)}, bf16[4,64,192]{2,1,0:T(8,128)(2,1)}) custom-call(bf16[4,64,192]{2,1,0:T(8,128)(2,1)S(1)} %get-tuple-element.57.grad, bf16[3,64,192]{2,1,0:T(8,128)(2,1)S(1)} %collective-permute-done.4.low, bf16[3,64,192]{2,1,0:T(8,128)(2,1)S(1)} %collective-permute-done.5.high, f32[7,7,192]{2,1,0:T(8,128)S(1)} %copy-done.2, ...), custom_call_target="tpu_custom_call" | custom-call | flops 8000000 | bytes 1000000 | tf_op jit(solution)/shard_map/backward/pallas_call | solution.py:315
  92.1 1.2 %all-to-all-done.3.arrived = bf16[16,8,96]{2,1,0:T(8,128)(2,1)S(1)} async-done(((bf16[16,8,96]{2,1,0:T(8,128)(2,1)}), bf16[16,8,96]{2,1,0:T(8,128)(2,1)S(1)}, u32[]{:S(2)}, u32[]{:S(2)}) %all-to-all-start.3) | async-done | bytes 24608 | tf_op jit(solution)/shard_map/all_to_all | solution.py:255
  93.4 13.5 %all_to_all.26.done = bf16[32,8,96]{2,1,0:T(8,128)(2,1)S(1)} all-to-all(bf16[32,8,96]{2,1,0:T(8,128)(2,1)S(1)} %spread.1), channel_id=1, replica_groups={{34,35,32,33,42,43,40,41,50,51,48,49,58,59,56,57,2,3,0,1,10,11,8,9,18,1..., dimensions={0} | all-to-all | bytes 98304 | tf_op jit(solution)/shard_map/all_to_all | solution.py:255
  106.9 0.7 final.1
  (17 shorter events, 0.2 us)
Async XLA Ops:
  0.6 0.7 copy-start.3
  1.4 20.3 %copy-start = (bf16[1,4,64,192]{3,2,1,0:T(8,128)(2,1)S(1)}, bf16[1,4,64,192]{3,2,1,0:T(8,128)(2,1)}, u32[]{:S(2)}) copy-start(bf16[1,4,64,192]{3,2,1,0:T(8,128)(2,1)} %param.8) | copy-start | bytes 294916
  2.1 29.4 %all-to-all-start = ((bf16[16,3,384]{2,1,0:T(4,128)(2,1)}), bf16[16,3,384]{2,1,0:T(4,128)(2,1)S(1)}, u32[]{:S(2)}, u32[]{:S(2)}) async-start(bf16[16,3,384]{2,1,0:T(4,128)(2,1)} %pad_maximum_fusion), calls=%async_computation | async-start | bytes 98304 | tf_op jit(solution)/shard_map/all_to_all | solution.py:255
  21.7 5.9 %copy-start.5 = (f32[192]{0:T(256)S(1)}, f32[192]{0:T(256)}, u32[]{:S(2)}) copy-start(f32[192]{0:T(256)} %param.11) | copy-start | bytes 2308
  21.7 5.9 %copy-start.6 = (f32[192]{0:T(256)S(1)}, f32[192]{0:T(256)}, u32[]{:S(2)}) copy-start(f32[192]{0:T(256)} %param.10) | copy-start | bytes 2308
  21.8 6.6 %collective-permute-start = (bf16[3,64,192]{2,1,0:T(8,128)(2,1)S(1)}, bf16[3,64,192]{2,1,0:T(8,128)(2,1)S(1)}, u32[]{:S(2)}, u32[]{:S(2)}) collective-permute-start(bf16[3,64,192]{2,1,0:T(8,128)(2,1)S(1)} %get-tuple-element.77), channel_id=1, source_target_pairs={{0,1},{1,2},{2,3},{4,5},{5,6},{6,7},{8,9},{9,10},{10,11},{12,13},{... | collective-permute-start | bytes 221192 | tf_op jit(solution)/shard_map/ppermute | solution.py:230
  24.9 6.5 %collective-permute-start.1 = (bf16[3,64,192]{2,1,0:T(8,128)(2,1)S(1)}, bf16[3,64,192]{2,1,0:T(8,128)(2,1)S(1)}, u32[]{:S(2)}, u32[]{:S(2)}) collective-permute-start(bf16[3,64,192]{2,1,0:T(8,128)(2,1)S(1)} %get-tuple-element.76), channel_id=1, source_target_pairs={{1,0},{2,1},{3,2},{5,4},{6,5},{7,6},{9,8},{10,9},{11,10},{13,12},{... | collective-permute-start | bytes 221192 | tf_op jit(solution)/shard_map/ppermute | solution.py:231
  27.6 0.7 copy-start.4
  31.5 16.9 %copy-start.1 = (bf16[1,4,64,192]{3,2,1,0:T(8,128)(2,1)S(1)}, bf16[1,4,64,192]{3,2,1,0:T(8,128)(2,1)}, u32[]{:S(2)}) copy-start(bf16[1,4,64,192]{3,2,1,0:T(8,128)(2,1)} %param.15) | copy-start | bytes 294916
  31.5 16.9 %copy-start.2 = (f32[7,7,192]{2,1,0:T(8,128)S(1)}, f32[7,7,192]{2,1,0:T(8,128)}, u32[]{:S(2)}) copy-start(f32[7,7,192]{2,1,0:T(8,128)} %taps.3) | copy-start | bytes 112900
  46.5 3.7 %collective-permute-start.2 = (bf16[384,384]{1,0:T(8,128)(2,1)S(1)}, bf16[384,384]{1,0:T(8,128)(2,1)S(1)}, u32[]{:S(2)}, u32[]{:S(2)}) collective-permute-start(bf16[384,384]{1,0:T(8,128)(2,1)S(1)} %bitcast.18), channel_id=1, source_target_pairs={{0,4},{4,0},{1,5},{5,1},{2,6},{6,2},{3,7},{7,3},{8,12},{12,8},{9,1... | collective-permute-start | bytes 884744 | tf_op jit(solution)/shard_map/ppermute | solution.py:236
  53.5 3.6 %collective-permute-start.3 = (bf16[32,40,128]{2,1,0:T(8,128)(2,1)S(1)}, bf16[32,40,128]{2,1,0:T(8,128)(2,1)S(1)}, u32[]{:S(2)}, u32[]{:S(2)}) collective-permute-start(bf16[32,40,128]{2,1,0:T(8,128)(2,1)S(1)} %get-tuple-element.55), channel_id=1, source_target_pairs={{0,4},{4,0},{1,5},{5,1},{2,6},{6,2},{3,7},{7,3},{8,12},{12,8},{9,1... | collective-permute-start | bytes 983048 | tf_op jit(solution)/shard_map/ppermute | solution.py:236
  58.0 19.6 %all-to-all-start.2 = ((bf16[32,40,128]{2,1,0:T(8,128)(2,1)}), bf16[32,40,128]{2,1,0:T(8,128)(2,1)S(1)}, u32[]{:S(2)}, u32[]{:S(2)}) async-start(bf16[32,40,128]{2,1,0:T(8,128)(2,1)} %add_convert_fusion), calls=%async_computation.2 | async-start | bytes 655360 | tf_op jit(solution)/shard_map/all_to_all | solution.py:255
  67.0 8.9 %collective-permute-start.4 = (bf16[3,64,192]{2,1,0:T(8,128)(2,1)S(1)}, bf16[3,64,192]{2,1,0:T(8,128)(2,1)S(1)}, u32[]{:S(2)}, u32[]{:S(2)}) collective-permute-start(bf16[3,64,192]{2,1,0:T(8,128)(2,1)S(1)} %get-tuple-element.75), channel_id=1, source_target_pairs={{0,1},{1,2},{2,3},{4,5},{5,6},{6,7},{8,9},{9,10},{10,11},{12,13},{... | collective-permute-start | bytes 221192 | tf_op jit(solution)/shard_map/ppermute | solution.py:230
  70.4 7.0 %collective-permute-start.5 = (bf16[3,64,192]{2,1,0:T(8,128)(2,1)S(1)}, bf16[3,64,192]{2,1,0:T(8,128)(2,1)S(1)}, u32[]{:S(2)}, u32[]{:S(2)}) collective-permute-start(bf16[3,64,192]{2,1,0:T(8,128)(2,1)S(1)} %get-tuple-element.74), channel_id=1, source_target_pairs={{1,0},{2,1},{3,2},{5,4},{6,5},{7,6},{9,8},{10,9},{11,10},{13,12},{... | collective-permute-start | bytes 221192 | tf_op jit(solution)/shard_map/ppermute | solution.py:231
  78.3 15.0 %all-to-all-start.3 = ((bf16[16,8,96]{2,1,0:T(8,128)(2,1)}), bf16[16,8,96]{2,1,0:T(8,128)(2,1)S(1)}, u32[]{:S(2)}, u32[]{:S(2)}) async-start(bf16[16,8,96]{2,1,0:T(8,128)(2,1)} %middle.1), calls=%async_computation.3 | async-start | bytes 65536 | tf_op jit(solution)/shard_map/all_to_all | solution.py:255
